TPU v7x, 256 devices: a whole 4x4x8 slice. The times are simulated.
256 devices in a mesh: gx: 8 (over y, x_hi), gy: 32 (over x_lo, z, core).
Axes of the slice: x: 4 (x_hi: 2, x_lo: 2; x = x_hi * 2 + x_lo), y: 4, z: 8, core: 2. Of those that a mesh axis runs over, the one named last changes fastest.
Arguments:
- draft_in: bfloat16 [64, 16384], P('gy', 'gx')
- verify_in: bfloat16 [256, 16384], P('gy', 'gx')
- accept_len: int32 [64], P('gy'), may hold values from 0 to 3
- norm_gain: bfloat16 [16384], P('gx'), may hold values from 0.099609375 to 1.8984375
- gate_weight: bfloat16 [16384, 28672], P('gx', 'gy'), may hold values from -0.046875 to 0.046875
- up_weight: bfloat16 [16384, 28672], P('gx', 'gy'), may hold values from -0.046875 to 0.046875
- down_weight: bfloat16 [28672, 16384], P('gy', 'gx'), may hold values from -0.03125 to 0.03125
Outputs:
- draft_out: bfloat16 [64, 16384], P('gy', 'gx')
- verify_out: bfloat16 [256, 16384], P('gy', 'gx')
All inputs are finite; a program needn't handle non-finite values.
Results may differ from a plain program's by a relative error of at most 0.033.
Values may be sent and summed in bfloat16 or wider, within the bound.
No kernel may reach another device: no remote copies, remote signals or barrier semaphores. Data moves between devices by JAX's collectives and lax.ppermute only.
A program may use at most 64 MiB of HBM per device.

v0:
```python
import jax
import jax.numpy as jnp
from jax import lax
from jax.sharding import PartitionSpec as P

D = 16384
DRAFT_STEPS = 3
POS = 4


epsilon = 1e-05


def delta_of(states, norm_gain, gate_weight, up_weight, down_weight):
    float_rows = states.astype(jnp.float32)
    squares = lax.psum(jnp.sum(float_rows * float_rows, axis=1), "gx")
    scale = lax.rsqrt(squares / D + epsilon)[:, None]
    normed_share = (float_rows * scale * norm_gain.astype(jnp.float32)).astype(jnp.bfloat16)
    normed = lax.all_gather(normed_share, "gy", axis=0, tiled=True)
    split_at = gate_weight.shape[1]
    block_rows = normed
    gate_part = jnp.dot(block_rows, gate_weight, preferred_element_type=jnp.float32)
    upper_part = jnp.dot(block_rows, up_weight, preferred_element_type=jnp.float32)
    both_halves = lax.psum_scatter(
        jnp.concatenate([gate_part, upper_part], axis=1).astype(jnp.bfloat16),
        "gx",
        scatter_dimension=0,
        tiled=True,
    ).astype(jnp.float32)
    hidden_share = (jax.nn.silu(both_halves[:, :split_at]) * both_halves[:, split_at:]).astype(
        jnp.bfloat16
    )
    hidden = lax.all_gather(hidden_share, "gx", axis=0, tiled=True)
    block_rows = hidden
    return lax.psum_scatter(
        jnp.dot(block_rows, down_weight, preferred_element_type=jnp.float32).astype(jnp.bfloat16),
        "gy",
        scatter_dimension=0,
        tiled=True,
    ).astype(jnp.float32)


def advance(state, weights):
    change = delta_of(state, *weights)
    return (state.astype(jnp.float32) + change).astype(jnp.bfloat16)


def run_drafts(draft_in, weights, count):
    state = draft_in
    for step in range(count):
        state = advance(state, weights)
    return state


def apply_live(verify_in, accept_len, change):
    live = (
        (jnp.arange(POS, dtype=jnp.int32)[None, :] <= accept_len[:, None])
        .reshape(-1, 1)
        .astype(jnp.float32)
    )
    return (verify_in.astype(jnp.float32) + live * change).astype(jnp.bfloat16)


def run_verify(verify_in, accept_len, weights):
    change = delta_of(verify_in, *weights)
    return apply_live(verify_in, accept_len, change)


def shards(draft_in, verify_in, accept_len, norm_gain, gate_weight, up_weight, down_weight):
    weights = (norm_gain, gate_weight, up_weight, down_weight)
    draft_out = run_drafts(draft_in, weights, DRAFT_STEPS)
    verify_out = run_verify(verify_in, accept_len, weights)
    return (draft_out, verify_out)


def solution(mesh):
    placed = (
        P("gy", "gx"),
        P("gy", "gx"),
        P("gy"),
        P("gx"),
        P("gx", "gy"),
        P("gx", "gy"),
        P("gy", "gx"),
    )
    return jax.shard_map(
        shards,
        mesh=mesh,
        in_specs=placed,
        out_specs=(P("gy", "gx"), P("gy", "gx")),
        check_vma=False,
    )
```

profile of v0, /device:TPU:32, one launch (start us, length us, event | category | flops | bytes accessed | tf_op | source)
XLA Modules:
  0.0 1347.9 jit_solution(8359693136059879718)
XLA Ops:
  7.2 0.8 fusion.8
  8.0 0.7 convert_element_type.110
  8.7 24.5 %psum.28 = f32[2]{0:T(128)S(1)} all-reduce(f32[2]{0:T(128)S(1)} %fusion.8), channel_id=1, replica_groups=mesh['gx'=8,'gy'=32] {'gx'}, use_global_device_ids=true, to_apply=%region_1.0 | all-reduce | flops 2 | bytes 16 | tf_op jit(solution)/shard_map/psum | solution.py:16
  33.2 0.8 fusion.22
  34.0 33.9 %all-gather = bf16[32,2,2048]{2,1,0:T(2,128)(2,1)S(1)} all-gather(bf16[1,2,2048]{2,1,0:T(2,128)(2,1)S(1)} %fusion.22), channel_id=1, replica_groups=mesh['gx'=8,'gy'=32] {'gy'}, dimensions={0}, use_global_device_ids=true | all-gather | bytes 270336 | tf_op jit(solution)/shard_map/all_gather | solution.py:19
  68.1 2.9 convolution_convert_fusion.10
  71.2 0.7 convolution_convert_fusion.11
  71.9 0.7 pad_maximum_fusion.1
  72.7 62.9 %reduce-scatter.6.cloned.1.call-done = bf16[8,1792]{1,0:T(8,128)(2,1)} async-done(((bf16[64,1792]{1,0:T(8,128)(2,1)}), bf16[8,1792]{1,0:T(8,128)(2,1)}) %reduce-scatter.6.cloned.1.call-update) | async-done | bytes 28688 | tf_op jit(solution)/shard_map/reduce_scatter | solution.py:24
  135.6 0.8 convert_element_type.112
  136.4 34.3 %all_gather.25 = bf16[64,896]{1,0:T(8,128)(2,1)S(1)} all-gather(bf16[8,896]{1,0:T(8,128)(2,1)S(1)} %fusion.7), channel_id=1, replica_groups=mesh['gx'=8,'gy'=32] {'gx'}, dimensions={0}, use_global_device_ids=true | all-gather | bytes 129024 | tf_op jit(solution)/shard_map/all_gather | solution.py:33
  170.7 3.5 convolution_convert_fusion.3
  174.3 0.6 dynamic-slice
  175.5 214.4 %all-reduce.8.cloned.1.call-done = bf16[64,2048]{1,0:T(8,128)(2,1)} async-done(((bf16[64,2048]{1,0:T(8,128)(2,1)}), bf16[64,2048]{1,0:T(8,128)(2,1)}) %all-reduce.8.cloned.1.call-update) | async-done | bytes 262160
  389.9 0.9 fusion.12
  390.8 23.9 %psum.29 = f32[2]{0:T(128)S(1)} all-reduce(f32[2]{0:T(128)S(1)} %get-tuple-element.6), channel_id=1, replica_groups=mesh['gx'=8,'gy'=32] {'gx'}, use_global_device_ids=true, to_apply=%region_5.6 | all-reduce | flops 2 | bytes 16 | tf_op jit(solution)/shard_map/psum | solution.py:16
  414.8 34.6 %all-gather.1 = bf16[32,2,2048]{2,1,0:T(2,128)(2,1)S(1)} all-gather(bf16[1,2,2048]{2,1,0:T(2,128)(2,1)S(1)} %fusion.21), channel_id=1, replica_groups=mesh['gx'=8,'gy'=32] {'gy'}, dimensions={0}, use_global_device_ids=true | all-gather | bytes 270336 | tf_op jit(solution)/shard_map/all_gather | solution.py:19
  449.6 2.9 convolution_convert_fusion.8
  452.7 0.7 convolution_convert_fusion.9
  453.4 0.7 pad_maximum_fusion.2
  454.2 60.4 %reduce-scatter.8.cloned.1.call-done = bf16[8,1792]{1,0:T(8,128)(2,1)} async-done(((bf16[64,1792]{1,0:T(8,128)(2,1)}), bf16[8,1792]{1,0:T(8,128)(2,1)}) %reduce-scatter.8.cloned.1.call-update) | async-done | bytes 28688 | tf_op jit(solution)/shard_map/reduce_scatter | solution.py:24
  514.6 0.8 convert_element_type.119
  515.4 34.3 %all_gather.27 = bf16[64,896]{1,0:T(8,128)(2,1)S(1)} all-gather(bf16[8,896]{1,0:T(8,128)(2,1)S(1)} %fusion.6), channel_id=1, replica_groups=mesh['gx'=8,'gy'=32] {'gx'}, dimensions={0}, use_global_device_ids=true | all-gather | bytes 129024 | tf_op jit(solution)/shard_map/all_gather | solution.py:33
  549.6 3.5 convolution_convert_fusion.2
  553.4 215.7 %all-reduce.10.cloned.1.call-done = bf16[64,2048]{1,0:T(8,128)(2,1)} async-done(((bf16[64,2048]{1,0:T(8,128)(2,1)}), bf16[64,2048]{1,0:T(8,128)(2,1)}) %all-reduce.10.cloned.1.call-update) | async-done | bytes 262160
  769.0 0.9 fusion.16
  769.9 23.9 %all-reduce.3 = (f32[2]{0:T(128)S(1)}, f32[8]{0:T(128)S(1)}) all-reduce(f32[2]{0:T(128)S(1)} %get-tuple-element.4, f32[8]{0:T(128)S(1)} %fusion.1), channel_id=1, replica_groups=mesh['gx'=8,'gy'=32] {'gx'}, use_global_device_ids=true, to_apply=%region_9.10 | all-reduce | flops 10 | bytes 80 | tf_op jit(solution)/shard_map/psum | solution.py:16
  793.8 0.7 fusion.3
  794.7 34.7 %all-gather.2 = bf16[32,2,2048]{2,1,0:T(2,128)(2,1)S(1)} all-gather(bf16[1,2,2048]{2,1,0:T(2,128)(2,1)S(1)} %fusion.20), channel_id=1, replica_groups=mesh['gx'=8,'gy'=32] {'gy'}, dimensions={0}, use_global_device_ids=true | all-gather | bytes 270336 | tf_op jit(solution)/shard_map/all_gather | solution.py:19
  829.5 2.9 convolution_convert_fusion.6
  832.6 0.7 convolution_convert_fusion.7
  833.3 0.7 pad_maximum_fusion.3
  834.1 17.4 %all-gather.5.cloned.1.call-done = bf16[256,2048]{1,0:T(8,128)(2,1)} async-done(((bf16[8,2048]{1,0:T(8,128)(2,1)}), bf16[256,2048]{1,0:T(8,128)(2,1)}) %all-gather.5.cloned.1.call-update) | async-done | bytes 1048592 | tf_op jit(solution)/shard_map/all_gather | solution.py:19
  851.5 3.8 convolution_convert_fusion.4
  855.3 1.3 convolution_convert_fusion.5
  856.6 1.0 pad_maximum_fusion
  857.6 66.0 %reduce-scatter.10.cloned.1.call-done = bf16[8,1792]{1,0:T(8,128)(2,1)} async-done(((bf16[64,1792]{1,0:T(8,128)(2,1)}), bf16[8,1792]{1,0:T(8,128)(2,1)}) %reduce-scatter.10.cloned.1.call-update) | async-done | bytes 28688 | tf_op jit(solution)/shard_map/reduce_scatter | solution.py:24
  923.6 0.8 convert_element_type.126
  924.4 34.5 %all_gather.29 = bf16[64,896]{1,0:T(8,128)(2,1)S(1)} all-gather(bf16[8,896]{1,0:T(8,128)(2,1)S(1)} %fusion.5), channel_id=1, replica_groups=mesh['gx'=8,'gy'=32] {'gx'}, dimensions={0}, use_global_device_ids=true | all-gather | bytes 129024 | tf_op jit(solution)/shard_map/all_gather | solution.py:33
  958.9 3.6 convolution_convert_fusion.1
  962.5 41.0 %reduce-scatter.12.cloned.1.call-done = bf16[32,1792]{1,0:T(8,128)(2,1)} async-done(((bf16[256,1792]{1,0:T(8,128)(2,1)}), bf16[32,1792]{1,0:T(8,128)(2,1)}) %reduce-scatter.12.cloned.1.call-update) | async-done | bytes 114704 | tf_op jit(solution)/shard_map/reduce_scatter | solution.py:24
  1003.5 0.9 convert_element_type.135
  1004.5 35.7 %all_gather.31 = bf16[256,896]{1,0:T(8,128)(2,1)S(1)} all-gather(bf16[32,896]{1,0:T(8,128)(2,1)S(1)} %fusion), channel_id=1, replica_groups=mesh['gx'=8,'gy'=32] {'gx'}, dimensions={0}, use_global_device_ids=true | all-gather | bytes 516096 | tf_op jit(solution)/shard_map/all_gather | solution.py:33
  1040.1 4.3 convolution_convert_fusion
  1044.6 178.1 %all-reduce.12.cloned.1.call-done = bf16[64,2048]{1,0:T(8,128)(2,1)} async-done(((bf16[64,2048]{1,0:T(8,128)(2,1)}), bf16[64,2048]{1,0:T(8,128)(2,1)}) %all-reduce.12.cloned.1.call-update) | async-done | bytes 262160
  1222.8 1.4 fusion.19
  1224.2 115.8 %reduce-scatter.14.cloned.1.call-done = bf16[8,2048]{1,0:T(8,128)(2,1)} async-done(((bf16[256,2048]{1,0:T(8,128)(2,1)}), bf16[8,2048]{1,0:T(8,128)(2,1)}) %reduce-scatter.14.cloned.1.call-update) | async-done | bytes 32784 | tf_op jit(solution)/shard_map/reduce_scatter | solution.py:35
  1339.9 1.4 fusion.4
  (52 shorter events, 2.1 us)
Async XLA Ops:
  7.2 128.5 %reduce-scatter.6.cloned.1.call-start = ((), (), s32[]{:S(2)}) async-start(), calls=%async_computation.5 | async-start | bytes 258048 | tf_op jit(solution)/shard_map/reduce_scatter | solution.py:24
  68.0 3.1 copy-start
  71.2 103.1 %copy-start.8 = (u32[256]{0:T(256)S(1)}, u32[256]{0:T(256)}, u32[]{:S(2)}) copy-start(u32[256]{0:T(256)} %constant.24) | copy-start | bytes 3076
  71.9 318.0 %copy-start.5 = (bf16[2,2048]{1,0:T(2,128)(2,1)S(1)}, bf16[2,2048]{1,0:T(2,128)(2,1)}, u32[]{:S(2)}) copy-start(bf16[2,2048]{1,0:T(2,128)(2,1)} %param.7) | copy-start | bytes 24580
  72.6 317.3 %all-reduce.8.cloned.1.call-start = ((), (), s32[]{:S(2)}) async-start(), calls=%async_computation.11 | async-start | bytes 524288
  174.2 340.4 %reduce-scatter.8.cloned.1.call-start = ((), (), s32[]{:S(2)}) async-start(), calls=%async_computation.6 | async-start | bytes 258048 | tf_op jit(solution)/shard_map/reduce_scatter | solution.py:24
  449.6 3.1 copy-start.1
  452.7 100.5 %copy-start.4 = (bf16[8,2048]{1,0:T(8,128)(2,1)S(1)}, bf16[8,2048]{1,0:T(8,128)(2,1)}, u32[]{:S(2)}) copy-start(bf16[8,2048]{1,0:T(8,128)(2,1)} %param.8) | copy-start | bytes 98308
  454.1 314.9 %all-reduce.10.cloned.1.call-start = ((), (), s32[]{:S(2)}) async-start(), calls=%async_computation.12 | async-start | bytes 524288
  553.2 298.3 %all-gather.5.cloned.1.call-start = ((), (), s32[]{:S(2)}) async-start(), calls=%async_computation.8 | async-start | bytes 1081344 | tf_op jit(solution)/shard_map/all_gather | solution.py:19
  794.6 129.0 %reduce-scatter.10.cloned.1.call-start = ((), (), s32[]{:S(2)}) async-start(), calls=%async_computation.7 | async-start | bytes 258048 | tf_op jit(solution)/shard_map/reduce_scatter | solution.py:24
  829.5 3.2 copy-start.2
  834.1 169.4 %reduce-scatter.12.cloned.1.call-start = ((), (), s32[]{:S(2)}) async-start(), calls=%async_computation.9 | async-start | bytes 1032192 | tf_op jit(solution)/shard_map/reduce_scatter | solution.py:24
  851.5 3.8 copy-start.3
  851.5 3.8 copy-start.6
  857.6 365.2 %all-reduce.12.cloned.1.call-start = ((), (), s32[]{:S(2)}) async-start(), calls=%async_computation.13 | async-start | bytes 524288
  962.4 377.5 %reduce-scatter.14.cloned.1.call-start = ((), (), s32[]{:S(2)}) async-start(), calls=%async_computation.10 | async-start | bytes 1081344 | tf_op jit(solution)/shard_map/reduce_scatter | solution.py:35
  1004.5 40.0 %copy-start.7 = (s32[2]{0:T(128)S(1)}, s32[2]{0:T(128)}, u32[]{:S(2)}) copy-start(s32[2]{0:T(128)} %param.9) | copy-start | bytes 28
Sparse Core Ops, SparseCore 0:
  72.8 62.8 reduce-scatter.5
  174.3 215.5 all-reduce.7
  454.3 60.2 reduce-scatter.7
  553.3 215.6 all-reduce.9
  794.7 56.7 all-gather.4
  855.0 68.5 reduce-scatter.9
  928.0 75.4 reduce-scatter.11
  1006.1 216.6 all-reduce.11
  1225.4 114.4 reduce-scatter.13
where the time goes:
time: 1350 us
  waiting for transfers between devices  972 us (72%)
  blocking collectives  314 us (23%)
  matrix products  30.8 us (2%)
  between operations  14.7 us (1%)
  other arithmetic  14.4 us (1%)
    unnamed x12, waiting for transfers between devices  608 us
    reduce_scatter x4, waiting for transfers between devices, delta_of(): lax.psum_scatter(jnp.concatenate([gate_part, upper_part], axis=1).astype(...  230 us
    all_gather x4, blocking collectives, delta_of(): hidden = lax.all_gather(hidden_share, 'gx', axis=0, tiled=True)  139 us
    reduce_scatter x1, waiting for transfers between devices, delta_of(): lax.psum_scatter(jnp.dot(block_rows, down_weight, preferred_element_type=...  116 us
    all_gather x3, blocking collectives, delta_of(): normed = lax.all_gather(normed_share, 'gy', axis=0, tiled=True)  103 us
    psum x3, blocking collectives, delta_of(): squares = lax.psum(jnp.sum(float_rows * float_rows, axis=1), 'gx')  72.3 us
  transfers between devices with their start and end apart: 9, of which 9 were waited for; matrix products, arithmetic and copies ran while one was open for 2% of the time, Pallas kernels for 0%

commit v1 on v0

v1 whole, which is shorter than its diff:
```python
import jax
import jax.numpy as jnp
from jax import lax
from jax.sharding import Mesh
from jax.sharding import PartitionSpec as P

D = 16384
DRAFT_STEPS = 3
POS = 4
SIZES = {"y": 4, "xh": 2, "xl": 2, "z": 8, "c": 2}
NAMES = tuple(SIZES)
GX = ("y", "xh")
CHIPS = ("xl", "z")
N_GX = 8
N_CHIPS = 16
LANES = 128
epsilon = 1e-05
SHRINK = 2.0**-12


def swap_core(x):
    return lax.ppermute(x, "c", [(0, 1), (1, 0)])


def exchange(x, axes):
    return lax.all_to_all(x, axes, 0, 0)


def spread(x, axes, count):
    return exchange(jnp.broadcast_to(x[None], (count,) + x.shape), axes)


def both_cores(own, core):
    other = swap_core(own)
    first = jnp.where(core == 0, own, other)
    second = jnp.where(core == 0, other, own)
    return jnp.concatenate([first, second], axis=0)


def sum_cores(partial, core):
    half = partial.shape[0] // 2
    low, high = partial[:half], partial[half:]
    other = swap_core(jnp.where(core == 0, high, low))
    own = jnp.where(core == 0, low, high)
    return (own.astype(jnp.float32) + other.astype(jnp.float32)).astype(jnp.bfloat16)


def feed_forward(rows, weights):
    gain, gate_weight, up_weight, down_weight = weights
    count, width = rows.shape
    units = gate_weight.shape[1]
    wide = rows.astype(jnp.float32)
    squares = jnp.sum(wide * wide, axis=1, keepdims=True)
    high = squares.astype(jnp.bfloat16)
    rest = squares - high.astype(jnp.float32)
    low = jnp.where(jnp.isfinite(rest), rest, 0.0).astype(jnp.bfloat16)
    scaled = (wide * (gain.astype(jnp.float32) * SHRINK)).astype(jnp.bfloat16)
    gate = jnp.dot(scaled, gate_weight, preferred_element_type=jnp.float32).astype(jnp.bfloat16)
    up = jnp.dot(scaled, up_weight, preferred_element_type=jnp.float32).astype(jnp.bfloat16)
    lane = lax.broadcasted_iota(jnp.int32, (count, LANES), 1)
    extra = jnp.where(lane == 0, high, jnp.where(lane == 1, low, jnp.zeros_like(high)))
    packet = jnp.concatenate([gate, up, extra], axis=1)
    packet = exchange(packet.reshape(N_GX, count // N_GX, 2 * units + LANES), GX)
    total = jnp.sum(packet.astype(jnp.float32), axis=0)
    sums = total[:, 2 * units : 2 * units + 1] + total[:, 2 * units + 1 : 2 * units + 2]
    scale = lax.rsqrt(sums / D + epsilon) * (1.0 / SHRINK)
    gate = total[:, :units] * scale
    up = total[:, units : 2 * units] * scale
    hidden = (jax.nn.silu(gate) * up).astype(jnp.bfloat16)
    hidden = spread(hidden, GX, N_GX).reshape(count, units)
    return jnp.dot(hidden, down_weight, preferred_element_type=jnp.float32).astype(jnp.bfloat16)


def shards(draft_in, verify_in, accept_len, norm_gain, gate_weight, up_weight, down_weight):
    weights = (norm_gain, gate_weight, up_weight, down_weight)
    core = lax.axis_index("c")
    n_draft, width = draft_in.shape
    n_verify = verify_in.shape[0]
    fold = n_verify // n_draft
    thin = width // fold
    all_draft, all_verify = N_CHIPS * n_draft, N_CHIPS * n_verify

    packet = jnp.concatenate([verify_in, draft_in.reshape(n_verify, thin)], axis=1)
    packet = spread(packet, CHIPS, N_CHIPS)
    own = jnp.concatenate(
        [
            packet[:, :, width:].reshape(all_draft, width),
            packet[:, :, :width].reshape(all_verify, width),
        ],
        axis=0,
    )
    partial = sum_cores(feed_forward(both_cores(own, core), weights), core)
    packet = jnp.concatenate(
        [
            partial[all_draft:].reshape(N_CHIPS, n_verify, width),
            partial[:all_draft].reshape(N_CHIPS, n_verify, thin),
        ],
        axis=2,
    )
    change = jnp.sum(exchange(packet, CHIPS).astype(jnp.float32), axis=0)
    live = (
        (jnp.arange(POS, dtype=jnp.int32)[None, :] <= accept_len[:, None])
        .reshape(-1, 1)
        .astype(jnp.float32)
    )
    verify_out = (verify_in.astype(jnp.float32) + live * change[:, :width]).astype(jnp.bfloat16)
    state = draft_in.astype(jnp.float32) + change[:, width:].reshape(n_draft, width)
    state = state.astype(jnp.bfloat16)

    for step in range(1, DRAFT_STEPS):
        own = spread(state, CHIPS, N_CHIPS).reshape(all_draft, width)
        partial = sum_cores(feed_forward(both_cores(own, core), weights), core)
        packet = exchange(partial.reshape(N_CHIPS, n_draft, width), CHIPS)
        change = jnp.sum(packet.astype(jnp.float32), axis=0)
        state = (state.astype(jnp.float32) + change).astype(jnp.bfloat16)
    return state, verify_out


def solution(mesh):
    split = Mesh(mesh.devices.reshape(tuple(SIZES.values())), NAMES)
    gy = ("xl", "z", "c")
    placed = (P(gy, GX), P(gy, GX), P(gy), P(GX), P(GX, gy), P(GX, gy), P(gy, GX))
    return jax.shard_map(
        shards,
        mesh=split,
        in_specs=placed,
        out_specs=(P(gy, GX), P(gy, GX)),
        check_vma=False,
    )
```

time: 1350 us -> 217 us (0.16)
  waiting for transfers between devices: 972 us -> 17.2 us
  blocking collectives: 314 us -> 172 us
  matrix products: 30.8 us -> 12.9 us
  between operations: 14.7 us -> 1.16 us
    unnamed x12 -> x0, waiting for transfers between devices: 608 us -> none
    reduce_scatter x5 -> x0, waiting for transfers between devices: 346 us -> none  [the longest x4 230 us: delta_of(): lax.psum_scatter(jnp.concatenate([gate_part, upper_part], axis=1).astype(...]
    all_gather x7 -> x0, blocking collectives: 242 us -> none  [the longest x4 139 us: delta_of(): hidden = lax.all_gather(hidden_share, 'gx', axis=0, tiled=True)]
    all_to_all x0 -> x11, blocking collectives: none -> 172 us  [exchange(): return lax.all_to_all(x, axes, 0, 0)]
    psum x3 -> x0, blocking collectives: 72.3 us -> none  [delta_of(): squares = lax.psum(jnp.sum(float_rows * float_rows, axis=1), 'gx')]
    dot_general x12 -> x9, matrix products: 30.8 us -> 12.9 us  [the longest x3 6.97 us: feed_forward(): jnp.dot(scaled, gate_weight, preferred_element_type=jnp.float32)]
    all_gather x1 -> x0, waiting for transfers between devices: 17.4 us -> none  [delta_of(): normed = lax.all_gather(normed_share, 'gy', axis=0, tiled=True)]
  transfers between devices with their start and end apart: 9 -> 7, of which waited for: 9 -> 7; matrix products, arithmetic and copies ran while one was open for 2% -> 0% of each run, Pallas kernels for 0% -> 0%
where the time goes in v1:
time: 217 us
  blocking collectives  172 us (79%)
  waiting for transfers between devices  17.2 us (8%)
  matrix products  12.9 us (6%)
  other arithmetic  5.73 us (3%)
  starting transfers between devices  4.56 us (2%)
  local copies, waits for them, and re-layouts  2.86 us (1%)
    all_to_all x11, blocking collectives, exchange(): return lax.all_to_all(x, axes, 0, 0)  172 us
    ppermute x6, waiting for transfers between devices, swap_core(): return lax.ppermute(x, 'c', [(0, 1), (1, 0)])  9.29 us
    all_to_all x1, waiting for transfers between devices, exchange(): return lax.all_to_all(x, axes, 0, 0)  7.89 us
    dot_general x3, matrix products, feed_forward(): jnp.dot(scaled, gate_weight, preferred_element_type=jnp.float32)  6.97 us
  transfers between devices with their start and end apart: 7, of which 7 were waited for; matrix products, arithmetic and copies ran while one was open for 0% of the time, Pallas kernels for 0%

profile of v1, /device:TPU:32, one launch (start us, length us, event | category | flops | bytes accessed | tf_op | source)
XLA Modules:
  0.0 216.6 jit_solution(8197101346268075015)
XLA Ops:
  0.6 0.7 reshape.126
  1.4 0.8 pad_maximum_fusion.12
  2.2 28.5 %all_to_all.60 = bf16[16,8,2560]{2,1,0:T(8,128)(2,1)S(1)} all-to-all(bf16[16,8,2560]{2,1,0:T(8,128)(2,1)S(1)} %broadcast_in_dim.115), channel_id=1, replica_groups=mesh['y'=4,'xh'=2,'xl'=2,'z'=8,'c'=2] {'xl','z'}, dimensions={0} | all-to-all | bytes 1310720 | tf_op jit(solution)/shard_map/all_to_all | solution.py:26
  31.0 2.0 collective-permute-done
  33.0 0.3 broadcast_select_fusion.2
  33.4 0.4 fusion.1
  33.7 1.5 convolution_convert_fusion.4
  35.3 0.5 copy-done.1
  35.8 1.5 convolution_convert_fusion.3
  37.3 0.1 select_select_fusion
  37.6 26.2 %all_to_all.61 = bf16[8,40,1920]{2,1,0:T(8,128)(2,1)S(1)} all-to-all(bf16[8,40,1920]{2,1,0:T(8,128)(2,1)S(1)} %bitcast.26), channel_id=1, replica_groups=mesh['y'=4,'xh'=2,'xl'=2,'z'=8,'c'=2] {'y','xh'}, dimensions={0} | all-to-all | bytes 2457600 | tf_op jit(solution)/shard_map/all_to_all | solution.py:26
  63.8 0.2 convert_reduce_fusion
  63.9 0.2 fusion.26
  64.1 0.1 fusion.13
  64.3 14.1 %all_to_all.62 = bf16[8,40,896]{2,1,0:T(8,128)(2,1)S(1)} all-to-all(bf16[8,40,896]{2,1,0:T(8,128)(2,1)S(1)} %broadcast_in_dim.120), channel_id=1, replica_groups=mesh['y'=4,'xh'=2,'xl'=2,'z'=8,'c'=2] {'y','xh'}, dimensions={0} | all-to-all | bytes 1146880 | tf_op jit(solution)/shard_map/all_to_all | solution.py:26
  78.4 1.5 convolution_convert_fusion
  80.1 2.1 collective-permute-done.1
  82.2 0.3 add_convert_fusion
  82.8 23.2 %all_to_all.63 = bf16[16,8,2560]{2,1,0:T(8,128)(2,1)S(1)} all-to-all(bf16[16,8,2560]{2,1,0:T(8,128)(2,1)S(1)} %pad_maximum_fusion.3), channel_id=1, replica_groups=mesh['y'=4,'xh'=2,'xl'=2,'z'=8,'c'=2] {'xl','z'}, dimensions={0} | all-to-all | bytes 1310720 | tf_op jit(solution)/shard_map/all_to_all | solution.py:26
  106.2 11.6 %all_to_all.64 = bf16[16,2,2048]{2,1,0:T(2,128)(2,1)S(1)} all-to-all(bf16[16,2,2048]{2,1,0:T(2,128)(2,1)S(1)} %broadcast_in_dim.121), channel_id=1, replica_groups=mesh['y'=4,'xh'=2,'xl'=2,'z'=8,'c'=2] {'xl','z'}, dimensions={0} | all-to-all | bytes 262144 | tf_op jit(solution)/shard_map/all_to_all | solution.py:26
  118.0 1.3 collective-permute-done.2
  119.4 2.7 %convolution_convert_fusion.8 = bf16[64,896]{1,0:T(8,128)(2,1)S(1)} fusion(bf16[2048,896]{1,0:T(8,128)(2,1)} %param.11, f32[2048]{0:T(1024)S(1)} %convert_multiply_fusion.6, bf16[32,2048]{1,0:T(8,128)(2,1)S(1)} %get-tuple-element.9, bf16[32,2048]{1,0:T(8,128)(2,1)S(1)} %get-tuple-element.8), kind=kOutput, calls=%fused_computation.17 | convolution fusion | flops 235724800 | bytes 4055040 | tf_op jit(solution)/shard_map/dot_general | solution.py:58
  122.1 0.7 convolution_convert_fusion.7
  122.8 0.2 fusion.5
  123.1 11.7 %all_to_all.65 = bf16[8,8,1920]{2,1,0:T(8,128)(2,1)S(1)} all-to-all(bf16[8,8,1920]{2,1,0:T(8,128)(2,1)S(1)} %maximum_bitcast_fusion), channel_id=1, replica_groups=mesh['y'=4,'xh'=2,'xl'=2,'z'=8,'c'=2] {'y','xh'}, dimensions={0} | all-to-all | bytes 491520 | tf_op jit(solution)/shard_map/all_to_all | solution.py:26
  134.9 0.2 fusion.36
  135.2 10.7 %all_to_all.66 = bf16[8,8,896]{2,1,0:T(8,128)(2,1)S(1)} all-to-all(bf16[8,8,896]{2,1,0:T(8,128)(2,1)S(1)} %broadcast_in_dim.126), channel_id=1, replica_groups=mesh['y'=4,'xh'=2,'xl'=2,'z'=8,'c'=2] {'y','xh'}, dimensions={0} | all-to-all | bytes 229376 | tf_op jit(solution)/shard_map/all_to_all | solution.py:26
  145.8 0.8 convolution_convert_fusion.2
  146.7 1.3 collective-permute-done.3
  148.1 0.1 reshape.137
  148.2 11.9 %all_to_all.67 = bf16[16,2,2048]{2,1,0:T(2,128)(2,1)S(1)} all-to-all(bf16[16,2,2048]{2,1,0:T(2,128)(2,1)S(1)} %reshape.137), channel_id=1, replica_groups=mesh['y'=4,'xh'=2,'xl'=2,'z'=8,'c'=2] {'xl','z'}, dimensions={0} | all-to-all | bytes 262144 | tf_op jit(solution)/shard_map/all_to_all | solution.py:26
  160.1 0.1 convert_reduce_fusion.5
  160.3 11.6 %all_to_all.68 = bf16[16,2,2048]{2,1,0:T(2,128)(2,1)S(1)} all-to-all(bf16[16,2,2048]{2,1,0:T(2,128)(2,1)S(1)} %broadcast_in_dim.127), channel_id=1, replica_groups=mesh['y'=4,'xh'=2,'xl'=2,'z'=8,'c'=2] {'xl','z'}, dimensions={0} | all-to-all | bytes 262144 | tf_op jit(solution)/shard_map/all_to_all | solution.py:26
  172.1 1.3 collective-permute-done.4
  173.4 2.7 %convolution_convert_fusion.6 = bf16[64,896]{1,0:T(8,128)(2,1)S(1)} fusion(bf16[2048,896]{1,0:T(8,128)(2,1)} %param.11, f32[2048]{0:T(1024)S(1)} %convert_multiply_fusion.6, bf16[32,2048]{1,0:T(8,128)(2,1)S(1)} %get-tuple-element.7, bf16[32,2048]{1,0:T(8,128)(2,1)S(1)} %get-tuple-element.6), kind=kOutput, calls=%fused_computation.15 | convolution fusion | flops 235724800 | bytes 4055040 | tf_op jit(solution)/shard_map/dot_general | solution.py:58
  176.2 0.7 convolution_convert_fusion.5
  176.9 0.2 fusion.7
  177.2 12.0 %all_to_all.69 = bf16[8,8,1920]{2,1,0:T(8,128)(2,1)S(1)} all-to-all(bf16[8,8,1920]{2,1,0:T(8,128)(2,1)S(1)} %maximum_bitcast_fusion.1), channel_id=1, replica_groups=mesh['y'=4,'xh'=2,'xl'=2,'z'=8,'c'=2] {'y','xh'}, dimensions={0} | all-to-all | bytes 491520 | tf_op jit(solution)/shard_map/all_to_all | solution.py:26
  189.3 0.2 fusion.31
  189.6 10.7 %all_to_all.70 = bf16[8,8,896]{2,1,0:T(8,128)(2,1)S(1)} all-to-all(bf16[8,8,896]{2,1,0:T(8,128)(2,1)S(1)} %broadcast_in_dim.130), channel_id=1, replica_groups=mesh['y'=4,'xh'=2,'xl'=2,'z'=8,'c'=2] {'y','xh'}, dimensions={0} | all-to-all | bytes 229376 | tf_op jit(solution)/shard_map/all_to_all | solution.py:26
  200.3 0.8 convolution_convert_fusion.1
  201.3 1.2 collective-permute-done.5
  202.5 0.7 reshape.141
  203.3 4.0 %all-to-all-start.11 = ((bf16[16,2,2048]{2,1,0:T(2,128)(2,1)}), bf16[16,2,2048]{2,1,0:T(2,128)(2,1)S(1)}, u32[]{:S(2)}, u32[]{:S(2)}) async-start(bf16[16,2,2048]{2,1,0:T(2,128)(2,1)} %reshape.141), calls=%async_computation.11 | async-start | bytes 262144 | tf_op jit(solution)/shard_map/all_to_all | solution.py:26
  207.3 0.7 fusion.17
  208.0 7.9 %all-to-all-done.11 = bf16[16,2,2048]{2,1,0:T(2,128)(2,1)S(1)} async-done(((bf16[16,2,2048]{2,1,0:T(2,128)(2,1)}), bf16[16,2,2048]{2,1,0:T(2,128)(2,1)S(1)}, u32[]{:S(2)}, u32[]{:S(2)}) %all-to-all-start.11) | async-done | bytes 131104 | tf_op jit(solution)/shard_map/all_to_all | solution.py:26
  215.9 0.1 convert_reduce_fusion.4
  216.0 0.6 add_convert_fusion.3
  (71 shorter events, 2.5 us)
Async XLA Ops:
  0.6 30.4 %copy-start.9 = (bf16[2048]{0:T(1024)(128)(2,1)S(1)}, bf16[2048]{0:T(1024)(128)(2,1)}, u32[]{:S(2)}) copy-start(bf16[2048]{0:T(1024)(128)(2,1)} %param.10) | copy-start | bytes 12292
  30.9 2.2 %collective-permute-start = (bf16[160,2048]{1,0:T(8,128)(2,1)S(1)}, bf16[160,2048]{1,0:T(8,128)(2,1)S(1)}, u32[]{:S(2)}, u32[]{:S(2)}) collective-permute-start(bf16[160,2048]{1,0:T(8,128)(2,1)S(1)} %pad_maximum_fusion.2), channel_id=1, source_target_pairs={{0,1},{1,0},{2,3},{3,2},{4,5},{5,4},{6,7},{7,6},{8,9},{9,8},{10,11... | collective-permute-start | bytes 1966088 | tf_op jit(solution)/shard_map/ppermute | solution.py:22
  31.0 2.8 %copy-start = (bf16[2048,896]{1,0:T(8,128)(2,1)S(1)}, bf16[2048,896]{1,0:T(8,128)(2,1)}, u32[]{:S(2)}) copy-start(bf16[2048,896]{1,0:T(8,128)(2,1)} %param.11) | copy-start | bytes 11010052
  33.7 2.0 copy-start.1
  37.6 40.9 %copy-start.4 = (bf16[896,2048]{1,0:T(8,128)(2,1)S(1)}, bf16[896,2048]{1,0:T(8,128)(2,1)}, u32[]{:S(2)}) copy-start(bf16[896,2048]{1,0:T(8,128)(2,1)} %param.13) | copy-start | bytes 11010052
  80.0 2.2 %collective-permute-start.1 = (bf16[160,2048]{1,0:T(8,128)(2,1)S(1)}, bf16[160,2048]{1,0:T(8,128)(2,1)S(1)}, u32[]{:S(2)}, u32[]{:S(2)}) collective-permute-start(bf16[160,2048]{1,0:T(8,128)(2,1)S(1)} %broadcast_select_fusion), channel_id=1, source_target_pairs={{0,1},{1,0},{2,3},{3,2},{4,5},{5,4},{6,7},{7,6},{8,9},{9,8},{10,11... | collective-permute-start | bytes 1966088 | tf_op jit(solution)/shard_map/ppermute | solution.py:22
  82.5 23.5 %copy-start.8 = (bf16[2,2048]{1,0:T(2,128)(2,1)S(1)}, bf16[2,2048]{1,0:T(2,128)(2,1)}, u32[]{:S(2)}) copy-start(bf16[2,2048]{1,0:T(2,128)(2,1)} %param.7) | copy-start | bytes 24580
  117.9 4.2 %copy-start.2 = (bf16[2048,896]{1,0:T(8,128)(2,1)S(1)}, bf16[2048,896]{1,0:T(8,128)(2,1)}, u32[]{:S(2)}) copy-start(bf16[2048,896]{1,0:T(8,128)(2,1)} %param.12) | copy-start | bytes 11010052
  117.9 1.4 collective-permute-start.2
  122.1 23.7 %copy-start.5 = (bf16[896,2048]{1,0:T(8,128)(2,1)S(1)}, bf16[896,2048]{1,0:T(8,128)(2,1)}, u32[]{:S(2)}) copy-start(bf16[896,2048]{1,0:T(8,128)(2,1)} %param.13) | copy-start | bytes 11010052
  146.6 1.4 collective-permute-start.3
  172.0 4.2 %copy-start.3 = (bf16[2048,896]{1,0:T(8,128)(2,1)S(1)}, bf16[2048,896]{1,0:T(8,128)(2,1)}, u32[]{:S(2)}) copy-start(bf16[2048,896]{1,0:T(8,128)(2,1)} %param.12) | copy-start | bytes 11010052
  172.0 1.4 collective-permute-start.4
  176.2 24.1 %copy-start.6 = (bf16[896,2048]{1,0:T(8,128)(2,1)S(1)}, bf16[896,2048]{1,0:T(8,128)(2,1)}, u32[]{:S(2)}) copy-start(bf16[896,2048]{1,0:T(8,128)(2,1)} %param.13) | copy-start | bytes 11010052
  189.2 11.9 %copy-start.10 = (s32[2]{0:T(128)S(1)}, s32[2]{0:T(128)}, u32[]{:S(2)}) copy-start(s32[2]{0:T(128)} %param.9) | copy-start | bytes 28
  200.2 7.0 %copy-start.7 = (bf16[8,2048]{1,0:T(8,128)(2,1)S(1)}, bf16[8,2048]{1,0:T(8,128)(2,1)}, u32[]{:S(2)}) copy-start(bf16[8,2048]{1,0:T(8,128)(2,1)} %param.8) | copy-start | bytes 98308
  201.0 1.4 collective-permute-start.5
  203.3 12.6 %all-to-all-start.11 = ((bf16[16,2,2048]{2,1,0:T(2,128)(2,1)}), bf16[16,2,2048]{2,1,0:T(2,128)(2,1)S(1)}, u32[]{:S(2)}, u32[]{:S(2)}) async-start(bf16[16,2,2048]{2,1,0:T(2,128)(2,1)} %reshape.141), calls=%async_computation.11 | async-start | bytes 262144 | tf_op jit(solution)/shard_map/all_to_all | solution.py:26

commit v2 on v1

v2 whole, which is shorter than its diff:
```python
import math

import jax
import jax.numpy as jnp
from jax import lax
from jax.experimental import pallas as pl
from jax.experimental.pallas import tpu as pltpu
from jax.sharding import Mesh
from jax.sharding import PartitionSpec as P

D = 16384
DRAFT_STEPS = 3
POS = 4
SIZES = {"y": 4, "xh": 2, "xl": 2, "z": 8, "c": 2}
NAMES = tuple(SIZES)
GX = ("y", "xh")
CHIPS = ("xl", "z")
N_GX = 8
N_CHIPS = 16
LANES = 128
LOAD = 32 << 20
epsilon = 1e-05
SHRINK = 2.0**-12


def swap(x, axis, distance):
    return lax.ppermute(x, axis, [(i, i ^ distance) for i in range(SIZES[axis])])


def exchange(x, axes):
    return lax.all_to_all(x, axes, 0, 0)


def repeat_kernel(x, out):
    values = x[...]
    for i in range(out.shape[0]):
        out[i] = values


def stack_kernel(first, second, out):
    count = first.shape[0]
    out[:count] = first[...]
    out[count:] = second[...]


def packet_kernel(verify, draft, out):
    width, thin = verify.shape[1], out.shape[2] - verify.shape[1]
    rows = draft[...].astype(jnp.float32)
    folded = [
        rows[r : r + 1, k * thin : (k + 1) * thin]
        for r in range(rows.shape[0])
        for k in range(width // thin)
    ]
    folded = jnp.concatenate(folded, axis=0).astype(out.dtype)
    values = verify[...]
    for i in range(out.shape[0]):
        out[i, :, :width] = values
        out[i, :, width:] = folded


def columns_kernel(blocks, out):
    size = blocks.shape[2]
    for k in range(blocks.shape[0]):
        out[:, k * size : (k + 1) * size] = blocks[k]


def rearrange(kernel, arrays, shape, name, load=0):
    vmem = pl.BlockSpec(memory_space=pltpu.VMEM)
    return pl.pallas_call(
        kernel,
        out_shape=jax.ShapeDtypeStruct(shape, jnp.bfloat16),
        in_specs=[vmem] * len(arrays),
        out_specs=vmem,
        compiler_params=pltpu.CompilerParams(vmem_limit_bytes=8 << 20),
        cost_estimate=pl.CostEstimate(
            flops=load * 600, bytes_accessed=4 * math.prod(shape) + load, transcendentals=0
        ),
        name=name,
    )(*arrays)


def spread(x, axes, count):
    copies = rearrange(repeat_kernel, (x,), (count,) + x.shape, "repeat", LOAD)
    return exchange(copies, axes)


def wide(x):
    return x.astype(jnp.float32)


def narrow(x):
    return x.astype(jnp.bfloat16)


def pair(own, axis, distance):
    return jnp.concatenate([own, swap(own, axis, distance)], axis=0)


def halves(rows, upper=None):
    half = rows.shape[0] // 2
    low, high = rows[:half], rows[half:]
    if upper is None:
        return low, high
    return jnp.where(upper, high, low), jnp.where(upper, low, high)


def columns(blocks):
    count, rows, lanes = blocks.shape
    return rearrange(columns_kernel, (blocks,), (rows, count * lanes), "columns")


def blocks_of(x, count):
    return jnp.transpose(x.reshape(x.shape[0], count, -1), (1, 0, 2))


def summed(packet):
    return jnp.sum(wide(packet), axis=0)


def up_product(rows, gain, marks, weights):
    gate_weight, up_weight = weights[:2]
    values = wide(rows)
    squares = jnp.sum(values * values, axis=1, keepdims=True)
    high = narrow(squares)
    rest = squares - wide(high)
    low = narrow(jnp.where(jnp.isfinite(rest), rest, 0.0))
    scaled = narrow(values * gain)
    gate = narrow(jnp.dot(scaled, gate_weight, preferred_element_type=jnp.float32))
    up = narrow(jnp.dot(scaled, up_weight, preferred_element_type=jnp.float32))
    first, second = marks
    extra = jnp.where(first, high, jnp.where(second, low, jnp.zeros_like(high)))
    return jnp.concatenate([gate, up, extra], axis=1)


def activate(total):
    units = (total.shape[1] - LANES) // 2
    sums = total[:, 2 * units : 2 * units + 1] + total[:, 2 * units + 1 : 2 * units + 2]
    scale = lax.rsqrt(sums / D + epsilon) * (1.0 / SHRINK)
    gate = total[:, :units] * scale
    up = total[:, units : 2 * units] * scale
    return narrow(jax.nn.silu(gate) * up)


def down_product(hidden, weights):
    return narrow(jnp.dot(hidden, weights[2], preferred_element_type=jnp.float32))


def shards(draft_in, verify_in, accept_len, norm_gain, gate_weight, up_weight, down_weight):
    weights = (gate_weight, up_weight, down_weight)
    n_draft, width = draft_in.shape
    n_verify = verify_in.shape[0]
    units = gate_weight.shape[1]
    thin = n_draft * width // n_verify
    all_draft, all_verify = N_CHIPS * n_draft, N_CHIPS * n_verify
    y, x_low, z = lax.axis_index("y"), lax.axis_index("xl"), lax.axis_index("z")
    near, across, far = y % 2 == 1, lax.axis_index("xh") == 1, y // 2 == 1
    chip = x_low * SIZES["z"] + z
    near, column = lax.optimization_barrier((near, chip * LANES))
    mine = (lax.broadcasted_iota(jnp.int32, (1, width), 1) // LANES) == chip
    always = accept_len[0] >= 0

    def part(body, *operands):
        def empty(*rest):
            return jax.tree.map(
                lambda a: jnp.zeros(a.shape, a.dtype), jax.eval_shape(body, *rest)
            )

        return lax.cond(always, body, empty, *operands)

    def beside(send, axis, distance, body, *operands):
        send, operands = lax.optimization_barrier((send, operands))
        arrived = swap(send, axis, distance)
        result = part(body, *operands)
        return lax.optimization_barrier((arrived, result))

    def add(keep, arrived):
        return wide(keep) + wide(arrived)

    def first_rows(draft, verify, gain):
        shape = (N_CHIPS, n_verify, width + thin)
        packet = exchange(rearrange(packet_kernel, (verify, draft), shape, "packet"), CHIPS)
        draft = packet[:, :, width:].reshape(all_draft, width)
        verify = packet[:, :, :width].reshape(all_verify, width)
        shape = (all_draft + all_verify, width)
        rows = pair(rearrange(stack_kernel, (draft, verify), shape, "stack", LOAD), "c", 1)
        gain = wide(gain) * SHRINK
        lane = lax.broadcasted_iota(jnp.int32, (1, LANES), 1)
        marks = lane == 0, lane == 1
        low, high = halves(up_product(rows, gain, marks, weights))
        keep = jnp.where(near, high[all_draft:], low[all_draft:])
        send = jnp.where(near, low[all_draft:], high[all_draft:])
        state = lax.dynamic_slice(
            draft, (0, column), (all_draft, LANES), allow_negative_indices=False
        )
        packet = jnp.concatenate([low[:all_draft], high[:all_draft]], axis=0)
        return packet, state, keep, send, gain, marks

    def rows_in(state, gain, marks):
        own = columns(spread(state, CHIPS, N_CHIPS))
        return up_product(pair(own, "c", 1), gain, marks, weights)

    def sum_width(packet):
        packet = packet.reshape(N_GX, -1, packet.shape[1])
        return activate(summed(exchange(packet, GX)))

    def share_hidden(hidden):
        hidden = spread(hidden, GX, N_GX).reshape(-1, units)
        keep, send = halves(down_product(hidden, weights))
        return narrow(add(keep, swap(send, "c", 1)))

    def share_last(hidden, state):
        hidden = spread(hidden, GX, N_GX).reshape(-1, units)
        keep, send = halves(down_product(hidden, weights))
        total = add(keep, swap(send, "c", 1))
        return narrow(total + jnp.where(mine, jnp.tile(wide(state), (1, N_CHIPS)), 0.0))

    def share_both(hidden, verify):
        n_own = hidden.shape[0]
        both = spread(jnp.concatenate([hidden, verify], axis=0), GX, N_GX)
        hidden = both[:, :n_own].reshape(-1, units)
        verify = both[:, n_own:].reshape(2, 2, 2, 2, 2, n_verify, units)
        verify = jnp.transpose(verify, (1, 2, 4, 3, 0, 5, 6)).reshape(2, all_verify, units)
        half = all_draft
        rows = [hidden[:half], verify[0], hidden[half:], verify[1]]
        keep, send = halves(down_product(jnp.concatenate(rows, axis=0), weights))
        total = narrow(add(keep, swap(send, "c", 1)))
        return total[:half], total[half:]

    def sum_units(partial, state):
        change = summed(exchange(blocks_of(partial, N_CHIPS), CHIPS))
        return narrow(wide(state) + change)

    def last_sum(partial):
        return narrow(summed(exchange(partial.reshape(N_CHIPS, n_draft, width), CHIPS)))

    packet, state, keep, send, gain, marks = part(first_rows, draft_in, verify_in, norm_gain)
    hidden = part(sum_width, packet)
    arrived, partial = beside(send, "y", 1, share_hidden, hidden)
    keep, send = halves(narrow(add(keep, arrived)), across)
    arrived, state = beside(send, "xh", 1, sum_units, partial, state)
    keep, send = halves(narrow(add(keep, arrived)), far)
    arrived, packet = beside(send, "y", 2, rows_in, state, gain, marks)
    verify = activate(add(keep, arrived))
    hidden = part(sum_width, packet)
    partial, verify = part(share_both, hidden, verify)
    keep, send = halves(verify, x_low == 1)
    arrived, state = beside(send, "xl", 1, sum_units, partial, state)
    keep, send = halves(narrow(add(keep, arrived)), z % 2 == 1)
    arrived, packet = beside(send, "z", 1, rows_in, state, gain, marks)
    keep, send = halves(narrow(add(keep, arrived)), z // 2 % 2 == 1)
    arrived, hidden = beside(send, "z", 2, sum_width, packet)
    keep, send = halves(narrow(add(keep, arrived)), z // 4 == 1)
    arrived, partial = beside(send, "z", 4, share_last, hidden, state)
    live = (
        (jnp.arange(POS, dtype=jnp.int32)[None, :] <= accept_len[:, None])
        .reshape(-1, 1)
        .astype(jnp.float32)
    )
    verify_out = narrow(wide(verify_in) + live * add(keep, arrived))
    draft_out = part(last_sum, partial)
    return draft_out, verify_out


def solution(mesh):
    split = Mesh(mesh.devices.reshape(tuple(SIZES.values())), NAMES)
    gy = ("xl", "z", "c")
    placed = (P(gy, GX), P(gy, GX), P(gy), P(GX), P(GX, gy), P(GX, gy), P(gy, GX))
    return jax.shard_map(
        shards,
        mesh=split,
        in_specs=placed,
        out_specs=(P(gy, GX), P(gy, GX)),
        check_vma=False,
    )
```

time: 217 us -> 209 us (0.963)
  waiting for transfers between devices: 17.2 us -> 8.86 us
  starting transfers between devices: 4.56 us -> 9.44 us
  matrix products: 12.9 us -> 8.88 us
    ppermute x6 -> x13, starting transfers between devices: 0.56 us -> 9.44 us  [swap(): lax.ppermute(x, axis, [(i, i ^ distance) for i in range(SIZES[axis])])]
    all_to_all x1 -> x0, waiting for transfers between devices: 7.89 us -> none  [exchange(): return lax.all_to_all(x, axes, 0, 0)]
    dot_general x9, matrix products: 12.9 us -> 8.88 us  [the longest x3 3.05 us: down_product(): jnp.dot(hidden, weights[2], preferred_element_type=jnp.float32)]
    all_to_all x1 -> x0, starting transfers between devices: 4.01 us -> none  [exchange(): return lax.all_to_all(x, axes, 0, 0)]
    all_to_all x11 -> x12, blocking collectives: 172 us -> 170 us  [exchange(): return lax.all_to_all(x, axes, 0, 0)]
    ppermute x6 -> x13, waiting for transfers between devices: 9.29 us -> 8.86 us  [swap(): lax.ppermute(x, axis, [(i, i ^ distance) for i in range(SIZES[axis])])]
  transfers between devices with their start and end apart: 7 -> 13, of which waited for: 7 -> 6; matrix products, arithmetic and copies ran while one was open for 0% -> 3% of each run, Pallas kernels for 0% -> 0%
where the time goes in v2:
time: 209 us; the launch traced here: 208 us
  blocking collectives  170 us (81%)
  starting transfers between devices  9.44 us (5%)
  matrix products  8.88 us (4%)
  waiting for transfers between devices  8.86 us (4%)
  other arithmetic  4.44 us (2%)
  local copies, waits for them, and re-layouts  2.94 us (1%)
    all_to_all x12, blocking collectives, exchange(): return lax.all_to_all(x, axes, 0, 0)  170 us
    ppermute x13, starting transfers between devices, swap(): lax.ppermute(x, axis, [(i, i ^ distance) for i in range(SIZES[axis])])  9.44 us
    ppermute x13, waiting for transfers between devices, swap(): lax.ppermute(x, axis, [(i, i ^ distance) for i in range(SIZES[axis])])  8.86 us
  transfers between devices with their start and end apart: 13, of which 6 were waited for; matrix products, arithmetic and copies ran while one was open for 3% of the time, Pallas kernels for 0%

profile of v2, /device:TPU:32, one launch (start us, length us, event | category | flops | bytes accessed | tf_op | source)
XLA Modules:
  0.0 207.8 jit_solution(16697448485127898734)
XLA Ops:
  1.3 36.6 %conditional.12 = (bf16[32,128]{1,0:T(8,128)(2,1)S(1)}, bf16[128,1920]{1,0:T(8,128)(2,1)S(1)}, f32[2048]{0:T(1024)S(1)}, pred[1,128]{1,0:T(4,128)(4,1)S(1)}, pre...) conditional(s32[]{:T(128)} %bitcast.18, () %tuple.112, ...), branch_computations={%region_0.1_spmd, %region_1.3_spmd} | conditional | flops 22500808704 | bytes 90064880 | solution.py:168
  1.3 0.8 packet.1
  2.1 28.5 %all_to_all.48 = bf16[16,8,2560]{2,1,0:T(8,128)(2,1)S(1)} all-to-all(bf16[16,8,2560]{2,1,0:T(8,128)(2,1)S(1)} %packet.1), channel_id=1, replica_groups=mesh['y'=4,'xh'=2,'xl'=2,'z'=8,'c'=2] {'xl','z'}, dimensions={0} | all-to-all | bytes 1310720 | tf_op jit(solution)/shard_map/cond/branch_1_fun/all_to_all | solution.py:31
  31.5 1.5 collective-permute-done
  33.6 1.5 convolution_convert_fusion.1
  35.1 0.5 copy-done.3
  35.6 1.5 convolution_convert_fusion
  37.9 15.6 %conditional.13 = (bf16[8,896]{1,0:T(8,128)(2,1)S(1)}) conditional(s32[]{:T(128)} %bitcast.18, () %tuple.115, bf16[64,1920]{1,0:T(8,128)(2,1)S(1)} %get-tuple-element.215), branch_computations={%region_3.4_spmd, %region_4.6_spmd} | conditional | flops 287776 | bytes 870536 | solution.py:168
  37.9 15.3 %all_to_all.49 = bf16[8,8,1920]{2,1,0:T(8,128)(2,1)S(1)} all-to-all(bf16[8,8,1920]{2,1,0:T(8,128)(2,1)S(1)} %bitcast.54), channel_id=1, replica_groups=mesh['y'=4,'xh'=2,'xl'=2,'z'=8,'c'=2] {'y','xh'}, dimensions={0} | all-to-all | bytes 491520 | tf_op jit(solution)/shard_map/cond/branch_1_fun/all_to_all | solution.py:31
  53.8 15.6 %conditional.14 = (bf16[32,2048]{1,0:T(8,128)(2,1)S(1)}) conditional(s32[]{:T(128)} %bitcast.18, () %tuple.117, (bf16[8,896]{1,0:T(8,128)(2,1)S(1)}, bf16[896,2048]{1,0:T(8,128)(2,1)}) %tuple.118), branch_computations={%region_6.7_spmd, %region_7.8_spmd} | conditional | flops 20367933440 | bytes 53919820 | solution.py:168
  53.9 13.4 %all_to_all.50 = bf16[8,8,896]{2,1,0:T(8,128)(2,1)S(1)} all-to-all(bf16[8,8,896]{2,1,0:T(8,128)(2,1)S(1)} %repeat.5), channel_id=1, replica_groups=mesh['y'=4,'xh'=2,'xl'=2,'z'=8,'c'=2] {'y','xh'}, dimensions={0} | all-to-all | bytes 229376 | tf_op jit(solution)/shard_map/cond/branch_1_fun/all_to_all | solution.py:31
  67.2 0.8 convolution_convert_fusion.2
  68.1 1.3 collective-permute-done.1
  69.6 1.6 collective-permute-start.7
  71.2 11.8 %conditional.15 = (bf16[32,128]{1,0:T(8,128)(2,1)S(1)}) conditional(s32[]{:T(128)} %bitcast.18, () %tuple.121, (bf16[32,128]{1,0:T(8,128)(2,1)S(1)}, bf16[32,2048]{1,0:T(8,128)(2,1)S(1)}) %tuple.122), branch_computations={%region_8.9_spmd, %region_9.11_spmd} | conditional | flops 139264 | bytes 966664 | solution.py:168
  71.3 11.7 %all_to_all.51 = bf16[16,32,128]{2,1,0:T(8,128)(2,1)S(1)} all-to-all(bf16[16,32,128]{2,1,0:T(8,128)(2,1)S(1)} %copy.19), channel_id=1, replica_groups=mesh['y'=4,'xh'=2,'xl'=2,'z'=8,'c'=2] {'xl','z'}, dimensions={0} | all-to-all | bytes 262144 | tf_op jit(solution)/shard_map/cond/branch_1_fun/all_to_all | solution.py:31
  83.2 1.6 collective-permute-start.8
  84.7 14.9 %conditional.16 = (bf16[64,1920]{1,0:T(8,128)(2,1)S(1)}) conditional(s32[]{:T(128)} %bitcast.18, () %tuple.125, (bf16[32,128]{1,0:T(8,128)(2,1)S(1)}, f32[2048]{0:T(1024)S(1)}, bf16[2048,896]{1,0:T(8,128)(2,1)}, bf16[2048,896]{1,0:T(8,128)(2,1)}, pred[1,128]{1,0:T(4,128)(4,1)S(1)}, /*index=5*/pred[1,128]{1,0:T(4,128)(4,1)S(1)}) %tuple.126), branch_computations={%region_11.12_spmd, %region_12.14_spmd} | conditional | flops 20605648896 | bytes 73106792 | solution.py:168
  84.7 11.7 %all_to_all.52.blocks = bf16[16,32,128]{2,1,0:T(8,128)(2,1)S(1)} all-to-all(bf16[16,32,128]{2,1,0:T(8,128)(2,1)S(1)} %repeat.6), channel_id=1, replica_groups=mesh['y'=4,'xh'=2,'xl'=2,'z'=8,'c'=2] {'xl','z'}, dimensions={0} | all-to-all | bytes 262144 | tf_op jit(solution)/shard_map/cond/branch_1_fun/all_to_all | solution.py:31
  96.6 1.3 collective-permute-done.2
  98.2 0.7 convolution_convert_fusion.4
  98.9 0.7 convolution_convert_fusion.3
  100.0 14.0 %conditional.17 = (bf16[8,896]{1,0:T(8,128)(2,1)S(1)}) conditional(s32[]{:T(128)} %bitcast.18, () %tuple.111, bf16[64,1920]{1,0:T(8,128)(2,1)S(1)} %get-tuple-element.327), branch_computations={%region_14.15_spmd, %region_15.17_spmd} | conditional | flops 287776 | bytes 870536 | solution.py:168
  100.0 13.6 %all_to_all.53 = bf16[8,8,1920]{2,1,0:T(8,128)(2,1)S(1)} all-to-all(bf16[8,8,1920]{2,1,0:T(8,128)(2,1)S(1)} %bitcast.55), channel_id=1, replica_groups=mesh['y'=4,'xh'=2,'xl'=2,'z'=8,'c'=2] {'y','xh'}, dimensions={0} | all-to-all | bytes 491520 | tf_op jit(solution)/shard_map/cond/branch_1_fun/all_to_all | solution.py:31
  114.0 19.1 %conditional.18 = (bf16[32,2048]{1,0:T(8,128)(2,1)S(1)}, bf16[128,2048]{1,0:T(8,128)(2,1)S(1)}, bf16[64,2048]{1,0:T(8,128)(2,1)S(1)}, bf16[64,2048]{1,0:T(8,128)(2,1)S(1)}) conditional(s32[]{:T(128)} %bitcast.18, () %tuple.110, (bf16[8,896]{1,0:T(8,128)(2,1)S(1)}, bf16[32,896]{1,0:T(8,128)(2,1)S(1)}, bf16[896,2048]{1,0:T(8,128)(2,1)}) %tuple.128), branch_computations={%region_17.18_spmd, %region_18.19_spmd} | conditional | flops 21311467520 | bytes 67465312 | solution.py:168
  114.1 14.6 %all_to_all.54 = bf16[8,40,896]{2,1,0:T(8,128)(2,1)S(1)} all-to-all(bf16[8,40,896]{2,1,0:T(8,128)(2,1)S(1)} %repeat.7), channel_id=1, replica_groups=mesh['y'=4,'xh'=2,'xl'=2,'z'=8,'c'=2] {'y','xh'}, dimensions={0} | all-to-all | bytes 1146880 | tf_op jit(solution)/shard_map/cond/branch_1_fun/all_to_all | solution.py:31
  128.8 1.5 convolution_convert_fusion.5
  130.5 2.1 %collective-permute-done.3 = bf16[160,2048]{1,0:T(8,128)(2,1)S(1)} collective-permute-done((bf16[160,2048]{1,0:T(8,128)(2,1)S(1)}, bf16[160,2048]{1,0:T(8,128)(2,1)S(1)}, u32[]{:S(2)}, u32[]{:S(2)}) %collective-permute-start.3) | collective-permute-done | bytes 655392 | tf_op jit(solution)/shard_map/cond/branch_1_fun/ppermute | solution.py:27
  133.5 13.0 %conditional.19 = (bf16[32,128]{1,0:T(8,128)(2,1)S(1)}) conditional(s32[]{:T(128)} %bitcast.18, () %tuple.130, (bf16[32,128]{1,0:T(8,128)(2,1)S(1)}, bf16[32,2048]{1,0:T(8,128)(2,1)S(1)}) %tuple.131), branch_computations={%region_19.20_spmd, %region_20.22_spmd} | conditional | flops 139264 | bytes 966664 | solution.py:168
  133.6 12.9 %all_to_all.55 = bf16[16,32,128]{2,1,0:T(8,128)(2,1)S(1)} all-to-all(bf16[16,32,128]{2,1,0:T(8,128)(2,1)S(1)} %copy.21), channel_id=1, replica_groups=mesh['y'=4,'xh'=2,'xl'=2,'z'=8,'c'=2] {'xl','z'}, dimensions={0} | all-to-all | bytes 262144 | tf_op jit(solution)/shard_map/cond/branch_1_fun/all_to_all | solution.py:31
  146.7 0.7 collective-permute-start.10
  147.3 15.7 %conditional.20 = (bf16[64,1920]{1,0:T(8,128)(2,1)S(1)}) conditional(s32[]{:T(128)} %bitcast.18, () %tuple.134, (bf16[32,128]{1,0:T(8,128)(2,1)S(1)}, f32[2048]{0:T(1024)S(1)}, bf16[2048,896]{1,0:T(8,128)(2,1)}, bf16[2048,896]{1,0:T(8,128)(2,1)}, pred[1,128]{1,0:T(4,128)(4,1)S(1)}, /*index=5*/pred[1,128]{1,0:T(4,128)(4,1)S(1)}) %tuple.135), branch_computations={%region_22.23_spmd, %region_23.25_spmd} | conditional | flops 20605648896 | bytes 73106792 | solution.py:168
  147.4 12.5 %all_to_all.56.blocks = bf16[16,32,128]{2,1,0:T(8,128)(2,1)S(1)} all-to-all(bf16[16,32,128]{2,1,0:T(8,128)(2,1)S(1)} %repeat.8), channel_id=1, replica_groups=mesh['y'=4,'xh'=2,'xl'=2,'z'=8,'c'=2] {'xl','z'}, dimensions={0} | all-to-all | bytes 262144 | tf_op jit(solution)/shard_map/cond/branch_1_fun/all_to_all | solution.py:31
  160.0 1.3 collective-permute-done.4
  161.6 0.7 convolution_convert_fusion.7
  162.3 0.7 convolution_convert_fusion.6
  163.1 0.9 collective-permute-start.11
  164.0 11.6 %conditional.21 = (bf16[8,896]{1,0:T(8,128)(2,1)S(1)}) conditional(s32[]{:T(128)} %bitcast.18, () %tuple.138, bf16[64,1920]{1,0:T(8,128)(2,1)S(1)} %get-tuple-element.330), branch_computations={%region_25.26_spmd, %region_26.28_spmd} | conditional | flops 287776 | bytes 870536 | solution.py:168
  164.0 11.3 %all_to_all.57 = bf16[8,8,1920]{2,1,0:T(8,128)(2,1)S(1)} all-to-all(bf16[8,8,1920]{2,1,0:T(8,128)(2,1)S(1)} %bitcast.56), channel_id=1, replica_groups=mesh['y'=4,'xh'=2,'xl'=2,'z'=8,'c'=2] {'y','xh'}, dimensions={0} | all-to-all | bytes 491520 | tf_op jit(solution)/shard_map/cond/branch_1_fun/all_to_all | solution.py:31
  175.7 3.4 %collective-permute-start.12 = (bf16[8,2048]{1,0:T(8,128)(2,1)S(1)}, bf16[8,2048]{1,0:T(8,128)(2,1)S(1)}, u32[]{:S(2)}, u32[]{:S(2)}) collective-permute-start(bf16[8,2048]{1,0:T(8,128)(2,1)S(1)} %broadcast_select_fusion.6), channel_id=1, source_target_pairs={{0,8},{2,10},{4,12},{6,14},{8,0},{10,2},{12,4},{14,6},{1,9},{3,11}... | collective-permute-start | bytes 98312 | tf_op jit(solution)/shard_map/ppermute | solution.py:27
  179.3 13.3 %conditional.22 = (bf16[32,2048]{1,0:T(8,128)(2,1)S(1)}) conditional(s32[]{:T(128)} %bitcast.18, () %tuple.141, (bf16[8,896]{1,0:T(8,128)(2,1)S(1)}, bf16[896,2048]{1,0:T(8,128)(2,1)}, s32[1,2048]{1,0:T(1,128)S(1)}, s32[]{:T(128)}, bf16[32,128]{1,0:T(8,128)(2,1)S(1)}) %tuple.142), branch_computations={%region_28.29_spmd, %region_29.30_spmd} | conditional | flops 20368082944 | bytes 54464592 | solution.py:168
  179.4 10.9 %all_to_all.58 = bf16[8,8,896]{2,1,0:T(8,128)(2,1)S(1)} all-to-all(bf16[8,8,896]{2,1,0:T(8,128)(2,1)S(1)} %repeat.9), channel_id=1, replica_groups=mesh['y'=4,'xh'=2,'xl'=2,'z'=8,'c'=2] {'y','xh'}, dimensions={0} | all-to-all | bytes 229376 | tf_op jit(solution)/shard_map/cond/branch_1_fun/all_to_all | solution.py:31
  190.3 0.8 convolution_convert_fusion.8
  191.3 1.3 collective-permute-done.5
  192.7 0.7 add_convert_fusion.9
  193.4 13.8 %conditional.23 = (bf16[2,2048]{1,0:T(2,128)(2,1)S(1)}) conditional(s32[]{:T(128)} %bitcast.18, () %tuple.109, bf16[32,2048]{1,0:T(8,128)(2,1)S(1)} %get-tuple-element.332), branch_computations={%region_30.31_spmd, %region_31.33_spmd} | conditional | flops 61440 | bytes 663562 | solution.py:168
  193.5 13.6 %all_to_all.59 = bf16[16,2,2048]{2,1,0:T(2,128)(2,1)S(1)} all-to-all(bf16[16,2,2048]{2,1,0:T(2,128)(2,1)S(1)} %reshape.168), channel_id=1, replica_groups=mesh['y'=4,'xh'=2,'xl'=2,'z'=8,'c'=2] {'xl','z'}, dimensions={0} | all-to-all | bytes 262144 | tf_op jit(solution)/shard_map/cond/branch_1_fun/all_to_all | solution.py:31
  207.3 0.6 copy-done.12
  (124 shorter events, 7.1 us)
Async XLA Ops:
  30.8 0.7 copy-start.13
  30.8 2.8 %copy-start = (bf16[2048,896]{1,0:T(8,128)(2,1)S(1)}, bf16[2048,896]{1,0:T(8,128)(2,1)}, u32[]{:S(2)}) copy-start(bf16[2048,896]{1,0:T(8,128)(2,1)} %get-tuple-element.132) | copy-start | bytes 11010052 | tf_op jit(solution)/shard_map/cond
  30.8 2.2 %collective-permute-start = (bf16[160,2048]{1,0:T(8,128)(2,1)S(1)}, bf16[160,2048]{1,0:T(8,128)(2,1)S(1)}, u32[]{:S(2)}, u32[]{:S(2)}) collective-permute-start(bf16[160,2048]{1,0:T(8,128)(2,1)S(1)} %stack.1), channel_id=1, source_target_pairs={{0,1},{1,0},{2,3},{3,2},{4,5},{5,4},{6,7},{7,6},{8,9},{9,8},{10,11... | collective-permute-start | bytes 1966088 | tf_op jit(solution)/shard_map/cond/branch_1_fun/ppermute | solution.py:27
  31.5 3.6 %copy-start.9 = (f32[2048]{0:T(1024)}, f32[2048]{0:T(1024)S(1)}, u32[]{:S(2)}) copy-start(f32[2048]{0:T(1024)S(1)} %convert_multiply_fusion.2) | copy-start | bytes 24580 | tf_op jit(solution)/shard_map/cond
  33.6 2.0 copy-start.3
  37.2 0.7 copy-start.10
  53.5 16.0 %collective-permute-start.6 = (bf16[128,1920]{1,0:T(8,128)(2,1)S(1)}, bf16[128,1920]{1,0:T(8,128)(2,1)S(1)}, u32[]{:S(2)}, u32[]{:S(2)}) collective-permute-start(bf16[128,1920]{1,0:T(8,128)(2,1)S(1)} %get-tuple-element.216), channel_id=1, source_target_pairs={{0,64},{64,0},{128,192},{192,128},{1,65},{65,1},{129,193},{193,129... | collective-permute-start | bytes 1474568 | tf_op jit(solution)/shard_map/ppermute | solution.py:27
  53.9 13.4 %copy-start.6 = (bf16[896,2048]{1,0:T(8,128)(2,1)S(1)}, bf16[896,2048]{1,0:T(8,128)(2,1)}, u32[]{:S(2)}) copy-start(bf16[896,2048]{1,0:T(8,128)(2,1)} %get-tuple-element.135) | copy-start | bytes 11010052 | tf_op jit(solution)/shard_map/cond
  68.0 1.4 collective-permute-start.1
  69.6 13.4 %collective-permute-start.7 = (bf16[64,1920]{1,0:T(8,128)(2,1)S(1)}, bf16[64,1920]{1,0:T(8,128)(2,1)S(1)}, u32[]{:S(2)}, u32[]{:S(2)}) collective-permute-start(bf16[64,1920]{1,0:T(8,128)(2,1)S(1)} %broadcast_select_fusion.2), channel_id=1, source_target_pairs={{0,32},{32,0},{1,33},{33,1},{2,34},{34,2},{3,35},{35,3},{4,36},{36... | collective-permute-start | bytes 737288 | tf_op jit(solution)/shard_map/ppermute | solution.py:27
  83.2 16.5 %collective-permute-start.8 = (bf16[32,1920]{1,0:T(8,128)(2,1)S(1)}, bf16[32,1920]{1,0:T(8,128)(2,1)S(1)}, u32[]{:S(2)}, u32[]{:S(2)}) collective-permute-start(bf16[32,1920]{1,0:T(8,128)(2,1)S(1)} %broadcast_select_fusion.4), channel_id=1, source_target_pairs={{0,128},{64,192},{128,0},{192,64},{1,129},{65,193},{129,1},{193,65... | collective-permute-start | bytes 368648 | tf_op jit(solution)/shard_map/ppermute | solution.py:27
  84.7 13.5 %copy-start.1 = (bf16[2048,896]{1,0:T(8,128)(2,1)S(1)}, bf16[2048,896]{1,0:T(8,128)(2,1)}, u32[]{:S(2)}) copy-start(bf16[2048,896]{1,0:T(8,128)(2,1)} %get-tuple-element.140) | copy-start | bytes 11010052 | tf_op jit(solution)/shard_map/cond
  84.7 14.2 %copy-start.4 = (bf16[2048,896]{1,0:T(8,128)(2,1)S(1)}, bf16[2048,896]{1,0:T(8,128)(2,1)}, u32[]{:S(2)}) copy-start(bf16[2048,896]{1,0:T(8,128)(2,1)} %get-tuple-element.141) | copy-start | bytes 11010052 | tf_op jit(solution)/shard_map/cond
  96.5 1.4 collective-permute-start.2
  114.1 14.7 %copy-start.7 = (bf16[896,2048]{1,0:T(8,128)(2,1)S(1)}, bf16[896,2048]{1,0:T(8,128)(2,1)}, u32[]{:S(2)}) copy-start(bf16[896,2048]{1,0:T(8,128)(2,1)} %get-tuple-element.146) | copy-start | bytes 11010052 | tf_op jit(solution)/shard_map/cond
  130.4 2.2 %collective-permute-start.3 = (bf16[160,2048]{1,0:T(8,128)(2,1)S(1)}, bf16[160,2048]{1,0:T(8,128)(2,1)S(1)}, u32[]{:S(2)}, u32[]{:S(2)}) collective-permute-start(bf16[160,2048]{1,0:T(8,128)(2,1)S(1)} %slice.198), channel_id=1, source_target_pairs={{0,1},{1,0},{2,3},{3,2},{4,5},{5,4},{6,7},{7,6},{8,9},{9,8},{10,11... | collective-permute-start | bytes 1966088 | tf_op jit(solution)/shard_map/cond/branch_1_fun/ppermute | solution.py:27
  133.1 13.4 %collective-permute-start.9 = (bf16[64,2048]{1,0:T(8,128)(2,1)S(1)}, bf16[64,2048]{1,0:T(8,128)(2,1)S(1)}, u32[]{:S(2)}, u32[]{:S(2)}) collective-permute-start(bf16[64,2048]{1,0:T(8,128)(2,1)S(1)} %broadcast_select_fusion.1), channel_id=1, source_target_pairs={{0,16},{16,0},{1,17},{17,1},{2,18},{18,2},{3,19},{19,3},{4,20},{20... | collective-permute-start | bytes 786440 | tf_op jit(solution)/shard_map/ppermute | solution.py:27
  146.7 16.4 %collective-permute-start.10 = (bf16[32,2048]{1,0:T(8,128)(2,1)S(1)}, bf16[32,2048]{1,0:T(8,128)(2,1)S(1)}, u32[]{:S(2)}, u32[]{:S(2)}) collective-permute-start(bf16[32,2048]{1,0:T(8,128)(2,1)S(1)} %broadcast_select_fusion.3), channel_id=1, source_target_pairs={{0,2},{2,0},{4,6},{6,4},{8,10},{10,8},{12,14},{14,12},{1,3},{3,1},... | collective-permute-start | bytes 393224 | tf_op jit(solution)/shard_map/ppermute | solution.py:27
  147.3 31.8 %copy-start.14 = (s32[2]{0:T(128)S(1)}, s32[2]{0:T(128)}, u32[]{:S(2)}) copy-start(s32[2]{0:T(128)} %param.33) | copy-start | bytes 28
  147.3 14.3 %copy-start.2 = (bf16[2048,896]{1,0:T(8,128)(2,1)S(1)}, bf16[2048,896]{1,0:T(8,128)(2,1)}, u32[]{:S(2)}) copy-start(bf16[2048,896]{1,0:T(8,128)(2,1)} %get-tuple-element.151) | copy-start | bytes 11010052 | tf_op jit(solution)/shard_map/cond
  147.4 14.9 %copy-start.5 = (bf16[2048,896]{1,0:T(8,128)(2,1)S(1)}, bf16[2048,896]{1,0:T(8,128)(2,1)}, u32[]{:S(2)}) copy-start(bf16[2048,896]{1,0:T(8,128)(2,1)} %get-tuple-element.152) | copy-start | bytes 11010052 | tf_op jit(solution)/shard_map/cond
  159.9 1.4 collective-permute-start.4
  163.1 12.6 %collective-permute-start.11 = (bf16[16,2048]{1,0:T(8,128)(2,1)S(1)}, bf16[16,2048]{1,0:T(8,128)(2,1)S(1)}, u32[]{:S(2)}, u32[]{:S(2)}) collective-permute-start(bf16[16,2048]{1,0:T(8,128)(2,1)S(1)} %broadcast_select_fusion.5), channel_id=1, source_target_pairs={{0,4},{2,6},{4,0},{6,2},{8,12},{10,14},{12,8},{14,10},{1,5},{3,7},... | collective-permute-start | bytes 196616 | tf_op jit(solution)/shard_map/ppermute | solution.py:27
  175.7 16.9 %collective-permute-start.12 = (bf16[8,2048]{1,0:T(8,128)(2,1)S(1)}, bf16[8,2048]{1,0:T(8,128)(2,1)S(1)}, u32[]{:S(2)}, u32[]{:S(2)}) collective-permute-start(bf16[8,2048]{1,0:T(8,128)(2,1)S(1)} %broadcast_select_fusion.6), channel_id=1, source_target_pairs={{0,8},{2,10},{4,12},{6,14},{8,0},{10,2},{12,4},{14,6},{1,9},{3,11}... | collective-permute-start | bytes 98312 | tf_op jit(solution)/shard_map/ppermute | solution.py:27
  179.3 13.4 %copy-start.11 = (bf16[8,2048]{1,0:T(8,128)(2,1)S(1)}, bf16[8,2048]{1,0:T(8,128)(2,1)}, u32[]{:S(2)}) copy-start(bf16[8,2048]{1,0:T(8,128)(2,1)} %param.32) | copy-start | bytes 98308
  179.4 11.0 %copy-start.8 = (bf16[896,2048]{1,0:T(8,128)(2,1)S(1)}, bf16[896,2048]{1,0:T(8,128)(2,1)}, u32[]{:S(2)}) copy-start(bf16[896,2048]{1,0:T(8,128)(2,1)} %get-tuple-element.156) | copy-start | bytes 11010052 | tf_op jit(solution)/shard_map/cond
  191.1 1.4 collective-permute-start.5
  207.2 0.6 copy-start.12

commit v3 on v2

--- a/solution.py
+++ b/solution.py
@@ -124,7 +124,7 @@
     high = narrow(squares)
     rest = squares - wide(high)
     low = narrow(jnp.where(jnp.isfinite(rest), rest, 0.0))
-    scaled = narrow(values * gain)
+    scaled = narrow(values * SHRINK * wide(gain))
     gate = narrow(jnp.dot(scaled, gate_weight, preferred_element_type=jnp.float32))
     up = narrow(jnp.dot(scaled, up_weight, preferred_element_type=jnp.float32))
     first, second = marks
@@ -183,7 +183,6 @@
         verify = packet[:, :, :width].reshape(all_verify, width)
         shape = (all_draft + all_verify, width)
         rows = pair(rearrange(stack_kernel, (draft, verify), shape, "stack", LOAD), "c", 1)
-        gain = wide(gain) * SHRINK
         lane = lax.broadcasted_iota(jnp.int32, (1, LANES), 1)
         marks = lane == 0, lane == 1
         low, high = halves(up_product(rows, gain, marks, weights))
@@ -193,7 +192,7 @@
             draft, (0, column), (all_draft, LANES), allow_negative_indices=False
         )
         packet = jnp.concatenate([low[:all_draft], high[:all_draft]], axis=0)
-        return packet, state, keep, send, gain, marks
+        return packet, state, keep, send, marks
 
     def rows_in(state, gain, marks):
         own = columns(spread(state, CHIPS, N_CHIPS))
@@ -233,20 +232,20 @@
     def last_sum(partial):
         return narrow(summed(exchange(partial.reshape(N_CHIPS, n_draft, width), CHIPS)))
 
-    packet, state, keep, send, gain, marks = part(first_rows, draft_in, verify_in, norm_gain)
+    packet, state, keep, send, marks = part(first_rows, draft_in, verify_in, norm_gain)
     hidden = part(sum_width, packet)
-    arrived, partial = beside(send, "y", 1, share_hidden, hidden)
+    partial = part(share_hidden, hidden)
+    arrived, state = beside(send, "y", 1, sum_units, partial, state)
     keep, send = halves(narrow(add(keep, arrived)), across)
-    arrived, state = beside(send, "xh", 1, sum_units, partial, state)
+    arrived, packet = beside(send, "xh", 1, rows_in, state, norm_gain, marks)
     keep, send = halves(narrow(add(keep, arrived)), far)
-    arrived, packet = beside(send, "y", 2, rows_in, state, gain, marks)
+    arrived, hidden = beside(send, "y", 2, sum_width, packet)
     verify = activate(add(keep, arrived))
-    hidden = part(sum_width, packet)
     partial, verify = part(share_both, hidden, verify)
     keep, send = halves(verify, x_low == 1)
     arrived, state = beside(send, "xl", 1, sum_units, partial, state)
     keep, send = halves(narrow(add(keep, arrived)), z % 2 == 1)
-    arrived, packet = beside(send, "z", 1, rows_in, state, gain, marks)
+    arrived, packet = beside(send, "z", 1, rows_in, state, norm_gain, marks)
     keep, send = halves(narrow(add(keep, arrived)), z // 2 % 2 == 1)
     arrived, hidden = beside(send, "z", 2, sum_width, packet)
     keep, send = halves(narrow(add(keep, arrived)), z // 4 == 1)

time: 209 us -> 206 us (0.986)
    all_to_all x12, blocking collectives: 170 us -> 168 us  [exchange(): return lax.all_to_all(x, axes, 0, 0)]
  transfers between devices with their start and end apart: 13 -> 13, of which waited for: 6 -> 7; matrix products, arithmetic and copies ran while one was open for 3% -> 3% of each run, Pallas kernels for 0% -> 0%
where the time goes in v3:
time: 206 us; the launch traced here: 205 us
  blocking collectives  168 us (82%)
  waiting for transfers between devices  9.9 us (5%)
  matrix products  8.86 us (4%)
  starting transfers between devices  8.76 us (4%)
  other arithmetic  4.45 us (2%)
  local copies, waits for them, and re-layouts  2.48 us (1%)
    all_to_all x12, blocking collectives, exchange(): return lax.all_to_all(x, axes, 0, 0)  168 us
    ppermute x13, waiting for transfers between devices, swap(): lax.ppermute(x, axis, [(i, i ^ distance) for i in range(SIZES[axis])])  9.9 us
    ppermute x13, starting transfers between devices, swap(): lax.ppermute(x, axis, [(i, i ^ distance) for i in range(SIZES[axis])])  8.76 us
  transfers between devices with their start and end apart: 13, of which 7 were waited for; matrix products, arithmetic and copies ran while one was open for 3% of the time, Pallas kernels for 0%

profile of v3, /device:TPU:32, one launch (start us, length us, event | category | flops | bytes accessed | tf_op | source)
XLA Modules:
  0.0 205.4 jit_solution(14999688291995434957)
XLA Ops:
  1.3 36.1 %conditional.12 = (bf16[32,128]{1,0:T(8,128)(2,1)S(1)}, bf16[128,1920]{1,0:T(8,128)(2,1)S(1)}, pred[1,128]{1,0:T(4,128)(4,1)S(1)}, pred[1,128]{1,0:T(4,128)(4,1)...) conditional(s32[]{:T(128)} %bitcast.18, () %tuple.111, (bf16[8,2048]{1,0:T(8,128)(2,1)}, ...), branch_computations={%region_0.1_spmd, %region_1.3_spmd} | conditional | flops 22500808704 | bytes 89999280 | solution.py:168
  1.3 0.8 packet.1
  2.1 28.5 %all_to_all.48 = bf16[16,8,2560]{2,1,0:T(8,128)(2,1)S(1)} all-to-all(bf16[16,8,2560]{2,1,0:T(8,128)(2,1)S(1)} %packet.1), channel_id=1, replica_groups=mesh['y'=4,'xh'=2,'xl'=2,'z'=8,'c'=2] {'xl','z'}, dimensions={0} | all-to-all | bytes 1310720 | tf_op jit(solution)/shard_map/cond/branch_1_fun/all_to_all | solution.py:31
  31.5 1.5 collective-permute-done
  33.6 1.5 convolution_convert_fusion.1
  35.6 1.5 convolution_convert_fusion
  37.4 15.7 %conditional.13 = (bf16[8,896]{1,0:T(8,128)(2,1)S(1)}) conditional(s32[]{:T(128)} %bitcast.18, () %tuple.115, bf16[64,1920]{1,0:T(8,128)(2,1)S(1)} %get-tuple-element.214), branch_computations={%region_3.4_spmd, %region_4.6_spmd} | conditional | flops 287776 | bytes 870536 | solution.py:168
  37.4 15.3 %all_to_all.49 = bf16[8,8,1920]{2,1,0:T(8,128)(2,1)S(1)} all-to-all(bf16[8,8,1920]{2,1,0:T(8,128)(2,1)S(1)} %bitcast.54), channel_id=1, replica_groups=mesh['y'=4,'xh'=2,'xl'=2,'z'=8,'c'=2] {'y','xh'}, dimensions={0} | all-to-all | bytes 491520 | tf_op jit(solution)/shard_map/cond/branch_1_fun/all_to_all | solution.py:31
  53.1 13.2 %conditional.14 = (bf16[32,2048]{1,0:T(8,128)(2,1)S(1)}) conditional(s32[]{:T(128)} %bitcast.18, () %tuple.114, (bf16[8,896]{1,0:T(8,128)(2,1)S(1)}, bf16[896,2048]{1,0:T(8,128)(2,1)}) %tuple.116), branch_computations={%region_6.7_spmd, %region_7.8_spmd} | conditional | flops 20367933440 | bytes 53919820 | solution.py:168
  53.1 10.9 %all_to_all.50 = bf16[8,8,896]{2,1,0:T(8,128)(2,1)S(1)} all-to-all(bf16[8,8,896]{2,1,0:T(8,128)(2,1)S(1)} %repeat.5), channel_id=1, replica_groups=mesh['y'=4,'xh'=2,'xl'=2,'z'=8,'c'=2] {'y','xh'}, dimensions={0} | all-to-all | bytes 229376 | tf_op jit(solution)/shard_map/cond/branch_1_fun/all_to_all | solution.py:31
  64.0 0.8 convolution_convert_fusion.2
  64.9 1.3 collective-permute-done.1
  66.8 11.8 %conditional.15 = (bf16[32,128]{1,0:T(8,128)(2,1)S(1)}) conditional(s32[]{:T(128)} %bitcast.18, () %tuple.118, (bf16[32,128]{1,0:T(8,128)(2,1)S(1)}, bf16[32,2048]{1,0:T(8,128)(2,1)S(1)}) %tuple.119), branch_computations={%region_8.9_spmd, %region_9.11_spmd} | conditional | flops 139264 | bytes 966664 | solution.py:168
  66.9 11.7 %all_to_all.51 = bf16[16,32,128]{2,1,0:T(8,128)(2,1)S(1)} all-to-all(bf16[16,32,128]{2,1,0:T(8,128)(2,1)S(1)} %copy.18), channel_id=1, replica_groups=mesh['y'=4,'xh'=2,'xl'=2,'z'=8,'c'=2] {'xl','z'}, dimensions={0} | all-to-all | bytes 262144 | tf_op jit(solution)/shard_map/cond/branch_1_fun/all_to_all | solution.py:31
  78.6 1.1 collective-permute-done.6
  79.8 0.8 collective-permute-start.7
  80.6 15.0 %conditional.16 = (bf16[64,1920]{1,0:T(8,128)(2,1)S(1)}) conditional(s32[]{:T(128)} %bitcast.18, () %tuple.122, (bf16[32,128]{1,0:T(8,128)(2,1)S(1)}, bf16[2048]{0:T(1024)(128)(2,1)S(1)}, bf16[2048,896]{1,0:T(8,128)(2,1)}, bf16[2048,896]{1,0:T(8,128)(2,1)}, pred[1,128]{1,0:T(4,128)(4,1)S(1)}, /*index=5*/pred[1,128]{1,0:T(4,128)(4,1)S(1)}) %tuple.184), branch_computations={%region_11.12_spmd, %region_12.14_spmd} | conditional | flops 20605652992 | bytes 73119080 | solution.py:168
  80.7 11.8 %all_to_all.52.blocks = bf16[16,32,128]{2,1,0:T(8,128)(2,1)S(1)} all-to-all(bf16[16,32,128]{2,1,0:T(8,128)(2,1)S(1)} %repeat.6), channel_id=1, replica_groups=mesh['y'=4,'xh'=2,'xl'=2,'z'=8,'c'=2] {'xl','z'}, dimensions={0} | all-to-all | bytes 262144 | tf_op jit(solution)/shard_map/cond/branch_1_fun/all_to_all | solution.py:31
  92.6 1.3 collective-permute-done.2
  94.2 0.7 convolution_convert_fusion.4
  94.9 0.7 convolution_convert_fusion.3
  95.7 1.3 collective-permute-start.8
  97.0 14.9 %conditional.17 = (bf16[8,896]{1,0:T(8,128)(2,1)S(1)}) conditional(s32[]{:T(128)} %bitcast.18, () %tuple.126, bf16[64,1920]{1,0:T(8,128)(2,1)S(1)} %get-tuple-element.321), branch_computations={%region_14.15_spmd, %region_15.17_spmd} | conditional | flops 287776 | bytes 870536 | solution.py:168
  97.0 14.6 %all_to_all.53 = bf16[8,8,1920]{2,1,0:T(8,128)(2,1)S(1)} all-to-all(bf16[8,8,1920]{2,1,0:T(8,128)(2,1)S(1)} %bitcast.55), channel_id=1, replica_groups=mesh['y'=4,'xh'=2,'xl'=2,'z'=8,'c'=2] {'y','xh'}, dimensions={0} | all-to-all | bytes 491520 | tf_op jit(solution)/shard_map/cond/branch_1_fun/all_to_all | solution.py:31
  112.3 18.3 %conditional.18 = (bf16[32,2048]{1,0:T(8,128)(2,1)S(1)}, bf16[128,2048]{1,0:T(8,128)(2,1)S(1)}, bf16[64,2048]{1,0:T(8,128)(2,1)S(1)}, bf16[64,2048]{1,0:T(8,128)(2,1)S(1)}) conditional(s32[]{:T(128)} %bitcast.18, () %tuple.110, (bf16[8,896]{1,0:T(8,128)(2,1)S(1)}, bf16[32,896]{1,0:T(8,128)(2,1)S(1)}, bf16[896,2048]{1,0:T(8,128)(2,1)}) %tuple.128), branch_computations={%region_17.18_spmd, %region_18.19_spmd} | conditional | flops 21311467520 | bytes 67465312 | solution.py:168
  112.4 13.8 %all_to_all.54 = bf16[8,40,896]{2,1,0:T(8,128)(2,1)S(1)} all-to-all(bf16[8,40,896]{2,1,0:T(8,128)(2,1)S(1)} %repeat.7), channel_id=1, replica_groups=mesh['y'=4,'xh'=2,'xl'=2,'z'=8,'c'=2] {'y','xh'}, dimensions={0} | all-to-all | bytes 1146880 | tf_op jit(solution)/shard_map/cond/branch_1_fun/all_to_all | solution.py:31
  126.4 1.5 convolution_convert_fusion.5
  128.1 2.1 %collective-permute-done.3 = bf16[160,2048]{1,0:T(8,128)(2,1)S(1)} collective-permute-done((bf16[160,2048]{1,0:T(8,128)(2,1)S(1)}, bf16[160,2048]{1,0:T(8,128)(2,1)S(1)}, u32[]{:S(2)}, u32[]{:S(2)}) %collective-permute-start.3) | collective-permute-done | bytes 655392 | tf_op jit(solution)/shard_map/cond/branch_1_fun/ppermute | solution.py:27
  131.3 12.8 %conditional.19 = (bf16[32,128]{1,0:T(8,128)(2,1)S(1)}) conditional(s32[]{:T(128)} %bitcast.18, () %tuple.130, (bf16[32,128]{1,0:T(8,128)(2,1)S(1)}, bf16[32,2048]{1,0:T(8,128)(2,1)S(1)}) %tuple.131), branch_computations={%region_19.20_spmd, %region_20.22_spmd} | conditional | flops 139264 | bytes 966664 | solution.py:168
  131.4 12.7 %all_to_all.55 = bf16[16,32,128]{2,1,0:T(8,128)(2,1)S(1)} all-to-all(bf16[16,32,128]{2,1,0:T(8,128)(2,1)S(1)} %copy.20), channel_id=1, replica_groups=mesh['y'=4,'xh'=2,'xl'=2,'z'=8,'c'=2] {'xl','z'}, dimensions={0} | all-to-all | bytes 262144 | tf_op jit(solution)/shard_map/cond/branch_1_fun/all_to_all | solution.py:31
  144.3 0.7 collective-permute-start.10
  144.9 15.7 %conditional.20 = (bf16[64,1920]{1,0:T(8,128)(2,1)S(1)}) conditional(s32[]{:T(128)} %bitcast.18, () %tuple.134, (bf16[32,128]{1,0:T(8,128)(2,1)S(1)}, bf16[2048]{0:T(1024)(128)(2,1)S(1)}, bf16[2048,896]{1,0:T(8,128)(2,1)}, bf16[2048,896]{1,0:T(8,128)(2,1)}, pred[1,128]{1,0:T(4,128)(4,1)S(1)}, /*index=5*/pred[1,128]{1,0:T(4,128)(4,1)S(1)}) %tuple.185), branch_computations={%region_22.23_spmd, %region_23.25_spmd} | conditional | flops 20605652992 | bytes 73119080 | solution.py:168
  145.0 12.5 %all_to_all.56.blocks = bf16[16,32,128]{2,1,0:T(8,128)(2,1)S(1)} all-to-all(bf16[16,32,128]{2,1,0:T(8,128)(2,1)S(1)} %repeat.8), channel_id=1, replica_groups=mesh['y'=4,'xh'=2,'xl'=2,'z'=8,'c'=2] {'xl','z'}, dimensions={0} | all-to-all | bytes 262144 | tf_op jit(solution)/shard_map/cond/branch_1_fun/all_to_all | solution.py:31
  157.6 1.3 collective-permute-done.4
  159.2 0.7 convolution_convert_fusion.7
  159.9 0.7 convolution_convert_fusion.6
  160.7 0.9 collective-permute-start.11
  161.6 11.6 %conditional.21 = (bf16[8,896]{1,0:T(8,128)(2,1)S(1)}) conditional(s32[]{:T(128)} %bitcast.18, () %tuple.138, bf16[64,1920]{1,0:T(8,128)(2,1)S(1)} %get-tuple-element.324), branch_computations={%region_25.26_spmd, %region_26.28_spmd} | conditional | flops 287776 | bytes 870536 | solution.py:168
  161.6 11.3 %all_to_all.57 = bf16[8,8,1920]{2,1,0:T(8,128)(2,1)S(1)} all-to-all(bf16[8,8,1920]{2,1,0:T(8,128)(2,1)S(1)} %bitcast.56), channel_id=1, replica_groups=mesh['y'=4,'xh'=2,'xl'=2,'z'=8,'c'=2] {'y','xh'}, dimensions={0} | all-to-all | bytes 491520 | tf_op jit(solution)/shard_map/cond/branch_1_fun/all_to_all | solution.py:31
  173.3 3.4 %collective-permute-start.12 = (bf16[8,2048]{1,0:T(8,128)(2,1)S(1)}, bf16[8,2048]{1,0:T(8,128)(2,1)S(1)}, u32[]{:S(2)}, u32[]{:S(2)}) collective-permute-start(bf16[8,2048]{1,0:T(8,128)(2,1)S(1)} %broadcast_select_fusion.6), channel_id=1, source_target_pairs={{0,8},{2,10},{4,12},{6,14},{8,0},{10,2},{12,4},{14,6},{1,9},{3,11}... | collective-permute-start | bytes 98312 | tf_op jit(solution)/shard_map/ppermute | solution.py:27
  176.9 13.3 %conditional.22 = (bf16[32,2048]{1,0:T(8,128)(2,1)S(1)}) conditional(s32[]{:T(128)} %bitcast.18, () %tuple.141, (bf16[8,896]{1,0:T(8,128)(2,1)S(1)}, bf16[896,2048]{1,0:T(8,128)(2,1)}, s32[1,2048]{1,0:T(1,128)S(1)}, s32[]{:T(128)}, bf16[32,128]{1,0:T(8,128)(2,1)S(1)}) %tuple.142), branch_computations={%region_28.29_spmd, %region_29.30_spmd} | conditional | flops 20368082944 | bytes 54464592 | solution.py:168
  177.0 10.9 %all_to_all.58 = bf16[8,8,896]{2,1,0:T(8,128)(2,1)S(1)} all-to-all(bf16[8,8,896]{2,1,0:T(8,128)(2,1)S(1)} %repeat.9), channel_id=1, replica_groups=mesh['y'=4,'xh'=2,'xl'=2,'z'=8,'c'=2] {'y','xh'}, dimensions={0} | all-to-all | bytes 229376 | tf_op jit(solution)/shard_map/cond/branch_1_fun/all_to_all | solution.py:31
  187.9 0.8 convolution_convert_fusion.8
  188.9 1.3 collective-permute-done.5
  190.3 0.7 add_convert_fusion.9
  191.0 13.8 %conditional.23 = (bf16[2,2048]{1,0:T(2,128)(2,1)S(1)}) conditional(s32[]{:T(128)} %bitcast.18, () %tuple.109, bf16[32,2048]{1,0:T(8,128)(2,1)S(1)} %get-tuple-element.326), branch_computations={%region_30.31_spmd, %region_31.33_spmd} | conditional | flops 61440 | bytes 663562 | solution.py:168
  191.1 13.6 %all_to_all.59 = bf16[16,2,2048]{2,1,0:T(2,128)(2,1)S(1)} all-to-all(bf16[16,2,2048]{2,1,0:T(2,128)(2,1)S(1)} %reshape.168), channel_id=1, replica_groups=mesh['y'=4,'xh'=2,'xl'=2,'z'=8,'c'=2] {'xl','z'}, dimensions={0} | all-to-all | bytes 262144 | tf_op jit(solution)/shard_map/cond/branch_1_fun/all_to_all | solution.py:31
  204.9 0.6 copy-done.12
  (124 shorter events, 7.5 us)
Async XLA Ops:
  30.8 0.7 copy-start.11
  30.8 2.8 %copy-start = (bf16[2048,896]{1,0:T(8,128)(2,1)S(1)}, bf16[2048,896]{1,0:T(8,128)(2,1)}, u32[]{:S(2)}) copy-start(bf16[2048,896]{1,0:T(8,128)(2,1)} %get-tuple-element.132) | copy-start | bytes 11010052 | tf_op jit(solution)/shard_map/cond
  30.8 2.2 %collective-permute-start = (bf16[160,2048]{1,0:T(8,128)(2,1)S(1)}, bf16[160,2048]{1,0:T(8,128)(2,1)S(1)}, u32[]{:S(2)}, u32[]{:S(2)}) collective-permute-start(bf16[160,2048]{1,0:T(8,128)(2,1)S(1)} %stack.1), channel_id=1, source_target_pairs={{0,1},{1,0},{2,3},{3,2},{4,5},{5,4},{6,7},{7,6},{8,9},{9,8},{10,11... | collective-permute-start | bytes 1966088 | tf_op jit(solution)/shard_map/cond/branch_1_fun/ppermute | solution.py:27
  33.6 2.0 copy-start.3
  53.1 11.0 %copy-start.6 = (bf16[896,2048]{1,0:T(8,128)(2,1)S(1)}, bf16[896,2048]{1,0:T(8,128)(2,1)}, u32[]{:S(2)}) copy-start(bf16[896,2048]{1,0:T(8,128)(2,1)} %get-tuple-element.135) | copy-start | bytes 11010052 | tf_op jit(solution)/shard_map/cond
  64.8 1.4 collective-permute-start.1
  66.3 14.3 %copy-start.10 = (bf16[2048]{0:T(1024)(128)(2,1)S(1)}, bf16[2048]{0:T(1024)(128)(2,1)}, u32[]{:S(2)}) copy-start(bf16[2048]{0:T(1024)(128)(2,1)} %param.34) | copy-start | bytes 12292
  66.3 13.4 %collective-permute-start.6 = (bf16[128,1920]{1,0:T(8,128)(2,1)S(1)}, bf16[128,1920]{1,0:T(8,128)(2,1)S(1)}, u32[]{:S(2)}, u32[]{:S(2)}) collective-permute-start(bf16[128,1920]{1,0:T(8,128)(2,1)S(1)} %get-tuple-element.216), channel_id=1, source_target_pairs={{0,64},{64,0},{128,192},{192,128},{1,65},{65,1},{129,193},{193,129... | collective-permute-start | bytes 1474568 | tf_op jit(solution)/shard_map/ppermute | solution.py:27
  79.8 15.8 %collective-permute-start.7 = (bf16[64,1920]{1,0:T(8,128)(2,1)S(1)}, bf16[64,1920]{1,0:T(8,128)(2,1)S(1)}, u32[]{:S(2)}, u32[]{:S(2)}) collective-permute-start(bf16[64,1920]{1,0:T(8,128)(2,1)S(1)} %broadcast_select_fusion.2), channel_id=1, source_target_pairs={{0,32},{32,0},{1,33},{33,1},{2,34},{34,2},{3,35},{35,3},{4,36},{36... | collective-permute-start | bytes 737288 | tf_op jit(solution)/shard_map/ppermute | solution.py:27
  80.6 13.5 %copy-start.1 = (bf16[2048,896]{1,0:T(8,128)(2,1)S(1)}, bf16[2048,896]{1,0:T(8,128)(2,1)}, u32[]{:S(2)}) copy-start(bf16[2048,896]{1,0:T(8,128)(2,1)} %get-tuple-element.140) | copy-start | bytes 11010052 | tf_op jit(solution)/shard_map/cond
  80.6 14.2 %copy-start.4 = (bf16[2048,896]{1,0:T(8,128)(2,1)S(1)}, bf16[2048,896]{1,0:T(8,128)(2,1)}, u32[]{:S(2)}) copy-start(bf16[2048,896]{1,0:T(8,128)(2,1)} %get-tuple-element.141) | copy-start | bytes 11010052 | tf_op jit(solution)/shard_map/cond
  92.5 1.4 collective-permute-start.2
  95.7 16.2 %collective-permute-start.8 = (bf16[32,1920]{1,0:T(8,128)(2,1)S(1)}, bf16[32,1920]{1,0:T(8,128)(2,1)S(1)}, u32[]{:S(2)}, u32[]{:S(2)}) collective-permute-start(bf16[32,1920]{1,0:T(8,128)(2,1)S(1)} %broadcast_select_fusion.4), channel_id=1, source_target_pairs={{0,128},{64,192},{128,0},{192,64},{1,129},{65,193},{129,1},{193,65... | collective-permute-start | bytes 368648 | tf_op jit(solution)/shard_map/ppermute | solution.py:27
  112.4 14.0 %copy-start.7 = (bf16[896,2048]{1,0:T(8,128)(2,1)S(1)}, bf16[896,2048]{1,0:T(8,128)(2,1)}, u32[]{:S(2)}) copy-start(bf16[896,2048]{1,0:T(8,128)(2,1)} %get-tuple-element.146) | copy-start | bytes 11010052 | tf_op jit(solution)/shard_map/cond
  128.0 2.2 %collective-permute-start.3 = (bf16[160,2048]{1,0:T(8,128)(2,1)S(1)}, bf16[160,2048]{1,0:T(8,128)(2,1)S(1)}, u32[]{:S(2)}, u32[]{:S(2)}) collective-permute-start(bf16[160,2048]{1,0:T(8,128)(2,1)S(1)} %slice.198), channel_id=1, source_target_pairs={{0,1},{1,0},{2,3},{3,2},{4,5},{5,4},{6,7},{7,6},{8,9},{9,8},{10,11... | collective-permute-start | bytes 1966088 | tf_op jit(solution)/shard_map/cond/branch_1_fun/ppermute | solution.py:27
  130.7 13.4 %collective-permute-start.9 = (bf16[64,2048]{1,0:T(8,128)(2,1)S(1)}, bf16[64,2048]{1,0:T(8,128)(2,1)S(1)}, u32[]{:S(2)}, u32[]{:S(2)}) collective-permute-start(bf16[64,2048]{1,0:T(8,128)(2,1)S(1)} %broadcast_select_fusion.1), channel_id=1, source_target_pairs={{0,16},{16,0},{1,17},{17,1},{2,18},{18,2},{3,19},{19,3},{4,20},{20... | collective-permute-start | bytes 786440 | tf_op jit(solution)/shard_map/ppermute | solution.py:27
  144.3 16.4 %collective-permute-start.10 = (bf16[32,2048]{1,0:T(8,128)(2,1)S(1)}, bf16[32,2048]{1,0:T(8,128)(2,1)S(1)}, u32[]{:S(2)}, u32[]{:S(2)}) collective-permute-start(bf16[32,2048]{1,0:T(8,128)(2,1)S(1)} %broadcast_select_fusion.3), channel_id=1, source_target_pairs={{0,2},{2,0},{4,6},{6,4},{8,10},{10,8},{12,14},{14,12},{1,3},{3,1},... | collective-permute-start | bytes 393224 | tf_op jit(solution)/shard_map/ppermute | solution.py:27
  144.9 31.8 %copy-start.13 = (s32[2]{0:T(128)S(1)}, s32[2]{0:T(128)}, u32[]{:S(2)}) copy-start(s32[2]{0:T(128)} %param.33) | copy-start | bytes 28
  144.9 14.3 %copy-start.2 = (bf16[2048,896]{1,0:T(8,128)(2,1)S(1)}, bf16[2048,896]{1,0:T(8,128)(2,1)}, u32[]{:S(2)}) copy-start(bf16[2048,896]{1,0:T(8,128)(2,1)} %get-tuple-element.151) | copy-start | bytes 11010052 | tf_op jit(solution)/shard_map/cond
  145.0 14.9 %copy-start.5 = (bf16[2048,896]{1,0:T(8,128)(2,1)S(1)}, bf16[2048,896]{1,0:T(8,128)(2,1)}, u32[]{:S(2)}) copy-start(bf16[2048,896]{1,0:T(8,128)(2,1)} %get-tuple-element.152) | copy-start | bytes 11010052 | tf_op jit(solution)/shard_map/cond
  157.5 1.4 collective-permute-start.4
  160.7 12.6 %collective-permute-start.11 = (bf16[16,2048]{1,0:T(8,128)(2,1)S(1)}, bf16[16,2048]{1,0:T(8,128)(2,1)S(1)}, u32[]{:S(2)}, u32[]{:S(2)}) collective-permute-start(bf16[16,2048]{1,0:T(8,128)(2,1)S(1)} %broadcast_select_fusion.5), channel_id=1, source_target_pairs={{0,4},{2,6},{4,0},{6,2},{8,12},{10,14},{12,8},{14,10},{1,5},{3,7},... | collective-permute-start | bytes 196616 | tf_op jit(solution)/shard_map/ppermute | solution.py:27
  173.3 16.9 %collective-permute-start.12 = (bf16[8,2048]{1,0:T(8,128)(2,1)S(1)}, bf16[8,2048]{1,0:T(8,128)(2,1)S(1)}, u32[]{:S(2)}, u32[]{:S(2)}) collective-permute-start(bf16[8,2048]{1,0:T(8,128)(2,1)S(1)} %broadcast_select_fusion.6), channel_id=1, source_target_pairs={{0,8},{2,10},{4,12},{6,14},{8,0},{10,2},{12,4},{14,6},{1,9},{3,11}... | collective-permute-start | bytes 98312 | tf_op jit(solution)/shard_map/ppermute | solution.py:27
  176.9 13.4 %copy-start.9 = (bf16[8,2048]{1,0:T(8,128)(2,1)S(1)}, bf16[8,2048]{1,0:T(8,128)(2,1)}, u32[]{:S(2)}) copy-start(bf16[8,2048]{1,0:T(8,128)(2,1)} %param.32) | copy-start | bytes 98308
  177.0 11.0 %copy-start.8 = (bf16[896,2048]{1,0:T(8,128)(2,1)S(1)}, bf16[896,2048]{1,0:T(8,128)(2,1)}, u32[]{:S(2)}) copy-start(bf16[896,2048]{1,0:T(8,128)(2,1)} %get-tuple-element.156) | copy-start | bytes 11010052 | tf_op jit(solution)/shard_map/cond
  188.7 1.4 collective-permute-start.5
  204.8 0.6 copy-start.12

commit v4 on v3

v4 whole, which is shorter than its diff:
```python
import math

import jax
import jax.numpy as jnp
from jax import lax
from jax.experimental import pallas as pl
from jax.experimental.pallas import tpu as pltpu
from jax.sharding import Mesh
from jax.sharding import PartitionSpec as P

D = 16384
DRAFT_STEPS = 3
POS = 4
SIZES = {"y": 4, "xh": 2, "xl": 2, "z": 8, "c": 2}
NAMES = tuple(SIZES)
GX = ("y", "xh")
CHIPS = ("xl", "z")
N_GX = 8
N_CHIPS = 16
LANES = 128
LOAD = 32 << 20
epsilon = 1e-05
SHRINK = 2.0**-12


def swap(x, axes, distance):
    count = math.prod(SIZES[axis] for axis in ([axes] if isinstance(axes, str) else axes))
    return lax.ppermute(x, axes, [(i, i ^ distance) for i in range(count)])


def exchange(x, axes):
    return lax.all_to_all(x, axes, 0, 0)


def repeat_kernel(x, out):
    values = x[...]
    for i in range(out.shape[0]):
        out[i] = values


def stack_kernel(*refs):
    rows = [ref[...].astype(jnp.float32) for ref in refs[:-1]]
    refs[-1][...] = jnp.concatenate(rows, axis=0).astype(refs[-1].dtype)


def copy_kernel(x, out):
    out[...] = x[...]


def columns_kernel(blocks, out):
    size = blocks.shape[2]
    for k in range(blocks.shape[0]):
        out[:, k * size : (k + 1) * size] = blocks[k]


def rearrange(kernel, arrays, shape, name, load=0):
    vmem = pl.BlockSpec(memory_space=pltpu.VMEM)
    return pl.pallas_call(
        kernel,
        out_shape=jax.ShapeDtypeStruct(shape, jnp.bfloat16),
        in_specs=[vmem] * len(arrays),
        out_specs=vmem,
        compiler_params=pltpu.CompilerParams(vmem_limit_bytes=8 << 20),
        cost_estimate=pl.CostEstimate(
            flops=load * 600, bytes_accessed=4 * math.prod(shape) + load, transcendentals=0
        ),
        name=name,
    )(*arrays)


def stack(*arrays):
    count, width = arrays[0].shape
    return rearrange(stack_kernel, arrays, (len(arrays) * count, width), "stack")


def spread(x, axes, count):
    copies = rearrange(repeat_kernel, (x,), (count,) + x.shape, "repeat", LOAD)
    return exchange(copies, axes)


def wide(x):
    return x.astype(jnp.float32)


def narrow(x):
    return x.astype(jnp.bfloat16)


def pair(own, axis, distance):
    return jnp.concatenate([own, swap(own, axis, distance)], axis=0)


def halves(rows, upper=None):
    half = rows.shape[0] // 2
    low, high = rows[:half], rows[half:]
    if upper is None:
        return low, high
    return jnp.where(upper, high, low), jnp.where(upper, low, high)


def columns(blocks):
    count, rows, lanes = blocks.shape
    return rearrange(columns_kernel, (blocks,), (rows, count * lanes), "columns")


def blocks_of(x, count):
    return jnp.transpose(x.reshape(x.shape[0], count, -1), (1, 0, 2))


def summed(packet):
    return jnp.sum(wide(packet), axis=0)


def up_product(rows, gain, marks, weights):
    gate_weight, up_weight = weights[:2]
    values = wide(rows)
    squares = jnp.sum(values * values, axis=1, keepdims=True)
    high = narrow(squares)
    rest = squares - wide(high)
    low = narrow(jnp.where(jnp.isfinite(rest), rest, 0.0))
    scaled = narrow(values * SHRINK * wide(gain))
    gate = narrow(jnp.dot(scaled, gate_weight, preferred_element_type=jnp.float32))
    up = narrow(jnp.dot(scaled, up_weight, preferred_element_type=jnp.float32))
    first, second = marks
    extra = jnp.where(first, high, jnp.where(second, low, jnp.zeros_like(high)))
    return jnp.concatenate([gate, up, extra], axis=1)


def activate(total):
    units = (total.shape[1] - LANES) // 2
    sums = total[:, 2 * units : 2 * units + 1] + total[:, 2 * units + 1 : 2 * units + 2]
    scale = lax.rsqrt(sums / D + epsilon) * (1.0 / SHRINK)
    gate = total[:, :units] * scale
    up = total[:, units : 2 * units] * scale
    return narrow(jax.nn.silu(gate) * up)


def down_product(hidden, weights):
    return narrow(jnp.dot(hidden, weights[2], preferred_element_type=jnp.float32))


def shards(draft_in, verify_in, accept_len, norm_gain, gate_weight, up_weight, down_weight):
    weights = (gate_weight, up_weight, down_weight)
    n_draft, width = draft_in.shape
    n_verify = verify_in.shape[0]
    units = gate_weight.shape[1]
    all_draft = N_CHIPS * n_draft
    y = lax.axis_index("y")
    near, across, far = y % 2 == 1, lax.axis_index("xh") == 1, y // 2 == 1
    chip = lax.axis_index("xl") * SIZES["z"] + lax.axis_index("z")
    lane = lax.broadcasted_iota(jnp.int32, (1, LANES), 1)
    near, column, lane = lax.optimization_barrier((near, chip * LANES, lane))
    marks = lane == 0, lane == 1
    mine = (lax.broadcasted_iota(jnp.int32, (1, width), 1) // LANES) == chip
    always = accept_len[0] >= 0

    def part(body, *operands):
        def empty(*rest):
            return jax.tree.map(
                lambda a: jnp.zeros(a.shape, a.dtype), jax.eval_shape(body, *rest)
            )

        return lax.cond(always, body, empty, *operands)

    def beside(send, swaps, body, *operands):
        send, operands = lax.optimization_barrier((send, operands))
        arrived = [swap(send, axes, distance) for axes, distance in swaps]
        result = part(body, *operands)
        return lax.optimization_barrier((*arrived, result))

    def add(keep, arrived):
        return wide(keep) + wide(arrived)

    def first_rows(draft, gain, marks):
        draft = spread(draft, CHIPS, N_CHIPS)
        draft, gain = lax.optimization_barrier((draft, gain))
        draft = draft.reshape(all_draft, width)
        own = rearrange(copy_kernel, (draft,), draft.shape, "own", LOAD)
        start = (0, column)
        state = lax.dynamic_slice(
            draft, start, (all_draft, LANES), allow_negative_indices=False
        )
        return up_product(pair(own, "c", 1), gain, marks, weights), state

    def rows_in(state, gain, marks):
        own = columns(spread(state, CHIPS, N_CHIPS))
        return up_product(pair(own, "c", 1), gain, marks, weights)

    def sum_width(packet):
        packet = packet.reshape(N_GX, -1, packet.shape[1])
        return activate(summed(exchange(packet, GX)))

    def share_hidden(hidden):
        hidden = spread(hidden, GX, N_GX).reshape(-1, units)
        keep, send = halves(down_product(hidden, weights))
        return narrow(add(keep, swap(send, "c", 1)))

    def share_first(hidden, verify, gain, marks):
        hidden = spread(hidden, GX, N_GX).reshape(-1, units)
        hidden, verify, gain = lax.optimization_barrier((hidden, verify, gain))
        keep, send = halves(down_product(hidden, weights))
        partial = narrow(add(keep, swap(send, "c", 1)))
        own = up_product(verify, gain, marks, weights)
        other = up_product(swap(verify, "c", 1), gain, marks, weights)
        return partial, jnp.where(near, other, own), jnp.where(near, own, other)

    def share_both(hidden, verify):
        n_own = hidden.shape[0]
        both = spread(jnp.concatenate([hidden, verify], axis=0), GX, N_GX)
        hidden = both[:, :n_own].reshape(-1, units)
        keep, send = halves(down_product(hidden, weights))
        partial = narrow(add(keep, swap(send, "c", 1)))
        verify = both[:, n_own:].reshape(2, 2, 2, 2, 2, n_verify, units)
        verify = jnp.transpose(verify, (1, 2, 0, 4, 3, 5, 6)).reshape(-1, units)
        return partial, *halves(down_product(verify, weights))

    def share_last(hidden, state):
        hidden = spread(hidden, GX, N_GX).reshape(-1, units)
        keep, send = halves(down_product(hidden, weights))
        total = add(keep, swap(send, "c", 1))
        return narrow(total + jnp.where(mine, jnp.tile(wide(state), (1, N_CHIPS)), 0.0))

    def sum_units(partial, state):
        change = summed(exchange(blocks_of(partial, N_CHIPS), CHIPS))
        return narrow(wide(state) + change)

    def last_sum(partial):
        return narrow(summed(exchange(partial.reshape(N_CHIPS, n_draft, width), CHIPS)))

    swaps = [("z", 4), ("z", 2), ("z", 6)]
    far_z, near_z, both_z, (packet, state) = beside(
        verify_in, swaps, first_rows, draft_in, norm_gain, marks
    )
    verify = stack(verify_in, near_z, far_z, both_z)
    swaps = [(CHIPS, 1), (CHIPS, 8), (CHIPS, 9)]
    near_z, low_x, both, hidden = beside(verify, swaps, sum_width, packet)
    verify = stack(verify, near_z, low_x, both)
    partial, keep, send = part(share_first, hidden, verify, norm_gain, marks)
    arrived, state = beside(send, [("y", 1)], sum_units, partial, state)
    keep, send = halves(narrow(add(keep, arrived)), across)
    arrived, packet = beside(send, [("xh", 1)], rows_in, state, norm_gain, marks)
    keep, send = halves(narrow(add(keep, arrived)), far)
    arrived, hidden = beside(send, [("y", 2)], sum_width, packet)
    verify = activate(add(keep, arrived))
    partial, keep, send = part(share_both, hidden, verify)
    arrived, state = beside(send, [("c", 1)], sum_units, partial, state)
    keep, send = halves(narrow(add(keep, arrived)))
    arrived, packet = beside(send, [("xl", 1)], rows_in, state, norm_gain, marks)
    keep, send = halves(narrow(add(keep, arrived)))
    arrived, hidden = beside(send, [("z", 1)], sum_width, packet)
    keep, send = halves(narrow(add(keep, arrived)))
    arrived, partial = beside(send, [("z", 2)], share_last, hidden, state)
    keep, send = halves(narrow(add(keep, arrived)))
    arrived, draft_out = beside(send, [("z", 4)], last_sum, partial)
    live = (
        (jnp.arange(POS, dtype=jnp.int32)[None, :] <= accept_len[:, None])
        .reshape(-1, 1)
        .astype(jnp.float32)
    )
    verify_out = narrow(wide(verify_in) + live * add(keep, arrived))
    return draft_out, verify_out


def solution(mesh):
    split = Mesh(mesh.devices.reshape(tuple(SIZES.values())), NAMES)
    gy = ("xl", "z", "c")
    placed = (P(gy, GX), P(gy, GX), P(gy), P(GX), P(GX, gy), P(GX, gy), P(gy, GX))
    return jax.shard_map(
        shards,
        mesh=split,
        in_specs=placed,
        out_specs=(P(gy, GX), P(gy, GX)),
        check_vma=False,
    )
```

time: 206 us -> 203 us (0.985)
  blocking collectives: 168 us -> 154 us
  starting transfers between devices: 8.76 us -> 21.7 us
  waiting for transfers between devices: 9.9 us -> 5.69 us
    all_to_all x12, blocking collectives: 168 us -> 154 us  [exchange(): return lax.all_to_all(x, axes, 0, 0)]
    ppermute x13 -> x21, starting transfers between devices: 8.76 us -> 21.7 us  [swap(): return lax.ppermute(x, axes, [(i, i ^ distance) for i in range(count)])]
    ppermute x13 -> x21, waiting for transfers between devices: 9.9 us -> 5.69 us  [swap(): return lax.ppermute(x, axes, [(i, i ^ distance) for i in range(count)])]
  transfers between devices with their start and end apart: 13 -> 21, of which waited for: 7 -> 5; matrix products, arithmetic and copies ran while one was open for 3% -> 6% of each run, Pallas kernels for 0% -> 0%
where the time goes in v4:
time: 203 us; the launch traced here: 202 us
  blocking collectives  154 us (76%)
  starting transfers between devices  21.7 us (11%)
  matrix products  10.7 us (5%)
  waiting for transfers between devices  5.69 us (3%)
  other arithmetic  4.64 us (2%)
    all_to_all x12, blocking collectives, exchange(): return lax.all_to_all(x, axes, 0, 0)  154 us
    ppermute x21, starting transfers between devices, swap(): return lax.ppermute(x, axes, [(i, i ^ distance) for i in range(count)])  21.7 us
    ppermute x21, waiting for transfers between devices, swap(): return lax.ppermute(x, axes, [(i, i ^ distance) for i in range(count)])  5.69 us
  transfers between devices with their start and end apart: 21, of which 5 were waited for; matrix products, arithmetic and copies ran while one was open for 6% of the time, Pallas kernels for 0%

profile of v4, /device:TPU:32, one launch (start us, length us, event | category | flops | bytes accessed | tf_op | source)
XLA Modules:
  0.0 202.1 jit_solution(13397057873362265012)
XLA Ops:
  0.7 6.4 %collective-permute-start.7 = (bf16[8,2048]{1,0:T(8,128)(2,1)}, bf16[8,2048]{1,0:T(8,128)(2,1)S(1)}, u32[]{:S(2)}, u32[]{:S(2)}) collective-permute-start(bf16[8,2048]{1,0:T(8,128)(2,1)} %refs_0_.1), channel_id=1, source_target_pairs={{0,8},{2,10},{4,12},{6,14},{8,0},{10,2},{12,4},{14,6},{1,9},{3,11}... | collective-permute-start | bytes 98312 | tf_op jit(solution)/shard_map/ppermute | solution.py:28
  7.0 1.5 collective-permute-start.8
  9.2 20.7 %conditional.12 = (bf16[64,1920]{1,0:T(8,128)(2,1)S(1)}, bf16[32,128]{1,0:T(8,128)(2,1)S(1)}) conditional(s32[]{:T(128)} %bitcast.19, () %tuple.119, (bf16[2,2048]{1,0:T(2,128)(2,1)}, bf16[2048]{0:T(1024)(128)(2,1)}, bf16[2048,896]{1,0:T(8,128)(2,1)}, bf16[2048,896]{1,0:T(8,128)(2,1)}, pred[1,128]{1,0:T(4,128)(4,1)S(1)}, ...), branch_computations={%region_0.1_spmd, %region_1.3_spmd} | conditional | flops 40738312192 | bytes 106968480 | solution.py:163
  9.9 16.0 %all_to_all.48 = bf16[16,2,2048]{2,1,0:T(2,128)(2,1)S(1)} all-to-all(bf16[16,2,2048]{2,1,0:T(2,128)(2,1)S(1)} %repeat.6), channel_id=1, replica_groups=mesh['y'=4,'xh'=2,'xl'=2,'z'=8,'c'=2] {'xl','z'}, dimensions={0} | all-to-all | bytes 262144 | tf_op jit(solution)/shard_map/cond/branch_1_fun/all_to_all | solution.py:32
  26.8 0.7 collective-permute-done
  30.0 0.8 collective-permute-start.10
  30.7 1.0 collective-permute-start.11
  31.7 1.8 collective-permute-start.12
  33.6 15.4 %conditional.13 = (bf16[8,896]{1,0:T(8,128)(2,1)S(1)}) conditional(s32[]{:T(128)} %bitcast.19, () %tuple.123, bf16[64,1920]{1,0:T(8,128)(2,1)S(1)} %get-tuple-element.265), branch_computations={%region_3.4_spmd, %region_4.6_spmd} | conditional | flops 287776 | bytes 870536 | solution.py:163
  33.6 15.1 %all_to_all.49 = bf16[8,8,1920]{2,1,0:T(8,128)(2,1)S(1)} all-to-all(bf16[8,8,1920]{2,1,0:T(8,128)(2,1)S(1)} %bitcast.57), channel_id=1, replica_groups=mesh['y'=4,'xh'=2,'xl'=2,'z'=8,'c'=2] {'y','xh'}, dimensions={0} | all-to-all | bytes 491520 | tf_op jit(solution)/shard_map/cond/branch_1_fun/all_to_all | solution.py:32
  49.1 16.2 %conditional.14 = (bf16[32,2048]{1,0:T(8,128)(2,1)S(1)}, bf16[128,1920]{1,0:T(8,128)(2,1)S(1)}, f32[128,1920]{1,0:T(8,128)S(1)}) conditional(s32[]{:T(128)} %bitcast.19, () %tuple.116, (bf16[8,896]{1,0:T(8,128)(2,1)S(1)}, bf16[128,2048]{1,0:T(8,128)(2,1)S(1)}, bf16[2048]{0:T(1024)(128)(2,1)}, bf16[896,2048]{1,0:T(8,128)(2,1)}, pred[]{:T(512)}, ...), branch_computations={%region_6.7_spmd, %region_7.10_spmd} | conditional | flops 22255915008 | bytes 106709472 | solution.py:163
  49.2 10.9 %all_to_all.50 = bf16[8,8,896]{2,1,0:T(8,128)(2,1)S(1)} all-to-all(bf16[8,8,896]{2,1,0:T(8,128)(2,1)S(1)} %repeat.7), channel_id=1, replica_groups=mesh['y'=4,'xh'=2,'xl'=2,'z'=8,'c'=2] {'y','xh'}, dimensions={0} | all-to-all | bytes 229376 | tf_op jit(solution)/shard_map/cond/branch_1_fun/all_to_all | solution.py:32
  60.4 0.8 convolution_convert_fusion.2
  61.8 0.7 convolution_convert_fusion.5
  62.5 0.7 convolution_convert_fusion.6
  63.7 0.7 convolution_convert_fusion.3
  64.4 0.7 convolution_convert_fusion.4
  65.9 12.1 %conditional.15 = (bf16[32,128]{1,0:T(8,128)(2,1)S(1)}) conditional(s32[]{:T(128)} %bitcast.19, () %tuple.127, (bf16[32,128]{1,0:T(8,128)(2,1)S(1)}, bf16[32,2048]{1,0:T(8,128)(2,1)S(1)}) %tuple.128), branch_computations={%region_10.11_spmd, %region_11.13_spmd} | conditional | flops 139264 | bytes 966664 | solution.py:163
  65.9 11.8 %all_to_all.51 = bf16[16,32,128]{2,1,0:T(8,128)(2,1)S(1)} all-to-all(bf16[16,32,128]{2,1,0:T(8,128)(2,1)S(1)} %copy.17), channel_id=1, replica_groups=mesh['y'=4,'xh'=2,'xl'=2,'z'=8,'c'=2] {'xl','z'}, dimensions={0} | all-to-all | bytes 262144 | tf_op jit(solution)/shard_map/cond/branch_1_fun/all_to_all | solution.py:32
  77.9 1.0 collective-permute-done.13
  79.1 0.8 collective-permute-start.14
  79.9 14.9 %conditional.16 = (bf16[64,1920]{1,0:T(8,128)(2,1)S(1)}) conditional(s32[]{:T(128)} %bitcast.19, () %tuple.131, (bf16[32,128]{1,0:T(8,128)(2,1)S(1)}, bf16[2048]{0:T(1024)(128)(2,1)S(1)}, bf16[2048,896]{1,0:T(8,128)(2,1)}, bf16[2048,896]{1,0:T(8,128)(2,1)}, pred[1,128]{1,0:T(4,128)(4,1)S(1)}, /*index=5*/pred[1,128]{1,0:T(4,128)(4,1)S(1)}) %tuple.196), branch_computations={%region_13.14_spmd, %region_14.16_spmd} | conditional | flops 20605652992 | bytes 73119080 | solution.py:163
  79.9 11.7 %all_to_all.52.blocks = bf16[16,32,128]{2,1,0:T(8,128)(2,1)S(1)} all-to-all(bf16[16,32,128]{2,1,0:T(8,128)(2,1)S(1)} %repeat.8), channel_id=1, replica_groups=mesh['y'=4,'xh'=2,'xl'=2,'z'=8,'c'=2] {'xl','z'}, dimensions={0} | all-to-all | bytes 262144 | tf_op jit(solution)/shard_map/cond/branch_1_fun/all_to_all | solution.py:32
  91.8 1.3 collective-permute-done.3
  94.9 1.5 collective-permute-start.15
  96.4 14.9 %conditional.17 = (bf16[8,896]{1,0:T(8,128)(2,1)S(1)}) conditional(s32[]{:T(128)} %bitcast.19, () %tuple.135, bf16[64,1920]{1,0:T(8,128)(2,1)S(1)} %get-tuple-element.389), branch_computations={%region_16.17_spmd, %region_17.19_spmd} | conditional | flops 287776 | bytes 870536 | solution.py:163
  96.4 14.6 %all_to_all.53 = bf16[8,8,1920]{2,1,0:T(8,128)(2,1)S(1)} all-to-all(bf16[8,8,1920]{2,1,0:T(8,128)(2,1)S(1)} %bitcast.58), channel_id=1, replica_groups=mesh['y'=4,'xh'=2,'xl'=2,'z'=8,'c'=2] {'y','xh'}, dimensions={0} | all-to-all | bytes 491520 | tf_op jit(solution)/shard_map/cond/branch_1_fun/all_to_all | solution.py:32
  111.7 16.4 %conditional.18 = (bf16[32,2048]{1,0:T(8,128)(2,1)S(1)}, bf16[128,2048]{1,0:T(8,128)(2,1)S(1)}, f32[128,2048]{1,0:T(8,128)S(1)}) conditional(s32[]{:T(128)} %bitcast.19, () %tuple.115, (bf16[8,896]{1,0:T(8,128)(2,1)S(1)}, bf16[32,896]{1,0:T(8,128)(2,1)S(1)}, bf16[896,2048]{1,0:T(8,128)(2,1)}) %tuple.137), branch_computations={%region_19.20_spmd, %region_20.21_spmd} | conditional | flops 21308387328 | bytes 65531996 | solution.py:163
  111.8 13.8 %all_to_all.54 = bf16[8,40,896]{2,1,0:T(8,128)(2,1)S(1)} all-to-all(bf16[8,40,896]{2,1,0:T(8,128)(2,1)S(1)} %repeat.9), channel_id=1, replica_groups=mesh['y'=4,'xh'=2,'xl'=2,'z'=8,'c'=2] {'y','xh'}, dimensions={0} | all-to-all | bytes 1146880 | tf_op jit(solution)/shard_map/cond/branch_1_fun/all_to_all | solution.py:32
  125.6 0.8 convolution_convert_fusion.10
  126.6 1.3 convolution_convert_fusion.9
  128.7 11.9 %conditional.19 = (bf16[32,128]{1,0:T(8,128)(2,1)S(1)}) conditional(s32[]{:T(128)} %bitcast.19, () %tuple.139, (bf16[32,128]{1,0:T(8,128)(2,1)S(1)}, bf16[32,2048]{1,0:T(8,128)(2,1)S(1)}) %tuple.140), branch_computations={%region_21.22_spmd, %region_22.24_spmd} | conditional | flops 139264 | bytes 966664 | solution.py:163
  128.8 11.8 %all_to_all.55 = bf16[16,32,128]{2,1,0:T(8,128)(2,1)S(1)} all-to-all(bf16[16,32,128]{2,1,0:T(8,128)(2,1)S(1)} %copy.19), channel_id=1, replica_groups=mesh['y'=4,'xh'=2,'xl'=2,'z'=8,'c'=2] {'xl','z'}, dimensions={0} | all-to-all | bytes 262144 | tf_op jit(solution)/shard_map/cond/branch_1_fun/all_to_all | solution.py:32
  140.8 0.9 collective-permute-start.17
  141.7 15.6 %conditional.20 = (bf16[64,1920]{1,0:T(8,128)(2,1)S(1)}) conditional(s32[]{:T(128)} %bitcast.19, () %tuple.143, (bf16[32,128]{1,0:T(8,128)(2,1)S(1)}, bf16[2048]{0:T(1024)(128)(2,1)S(1)}, bf16[2048,896]{1,0:T(8,128)(2,1)}, bf16[2048,896]{1,0:T(8,128)(2,1)}, pred[1,128]{1,0:T(4,128)(4,1)S(1)}, /*index=5*/pred[1,128]{1,0:T(4,128)(4,1)S(1)}) %tuple.197), branch_computations={%region_24.25_spmd, %region_25.27_spmd} | conditional | flops 20605652992 | bytes 73119080 | solution.py:163
  141.7 12.4 %all_to_all.56.blocks = bf16[16,32,128]{2,1,0:T(8,128)(2,1)S(1)} all-to-all(bf16[16,32,128]{2,1,0:T(8,128)(2,1)S(1)} %repeat.10), channel_id=1, replica_groups=mesh['y'=4,'xh'=2,'xl'=2,'z'=8,'c'=2] {'xl','z'}, dimensions={0} | all-to-all | bytes 262144 | tf_op jit(solution)/shard_map/cond/branch_1_fun/all_to_all | solution.py:32
  154.3 1.3 collective-permute-done.5
  157.4 0.9 collective-permute-start.18
  158.4 11.6 %conditional.21 = (bf16[8,896]{1,0:T(8,128)(2,1)S(1)}) conditional(s32[]{:T(128)} %bitcast.19, () %tuple.147, bf16[64,1920]{1,0:T(8,128)(2,1)S(1)} %get-tuple-element.392), branch_computations={%region_27.28_spmd, %region_28.30_spmd} | conditional | flops 287776 | bytes 870536 | solution.py:163
  158.4 11.3 %all_to_all.57 = bf16[8,8,1920]{2,1,0:T(8,128)(2,1)S(1)} all-to-all(bf16[8,8,1920]{2,1,0:T(8,128)(2,1)S(1)} %bitcast.59), channel_id=1, replica_groups=mesh['y'=4,'xh'=2,'xl'=2,'z'=8,'c'=2] {'y','xh'}, dimensions={0} | all-to-all | bytes 491520 | tf_op jit(solution)/shard_map/cond/branch_1_fun/all_to_all | solution.py:32
  170.1 1.4 collective-permute-start.19
  171.5 13.4 %conditional.22 = (bf16[32,2048]{1,0:T(8,128)(2,1)S(1)}) conditional(s32[]{:T(128)} %bitcast.19, () %tuple.150, (bf16[8,896]{1,0:T(8,128)(2,1)S(1)}, bf16[896,2048]{1,0:T(8,128)(2,1)}, s32[1,2048]{1,0:T(1,128)S(1)}, s32[]{:T(128)}, bf16[32,128]{1,0:T(8,128)(2,1)S(1)}) %tuple.151), branch_computations={%region_30.31_spmd, %region_31.32_spmd} | conditional | flops 20368082944 | bytes 54464592 | solution.py:163
  171.5 10.9 %all_to_all.58 = bf16[8,8,896]{2,1,0:T(8,128)(2,1)S(1)} all-to-all(bf16[8,8,896]{2,1,0:T(8,128)(2,1)S(1)} %repeat.11), channel_id=1, replica_groups=mesh['y'=4,'xh'=2,'xl'=2,'z'=8,'c'=2] {'y','xh'}, dimensions={0} | all-to-all | bytes 229376 | tf_op jit(solution)/shard_map/cond/branch_1_fun/all_to_all | solution.py:32
  182.5 0.8 convolution_convert_fusion.13
  183.4 1.3 collective-permute-done.6
  184.9 2.6 %collective-permute-start.20 = (bf16[8,2048]{1,0:T(8,128)(2,1)S(1)}, bf16[8,2048]{1,0:T(8,128)(2,1)S(1)}, u32[]{:S(2)}, u32[]{:S(2)}) collective-permute-start(bf16[8,2048]{1,0:T(8,128)(2,1)S(1)} %slice.170), channel_id=1, source_target_pairs={{0,8},{2,10},{4,12},{6,14},{8,0},{10,2},{12,4},{14,6},{1,9},{3,11}... | collective-permute-start | bytes 98312 | tf_op jit(solution)/shard_map/ppermute | solution.py:28
  187.6 13.8 %conditional.23 = (bf16[2,2048]{1,0:T(2,128)(2,1)S(1)}) conditional(s32[]{:T(128)} %bitcast.19, () %tuple.154, bf16[32,2048]{1,0:T(8,128)(2,1)S(1)} %get-tuple-element.394), branch_computations={%region_32.33_spmd, %region_33.35_spmd} | conditional | flops 61440 | bytes 663562 | solution.py:163
  187.7 13.6 %all_to_all.59 = bf16[16,2,2048]{2,1,0:T(2,128)(2,1)S(1)} all-to-all(bf16[16,2,2048]{2,1,0:T(2,128)(2,1)S(1)} %reshape.178), channel_id=1, replica_groups=mesh['y'=4,'xh'=2,'xl'=2,'z'=8,'c'=2] {'xl','z'}, dimensions={0} | all-to-all | bytes 262144 | tf_op jit(solution)/shard_map/cond/branch_1_fun/all_to_all | solution.py:32
  (153 shorter events, 14.0 us)
Async XLA Ops:
  0.7 29.3 %collective-permute-start.7 = (bf16[8,2048]{1,0:T(8,128)(2,1)}, bf16[8,2048]{1,0:T(8,128)(2,1)S(1)}, u32[]{:S(2)}, u32[]{:S(2)}) collective-permute-start(bf16[8,2048]{1,0:T(8,128)(2,1)} %refs_0_.1), channel_id=1, source_target_pairs={{0,8},{2,10},{4,12},{6,14},{8,0},{10,2},{12,4},{14,6},{1,9},{3,11}... | collective-permute-start | bytes 98312 | tf_op jit(solution)/shard_map/ppermute | solution.py:28
  7.0 22.9 %collective-permute-start.8 = (bf16[8,2048]{1,0:T(8,128)(2,1)}, bf16[8,2048]{1,0:T(8,128)(2,1)S(1)}, u32[]{:S(2)}, u32[]{:S(2)}) collective-permute-start(bf16[8,2048]{1,0:T(8,128)(2,1)} %refs_0_.1), channel_id=1, source_target_pairs={{0,4},{2,6},{4,0},{6,2},{8,12},{10,14},{12,8},{14,10},{1,5},{3,7},... | collective-permute-start | bytes 98312 | tf_op jit(solution)/shard_map/ppermute | solution.py:28
  8.5 21.4 %collective-permute-start.9 = (bf16[8,2048]{1,0:T(8,128)(2,1)}, bf16[8,2048]{1,0:T(8,128)(2,1)S(1)}, u32[]{:S(2)}, u32[]{:S(2)}) collective-permute-start(bf16[8,2048]{1,0:T(8,128)(2,1)} %refs_0_.1), channel_id=1, source_target_pairs={{0,12},{2,14},{4,8},{6,10},{8,4},{10,6},{12,0},{14,2},{1,13},{3,15... | collective-permute-start | bytes 98312 | tf_op jit(solution)/shard_map/ppermute | solution.py:28
  9.2 20.8 %copy-start = (bf16[8,2048]{1,0:T(8,128)(2,1)S(1)}, bf16[8,2048]{1,0:T(8,128)(2,1)}, u32[]{:S(2)}) copy-start(bf16[8,2048]{1,0:T(8,128)(2,1)} %refs_0_.1) | copy-start | bytes 98308
  26.0 0.7 copy-start.13
  26.0 2.0 %copy-start.5 = (bf16[2048,896]{1,0:T(8,128)(2,1)S(1)}, bf16[2048,896]{1,0:T(8,128)(2,1)}, u32[]{:S(2)}) copy-start(bf16[2048,896]{1,0:T(8,128)(2,1)} %get-tuple-element.141) | copy-start | bytes 11010052 | tf_op jit(solution)/shard_map/cond
  26.1 3.1 %copy-start.1 = (bf16[2048,896]{1,0:T(8,128)(2,1)S(1)}, bf16[2048,896]{1,0:T(8,128)(2,1)}, u32[]{:S(2)}) copy-start(bf16[2048,896]{1,0:T(8,128)(2,1)} %get-tuple-element.140) | copy-start | bytes 11010052 | tf_op jit(solution)/shard_map/cond
  26.1 1.4 collective-permute-start
  30.0 19.0 %collective-permute-start.10 = (bf16[32,2048]{1,0:T(8,128)(2,1)S(1)}, bf16[32,2048]{1,0:T(8,128)(2,1)S(1)}, u32[]{:S(2)}, u32[]{:S(2)}) collective-permute-start(bf16[32,2048]{1,0:T(8,128)(2,1)S(1)} %stack.2.refs_0_), channel_id=1, source_target_pairs={{0,2},{2,0},{4,6},{6,4},{8,10},{10,8},{12,14},{14,12},{16,18},{18,... | collective-permute-start | bytes 393224 | tf_op jit(solution)/shard_map/ppermute | solution.py:28
  30.7 18.3 %collective-permute-start.11 = (bf16[32,2048]{1,0:T(8,128)(2,1)S(1)}, bf16[32,2048]{1,0:T(8,128)(2,1)S(1)}, u32[]{:S(2)}, u32[]{:S(2)}) collective-permute-start(bf16[32,2048]{1,0:T(8,128)(2,1)S(1)} %stack.2.refs_0_), channel_id=1, source_target_pairs={{0,16},{2,18},{4,20},{6,22},{8,24},{10,26},{12,28},{14,30},{16,0},... | collective-permute-start | bytes 393224 | tf_op jit(solution)/shard_map/ppermute | solution.py:28
  31.7 17.3 %collective-permute-start.12 = (bf16[32,2048]{1,0:T(8,128)(2,1)S(1)}, bf16[32,2048]{1,0:T(8,128)(2,1)S(1)}, u32[]{:S(2)}, u32[]{:S(2)}) collective-permute-start(bf16[32,2048]{1,0:T(8,128)(2,1)S(1)} %stack.2.refs_0_), channel_id=1, source_target_pairs={{0,18},{2,16},{4,22},{6,20},{8,26},{10,24},{12,30},{14,28},{16,2},... | collective-permute-start | bytes 393224 | tf_op jit(solution)/shard_map/ppermute | solution.py:28
  49.1 11.3 %copy-start.9 = (bf16[896,2048]{1,0:T(8,128)(2,1)S(1)}, bf16[896,2048]{1,0:T(8,128)(2,1)}, u32[]{:S(2)}) copy-start(bf16[896,2048]{1,0:T(8,128)(2,1)} %get-tuple-element.149) | copy-start | bytes 11010052 | tf_op jit(solution)/shard_map/cond
  49.1 12.6 %copy-start.14 = (bf16[2048]{0:T(1024)(128)(2,1)S(1)}, bf16[2048]{0:T(1024)(128)(2,1)}, u32[]{:S(2)}) copy-start(bf16[2048]{0:T(1024)(128)(2,1)} %get-tuple-element.152) | copy-start | bytes 12292 | tf_op jit(solution)/shard_map/cond
  49.2 12.6 %copy-start.6 = (bf16[2048,896]{1,0:T(8,128)(2,1)S(1)}, bf16[2048,896]{1,0:T(8,128)(2,1)}, u32[]{:S(2)}) copy-start(bf16[2048,896]{1,0:T(8,128)(2,1)} %get-tuple-element.154) | copy-start | bytes 11010052 | tf_op jit(solution)/shard_map/cond
  60.3 3.1 %collective-permute-start.2 = (bf16[128,2048]{1,0:T(8,128)(2,1)S(1)}, bf16[128,2048]{1,0:T(8,128)(2,1)S(1)}, u32[]{:S(2)}, u32[]{:S(2)}) collective-permute-start(bf16[128,2048]{1,0:T(8,128)(2,1)S(1)} %get-tuple-element.151), channel_id=1, source_target_pairs={{0,1},{1,0},{2,3},{3,2},{4,5},{5,4},{6,7},{7,6},{8,9},{9,8},{10,11... | collective-permute-start | bytes 1572872 | tf_op jit(solution)/shard_map/cond/branch_1_fun/ppermute | solution.py:28
  60.4 2.1 %copy-start.2 = (bf16[2048,896]{1,0:T(8,128)(2,1)S(1)}, bf16[2048,896]{1,0:T(8,128)(2,1)}, u32[]{:S(2)}) copy-start(bf16[2048,896]{1,0:T(8,128)(2,1)} %get-tuple-element.153) | copy-start | bytes 11010052 | tf_op jit(solution)/shard_map/cond
  61.2 2.1 %collective-permute-start.1 = (bf16[32,2048]{1,0:T(8,128)(2,1)S(1)}, bf16[32,2048]{1,0:T(8,128)(2,1)S(1)}, u32[]{:S(2)}, u32[]{:S(2)}) collective-permute-start(bf16[32,2048]{1,0:T(8,128)(2,1)S(1)} %slice.135), channel_id=1, source_target_pairs={{0,1},{1,0},{2,3},{3,2},{4,5},{5,4},{6,7},{7,6},{8,9},{9,8},{10,11... | collective-permute-start | bytes 393224 | tf_op jit(solution)/shard_map/cond/branch_1_fun/ppermute | solution.py:28
  65.3 14.5 %copy-start.12 = (bf16[2048]{0:T(1024)(128)(2,1)S(1)}, bf16[2048]{0:T(1024)(128)(2,1)}, u32[]{:S(2)}) copy-start(bf16[2048]{0:T(1024)(128)(2,1)} %param.34) | copy-start | bytes 12292
  65.4 13.6 %collective-permute-start.13 = (bf16[128,1920]{1,0:T(8,128)(2,1)S(1)}, bf16[128,1920]{1,0:T(8,128)(2,1)S(1)}, u32[]{:S(2)}, u32[]{:S(2)}) collective-permute-start(bf16[128,1920]{1,0:T(8,128)(2,1)S(1)} %get-tuple-element.275), channel_id=1, source_target_pairs={{0,64},{64,0},{128,192},{192,128},{1,65},{65,1},{129,193},{193,129... | collective-permute-start | bytes 1474568 | tf_op jit(solution)/shard_map/ppermute | solution.py:28
  79.1 15.7 %collective-permute-start.14 = (bf16[64,1920]{1,0:T(8,128)(2,1)S(1)}, bf16[64,1920]{1,0:T(8,128)(2,1)S(1)}, u32[]{:S(2)}, u32[]{:S(2)}) collective-permute-start(bf16[64,1920]{1,0:T(8,128)(2,1)S(1)} %broadcast_select_fusion.1), channel_id=1, source_target_pairs={{0,32},{32,0},{1,33},{33,1},{2,34},{34,2},{3,35},{35,3},{4,36},{36... | collective-permute-start | bytes 737288 | tf_op jit(solution)/shard_map/ppermute | solution.py:28
  79.9 13.5 %copy-start.7 = (bf16[2048,896]{1,0:T(8,128)(2,1)S(1)}, bf16[2048,896]{1,0:T(8,128)(2,1)}, u32[]{:S(2)}) copy-start(bf16[2048,896]{1,0:T(8,128)(2,1)} %get-tuple-element.162) | copy-start | bytes 11010052 | tf_op jit(solution)/shard_map/cond
  79.9 14.1 %copy-start.3 = (bf16[2048,896]{1,0:T(8,128)(2,1)S(1)}, bf16[2048,896]{1,0:T(8,128)(2,1)}, u32[]{:S(2)}) copy-start(bf16[2048,896]{1,0:T(8,128)(2,1)} %get-tuple-element.161) | copy-start | bytes 11010052 | tf_op jit(solution)/shard_map/cond
  91.6 1.4 collective-permute-start.3
  94.9 16.4 %collective-permute-start.15 = (bf16[32,1920]{1,0:T(8,128)(2,1)S(1)}, bf16[32,1920]{1,0:T(8,128)(2,1)S(1)}, u32[]{:S(2)}, u32[]{:S(2)}) collective-permute-start(bf16[32,1920]{1,0:T(8,128)(2,1)S(1)} %broadcast_select_fusion.2), channel_id=1, source_target_pairs={{0,128},{64,192},{128,0},{192,64},{1,129},{65,193},{129,1},{193,65... | collective-permute-start | bytes 368648 | tf_op jit(solution)/shard_map/ppermute | solution.py:28
  111.8 13.9 %copy-start.10 = (bf16[896,2048]{1,0:T(8,128)(2,1)S(1)}, bf16[896,2048]{1,0:T(8,128)(2,1)}, u32[]{:S(2)}) copy-start(bf16[896,2048]{1,0:T(8,128)(2,1)} %get-tuple-element.167) | copy-start | bytes 11010052 | tf_op jit(solution)/shard_map/cond
  126.5 1.6 collective-permute-start.4
  128.1 12.5 %collective-permute-start.16 = (bf16[128,2048]{1,0:T(8,128)(2,1)S(1)}, bf16[128,2048]{1,0:T(8,128)(2,1)S(1)}, u32[]{:S(2)}, u32[]{:S(2)}) collective-permute-start(bf16[128,2048]{1,0:T(8,128)(2,1)S(1)} %get-tuple-element.294), channel_id=1, source_target_pairs={{0,1},{1,0},{2,3},{3,2},{4,5},{5,4},{6,7},{7,6},{8,9},{9,8},{10,11... | collective-permute-start | bytes 1572872 | tf_op jit(solution)/shard_map/ppermute | solution.py:28
  140.8 16.6 %collective-permute-start.17 = (bf16[64,2048]{1,0:T(8,128)(2,1)S(1)}, bf16[64,2048]{1,0:T(8,128)(2,1)S(1)}, u32[]{:S(2)}, u32[]{:S(2)}) collective-permute-start(bf16[64,2048]{1,0:T(8,128)(2,1)S(1)} %slice.165), channel_id=1, source_target_pairs={{0,16},{16,0},{1,17},{17,1},{2,18},{18,2},{3,19},{19,3},{4,20},{20... | collective-permute-start | bytes 786440 | tf_op jit(solution)/shard_map/ppermute | solution.py:28
  141.7 14.2 %copy-start.8 = (bf16[2048,896]{1,0:T(8,128)(2,1)S(1)}, bf16[2048,896]{1,0:T(8,128)(2,1)}, u32[]{:S(2)}) copy-start(bf16[2048,896]{1,0:T(8,128)(2,1)} %get-tuple-element.173) | copy-start | bytes 11010052 | tf_op jit(solution)/shard_map/cond
  141.7 14.9 %copy-start.4 = (bf16[2048,896]{1,0:T(8,128)(2,1)S(1)}, bf16[2048,896]{1,0:T(8,128)(2,1)}, u32[]{:S(2)}) copy-start(bf16[2048,896]{1,0:T(8,128)(2,1)} %get-tuple-element.172) | copy-start | bytes 11010052 | tf_op jit(solution)/shard_map/cond
  154.2 1.4 collective-permute-start.5
  157.4 12.6 %collective-permute-start.18 = (bf16[32,2048]{1,0:T(8,128)(2,1)S(1)}, bf16[32,2048]{1,0:T(8,128)(2,1)S(1)}, u32[]{:S(2)}, u32[]{:S(2)}) collective-permute-start(bf16[32,2048]{1,0:T(8,128)(2,1)S(1)} %slice.167), channel_id=1, source_target_pairs={{0,2},{2,0},{4,6},{6,4},{8,10},{10,8},{12,14},{14,12},{1,3},{3,1},... | collective-permute-start | bytes 393224 | tf_op jit(solution)/shard_map/ppermute | solution.py:28
  170.1 14.7 %collective-permute-start.19 = (bf16[16,2048]{1,0:T(8,128)(2,1)S(1)}, bf16[16,2048]{1,0:T(8,128)(2,1)S(1)}, u32[]{:S(2)}, u32[]{:S(2)}) collective-permute-start(bf16[16,2048]{1,0:T(8,128)(2,1)S(1)} %slice.169), channel_id=1, source_target_pairs={{0,4},{2,6},{4,0},{6,2},{8,12},{10,14},{12,8},{14,10},{1,5},{3,7},... | collective-permute-start | bytes 196616 | tf_op jit(solution)/shard_map/ppermute | solution.py:28
  171.5 16.0 %copy-start.16 = (s32[2]{0:T(128)S(1)}, s32[2]{0:T(128)}, u32[]{:S(2)}) copy-start(s32[2]{0:T(128)} %param.33) | copy-start | bytes 28
  171.5 11.0 %copy-start.11 = (bf16[896,2048]{1,0:T(8,128)(2,1)S(1)}, bf16[896,2048]{1,0:T(8,128)(2,1)}, u32[]{:S(2)}) copy-start(bf16[896,2048]{1,0:T(8,128)(2,1)} %get-tuple-element.177) | copy-start | bytes 11010052 | tf_op jit(solution)/shard_map/cond
  183.2 1.4 collective-permute-start.6
  184.9 16.6 %collective-permute-start.20 = (bf16[8,2048]{1,0:T(8,128)(2,1)S(1)}, bf16[8,2048]{1,0:T(8,128)(2,1)S(1)}, u32[]{:S(2)}, u32[]{:S(2)}) collective-permute-start(bf16[8,2048]{1,0:T(8,128)(2,1)S(1)} %slice.170), channel_id=1, source_target_pairs={{0,8},{2,10},{4,12},{6,14},{8,0},{10,2},{12,4},{14,6},{1,9},{3,11}... | collective-permute-start | bytes 98312 | tf_op jit(solution)/shard_map/ppermute | solution.py:28
  201.4 0.7 copy-start.15

commit v5 on v4

--- a/solution.py
+++ b/solution.py
@@ -151,8 +151,8 @@
     lane = lax.broadcasted_iota(jnp.int32, (1, LANES), 1)
     near, column, lane = lax.optimization_barrier((near, chip * LANES, lane))
     marks = lane == 0, lane == 1
+    always = column >= 0
     mine = (lax.broadcasted_iota(jnp.int32, (1, width), 1) // LANES) == chip
-    always = accept_len[0] >= 0
 
     def part(body, *operands):
         def empty(*rest):

time: 203 us -> 202 us (level)
  no operation moved by 1% of the time
where the time goes in v5:
time: 202 us; the launch traced here: 201 us
  blocking collectives  154 us (76%)
  starting transfers between devices  21.4 us (11%)
  matrix products  10.7 us (5%)
  waiting for transfers between devices  5.88 us (3%)
  other arithmetic  4.64 us (2%)
    all_to_all x12, blocking collectives, exchange(): return lax.all_to_all(x, axes, 0, 0)  154 us
    ppermute x21, starting transfers between devices, swap(): return lax.ppermute(x, axes, [(i, i ^ distance) for i in range(count)])  21.4 us
    ppermute x21, waiting for transfers between devices, swap(): return lax.ppermute(x, axes, [(i, i ^ distance) for i in range(count)])  5.88 us
  transfers between devices with their start and end apart: 21, of which 5 were waited for; matrix products, arithmetic and copies ran while one was open for 6% of the time, Pallas kernels for 0%

profile of v5, /device:TPU:32, one launch (start us, length us, event | category | flops | bytes accessed | tf_op | source)
XLA Modules:
  0.0 201.3 jit_solution(3311425642173129499)
XLA Ops:
  0.7 6.4 %collective-permute-start.7 = (bf16[8,2048]{1,0:T(8,128)(2,1)}, bf16[8,2048]{1,0:T(8,128)(2,1)S(1)}, u32[]{:S(2)}, u32[]{:S(2)}) collective-permute-start(bf16[8,2048]{1,0:T(8,128)(2,1)} %refs_0_.1), channel_id=1, source_target_pairs={{0,8},{2,10},{4,12},{6,14},{8,0},{10,2},{12,4},{14,6},{1,9},{3,11}... | collective-permute-start | bytes 98312 | tf_op jit(solution)/shard_map/ppermute | solution.py:28
  7.0 1.5 collective-permute-start.8
  8.5 20.7 %conditional.12 = (bf16[64,1920]{1,0:T(8,128)(2,1)S(1)}, bf16[32,128]{1,0:T(8,128)(2,1)S(1)}) conditional(s32[]{:T(128)} %convert_element_type.394, () %tuple.119, (bf16[2,2048]{1,0:T(2,128)(2,1)}, bf16[2048]{0:T(1024)(128)(2,1)}, bf16[2048,896]{1,0:T(8,128)(2,1)}, bf16[2048,896]{1,0:T(8,128)(2,1)}, pred[1,128]{1,0:T(4,128)(4,1)S(1)}, ...), branch_computations={%region_0.1_spmd, %region_1.3_spmd} | conditional | flops 40738312192 | bytes 106968480 | solution.py:163
  9.2 16.0 %all_to_all.48 = bf16[16,2,2048]{2,1,0:T(2,128)(2,1)S(1)} all-to-all(bf16[16,2,2048]{2,1,0:T(2,128)(2,1)S(1)} %repeat.6), channel_id=1, replica_groups=mesh['y'=4,'xh'=2,'xl'=2,'z'=8,'c'=2] {'xl','z'}, dimensions={0} | all-to-all | bytes 262144 | tf_op jit(solution)/shard_map/cond/branch_1_fun/all_to_all | solution.py:32
  26.1 0.7 collective-permute-done
  29.3 0.8 collective-permute-start.10
  30.1 1.0 collective-permute-start.11
  31.1 1.8 collective-permute-start.12
  32.9 15.4 %conditional.13 = (bf16[8,896]{1,0:T(8,128)(2,1)S(1)}) conditional(s32[]{:T(128)} %convert_element_type.394, () %tuple.123, bf16[64,1920]{1,0:T(8,128)(2,1)S(1)} %get-tuple-element.265), branch_computations={%region_3.4_spmd, %region_4.6_spmd} | conditional | flops 287776 | bytes 870536 | solution.py:163
  32.9 15.1 %all_to_all.49 = bf16[8,8,1920]{2,1,0:T(8,128)(2,1)S(1)} all-to-all(bf16[8,8,1920]{2,1,0:T(8,128)(2,1)S(1)} %bitcast.55), channel_id=1, replica_groups=mesh['y'=4,'xh'=2,'xl'=2,'z'=8,'c'=2] {'y','xh'}, dimensions={0} | all-to-all | bytes 491520 | tf_op jit(solution)/shard_map/cond/branch_1_fun/all_to_all | solution.py:32
  48.4 16.2 %conditional.14 = (bf16[32,2048]{1,0:T(8,128)(2,1)S(1)}, bf16[128,1920]{1,0:T(8,128)(2,1)S(1)}, f32[128,1920]{1,0:T(8,128)S(1)}) conditional(s32[]{:T(128)} %convert_element_type.394, () %tuple.117, (bf16[8,896]{1,0:T(8,128)(2,1)S(1)}, bf16[128,2048]{1,0:T(8,128)(2,1)S(1)}, bf16[2048]{0:T(1024)(128)(2,1)}, bf16[896,2048]{1,0:T(8,128)(2,1)}, ...), branch_computations={%region_6.7_spmd, %region_7.10_spmd} | conditional | flops 22255915008 | bytes 106709472 | solution.py:163
  48.5 10.9 %all_to_all.50 = bf16[8,8,896]{2,1,0:T(8,128)(2,1)S(1)} all-to-all(bf16[8,8,896]{2,1,0:T(8,128)(2,1)S(1)} %repeat.7), channel_id=1, replica_groups=mesh['y'=4,'xh'=2,'xl'=2,'z'=8,'c'=2] {'y','xh'}, dimensions={0} | all-to-all | bytes 229376 | tf_op jit(solution)/shard_map/cond/branch_1_fun/all_to_all | solution.py:32
  59.7 0.8 convolution_convert_fusion.2
  61.1 0.7 convolution_convert_fusion.5
  61.9 0.7 convolution_convert_fusion.6
  63.0 0.7 convolution_convert_fusion.3
  63.8 0.7 convolution_convert_fusion.4
  65.2 11.8 %conditional.15 = (bf16[32,128]{1,0:T(8,128)(2,1)S(1)}) conditional(s32[]{:T(128)} %convert_element_type.394, () %tuple.127, (bf16[32,128]{1,0:T(8,128)(2,1)S(1)}, bf16[32,2048]{1,0:T(8,128)(2,1)S(1)}) %tuple.128), branch_computations={%region_10.11_spmd, %region_11.13_spmd} | conditional | flops 139264 | bytes 966664 | solution.py:163
  65.3 11.7 %all_to_all.51 = bf16[16,32,128]{2,1,0:T(8,128)(2,1)S(1)} all-to-all(bf16[16,32,128]{2,1,0:T(8,128)(2,1)S(1)} %copy.17), channel_id=1, replica_groups=mesh['y'=4,'xh'=2,'xl'=2,'z'=8,'c'=2] {'xl','z'}, dimensions={0} | all-to-all | bytes 262144 | tf_op jit(solution)/shard_map/cond/branch_1_fun/all_to_all | solution.py:32
  77.0 1.2 collective-permute-done.13
  78.4 0.8 collective-permute-start.14
  79.2 14.9 %conditional.16 = (bf16[64,1920]{1,0:T(8,128)(2,1)S(1)}) conditional(s32[]{:T(128)} %convert_element_type.394, () %tuple.131, (bf16[32,128]{1,0:T(8,128)(2,1)S(1)}, bf16[2048]{0:T(1024)(128)(2,1)S(1)}, bf16[2048,896]{1,0:T(8,128)(2,1)}, bf16[2048,896]{1,0:T(8,128)(2,1)}, pred[1,128]{1,0:T(4,128)(4,1)S(1)}, ...), branch_computations={%region_13.14_spmd, %region_14.16_spmd} | conditional | flops 20605652992 | bytes 73119080 | solution.py:163
  79.2 11.7 %all_to_all.52.blocks = bf16[16,32,128]{2,1,0:T(8,128)(2,1)S(1)} all-to-all(bf16[16,32,128]{2,1,0:T(8,128)(2,1)S(1)} %repeat.8), channel_id=1, replica_groups=mesh['y'=4,'xh'=2,'xl'=2,'z'=8,'c'=2] {'xl','z'}, dimensions={0} | all-to-all | bytes 262144 | tf_op jit(solution)/shard_map/cond/branch_1_fun/all_to_all | solution.py:32
  91.1 1.3 collective-permute-done.3
  94.2 1.2 collective-permute-start.15
  95.5 15.0 %conditional.17 = (bf16[8,896]{1,0:T(8,128)(2,1)S(1)}) conditional(s32[]{:T(128)} %convert_element_type.394, () %tuple.135, bf16[64,1920]{1,0:T(8,128)(2,1)S(1)} %get-tuple-element.389), branch_computations={%region_16.17_spmd, %region_17.19_spmd} | conditional | flops 287776 | bytes 870536 | solution.py:163
  95.5 14.7 %all_to_all.53 = bf16[8,8,1920]{2,1,0:T(8,128)(2,1)S(1)} all-to-all(bf16[8,8,1920]{2,1,0:T(8,128)(2,1)S(1)} %bitcast.56), channel_id=1, replica_groups=mesh['y'=4,'xh'=2,'xl'=2,'z'=8,'c'=2] {'y','xh'}, dimensions={0} | all-to-all | bytes 491520 | tf_op jit(solution)/shard_map/cond/branch_1_fun/all_to_all | solution.py:32
  110.8 16.4 %conditional.18 = (bf16[32,2048]{1,0:T(8,128)(2,1)S(1)}, bf16[128,2048]{1,0:T(8,128)(2,1)S(1)}, f32[128,2048]{1,0:T(8,128)S(1)}) conditional(s32[]{:T(128)} %convert_element_type.394, () %tuple.116, (bf16[8,896]{1,0:T(8,128)(2,1)S(1)}, bf16[32,896]{1,0:T(8,128)(2,1)S(1)}, bf16[896,2048]{1,0:T(8,128)(2,1)}) %tuple.137), branch_computations={%region_19.20_spmd, %region_20.21_spmd} | conditional | flops 21308387328 | bytes 65531996 | solution.py:163
  110.9 13.8 %all_to_all.54 = bf16[8,40,896]{2,1,0:T(8,128)(2,1)S(1)} all-to-all(bf16[8,40,896]{2,1,0:T(8,128)(2,1)S(1)} %repeat.9), channel_id=1, replica_groups=mesh['y'=4,'xh'=2,'xl'=2,'z'=8,'c'=2] {'y','xh'}, dimensions={0} | all-to-all | bytes 1146880 | tf_op jit(solution)/shard_map/cond/branch_1_fun/all_to_all | solution.py:32
  124.7 0.8 convolution_convert_fusion.10
  125.7 1.3 convolution_convert_fusion.9
  127.8 11.9 %conditional.19 = (bf16[32,128]{1,0:T(8,128)(2,1)S(1)}) conditional(s32[]{:T(128)} %convert_element_type.394, () %tuple.139, (bf16[32,128]{1,0:T(8,128)(2,1)S(1)}, bf16[32,2048]{1,0:T(8,128)(2,1)S(1)}) %tuple.140), branch_computations={%region_21.22_spmd, %region_22.24_spmd} | conditional | flops 139264 | bytes 966664 | solution.py:163
  127.9 11.8 %all_to_all.55 = bf16[16,32,128]{2,1,0:T(8,128)(2,1)S(1)} all-to-all(bf16[16,32,128]{2,1,0:T(8,128)(2,1)S(1)} %copy.19), channel_id=1, replica_groups=mesh['y'=4,'xh'=2,'xl'=2,'z'=8,'c'=2] {'xl','z'}, dimensions={0} | all-to-all | bytes 262144 | tf_op jit(solution)/shard_map/cond/branch_1_fun/all_to_all | solution.py:32
  139.9 0.9 collective-permute-start.17
  140.8 15.7 %conditional.20 = (bf16[64,1920]{1,0:T(8,128)(2,1)S(1)}) conditional(s32[]{:T(128)} %convert_element_type.394, () %tuple.143, (bf16[32,128]{1,0:T(8,128)(2,1)S(1)}, bf16[2048]{0:T(1024)(128)(2,1)S(1)}, bf16[2048,896]{1,0:T(8,128)(2,1)}, bf16[2048,896]{1,0:T(8,128)(2,1)}, pred[1,128]{1,0:T(4,128)(4,1)S(1)}, ...), branch_computations={%region_24.25_spmd, %region_25.27_spmd} | conditional | flops 20605652992 | bytes 73119080 | solution.py:163
  140.8 12.5 %all_to_all.56.blocks = bf16[16,32,128]{2,1,0:T(8,128)(2,1)S(1)} all-to-all(bf16[16,32,128]{2,1,0:T(8,128)(2,1)S(1)} %repeat.10), channel_id=1, replica_groups=mesh['y'=4,'xh'=2,'xl'=2,'z'=8,'c'=2] {'xl','z'}, dimensions={0} | all-to-all | bytes 262144 | tf_op jit(solution)/shard_map/cond/branch_1_fun/all_to_all | solution.py:32
  153.5 1.3 collective-permute-done.5
  156.6 0.9 collective-permute-start.18
  157.5 11.6 %conditional.21 = (bf16[8,896]{1,0:T(8,128)(2,1)S(1)}) conditional(s32[]{:T(128)} %convert_element_type.394, () %tuple.147, bf16[64,1920]{1,0:T(8,128)(2,1)S(1)} %get-tuple-element.392), branch_computations={%region_27.28_spmd, %region_28.30_spmd} | conditional | flops 287776 | bytes 870536 | solution.py:163
  157.5 11.3 %all_to_all.57 = bf16[8,8,1920]{2,1,0:T(8,128)(2,1)S(1)} all-to-all(bf16[8,8,1920]{2,1,0:T(8,128)(2,1)S(1)} %bitcast.57), channel_id=1, replica_groups=mesh['y'=4,'xh'=2,'xl'=2,'z'=8,'c'=2] {'y','xh'}, dimensions={0} | all-to-all | bytes 491520 | tf_op jit(solution)/shard_map/cond/branch_1_fun/all_to_all | solution.py:32
  169.2 1.4 collective-permute-start.19
  170.6 13.3 %conditional.22 = (bf16[32,2048]{1,0:T(8,128)(2,1)S(1)}) conditional(s32[]{:T(128)} %convert_element_type.394, () %tuple.150, (bf16[8,896]{1,0:T(8,128)(2,1)S(1)}, bf16[896,2048]{1,0:T(8,128)(2,1)}, s32[1,2048]{1,0:T(1,128)S(1)}, s32[]{:T(128)}, bf16[32,128]{1,0:T(8,128)(2,1)S(1)}) %tuple.151), branch_computations={%region_30.31_spmd, %region_31.32_spmd} | conditional | flops 20368082944 | bytes 54464592 | solution.py:163
  170.7 10.9 %all_to_all.58 = bf16[8,8,896]{2,1,0:T(8,128)(2,1)S(1)} all-to-all(bf16[8,8,896]{2,1,0:T(8,128)(2,1)S(1)} %repeat.11), channel_id=1, replica_groups=mesh['y'=4,'xh'=2,'xl'=2,'z'=8,'c'=2] {'y','xh'}, dimensions={0} | all-to-all | bytes 229376 | tf_op jit(solution)/shard_map/cond/branch_1_fun/all_to_all | solution.py:32
  181.6 0.8 convolution_convert_fusion.13
  182.5 1.3 collective-permute-done.6
  184.0 2.5 %collective-permute-start.20 = (bf16[8,2048]{1,0:T(8,128)(2,1)S(1)}, bf16[8,2048]{1,0:T(8,128)(2,1)S(1)}, u32[]{:S(2)}, u32[]{:S(2)}) collective-permute-start(bf16[8,2048]{1,0:T(8,128)(2,1)S(1)} %slice.166), channel_id=1, source_target_pairs={{0,8},{2,10},{4,12},{6,14},{8,0},{10,2},{12,4},{14,6},{1,9},{3,11}... | collective-permute-start | bytes 98312 | tf_op jit(solution)/shard_map/ppermute | solution.py:28
  186.7 13.9 %conditional.23 = (bf16[2,2048]{1,0:T(2,128)(2,1)S(1)}) conditional(s32[]{:T(128)} %convert_element_type.394, () %tuple.154, bf16[32,2048]{1,0:T(8,128)(2,1)S(1)} %get-tuple-element.394), branch_computations={%region_32.33_spmd, %region_33.35_spmd} | conditional | flops 61440 | bytes 663562 | solution.py:163
  186.8 13.6 %all_to_all.59 = bf16[16,2,2048]{2,1,0:T(2,128)(2,1)S(1)} all-to-all(bf16[16,2,2048]{2,1,0:T(2,128)(2,1)S(1)} %reshape.174), channel_id=1, replica_groups=mesh['y'=4,'xh'=2,'xl'=2,'z'=8,'c'=2] {'xl','z'}, dimensions={0} | all-to-all | bytes 262144 | tf_op jit(solution)/shard_map/cond/branch_1_fun/all_to_all | solution.py:32
  (153 shorter events, 14.0 us)
Async XLA Ops:
  0.7 28.6 %collective-permute-start.7 = (bf16[8,2048]{1,0:T(8,128)(2,1)}, bf16[8,2048]{1,0:T(8,128)(2,1)S(1)}, u32[]{:S(2)}, u32[]{:S(2)}) collective-permute-start(bf16[8,2048]{1,0:T(8,128)(2,1)} %refs_0_.1), channel_id=1, source_target_pairs={{0,8},{2,10},{4,12},{6,14},{8,0},{10,2},{12,4},{14,6},{1,9},{3,11}... | collective-permute-start | bytes 98312 | tf_op jit(solution)/shard_map/ppermute | solution.py:28
  7.0 22.2 %collective-permute-start.8 = (bf16[8,2048]{1,0:T(8,128)(2,1)}, bf16[8,2048]{1,0:T(8,128)(2,1)S(1)}, u32[]{:S(2)}, u32[]{:S(2)}) collective-permute-start(bf16[8,2048]{1,0:T(8,128)(2,1)} %refs_0_.1), channel_id=1, source_target_pairs={{0,4},{2,6},{4,0},{6,2},{8,12},{10,14},{12,8},{14,10},{1,5},{3,7},... | collective-permute-start | bytes 98312 | tf_op jit(solution)/shard_map/ppermute | solution.py:28
  8.5 20.8 %collective-permute-start.9 = (bf16[8,2048]{1,0:T(8,128)(2,1)}, bf16[8,2048]{1,0:T(8,128)(2,1)S(1)}, u32[]{:S(2)}, u32[]{:S(2)}) collective-permute-start(bf16[8,2048]{1,0:T(8,128)(2,1)} %refs_0_.1), channel_id=1, source_target_pairs={{0,12},{2,14},{4,8},{6,10},{8,4},{10,6},{12,0},{14,2},{1,13},{3,15... | collective-permute-start | bytes 98312 | tf_op jit(solution)/shard_map/ppermute | solution.py:28
  8.5 20.8 %copy-start = (bf16[8,2048]{1,0:T(8,128)(2,1)S(1)}, bf16[8,2048]{1,0:T(8,128)(2,1)}, u32[]{:S(2)}) copy-start(bf16[8,2048]{1,0:T(8,128)(2,1)} %refs_0_.1) | copy-start | bytes 98308
  25.3 0.7 copy-start.13
  25.4 2.0 %copy-start.5 = (bf16[2048,896]{1,0:T(8,128)(2,1)S(1)}, bf16[2048,896]{1,0:T(8,128)(2,1)}, u32[]{:S(2)}) copy-start(bf16[2048,896]{1,0:T(8,128)(2,1)} %get-tuple-element.141) | copy-start | bytes 11010052 | tf_op jit(solution)/shard_map/cond
  25.4 3.1 %copy-start.1 = (bf16[2048,896]{1,0:T(8,128)(2,1)S(1)}, bf16[2048,896]{1,0:T(8,128)(2,1)}, u32[]{:S(2)}) copy-start(bf16[2048,896]{1,0:T(8,128)(2,1)} %get-tuple-element.140) | copy-start | bytes 11010052 | tf_op jit(solution)/shard_map/cond
  25.4 1.4 collective-permute-start
  29.3 19.0 %collective-permute-start.10 = (bf16[32,2048]{1,0:T(8,128)(2,1)S(1)}, bf16[32,2048]{1,0:T(8,128)(2,1)S(1)}, u32[]{:S(2)}, u32[]{:S(2)}) collective-permute-start(bf16[32,2048]{1,0:T(8,128)(2,1)S(1)} %stack.2.refs_0_), channel_id=1, source_target_pairs={{0,2},{2,0},{4,6},{6,4},{8,10},{10,8},{12,14},{14,12},{16,18},{18,... | collective-permute-start | bytes 393224 | tf_op jit(solution)/shard_map/ppermute | solution.py:28
  30.1 18.3 %collective-permute-start.11 = (bf16[32,2048]{1,0:T(8,128)(2,1)S(1)}, bf16[32,2048]{1,0:T(8,128)(2,1)S(1)}, u32[]{:S(2)}, u32[]{:S(2)}) collective-permute-start(bf16[32,2048]{1,0:T(8,128)(2,1)S(1)} %stack.2.refs_0_), channel_id=1, source_target_pairs={{0,16},{2,18},{4,20},{6,22},{8,24},{10,26},{12,28},{14,30},{16,0},... | collective-permute-start | bytes 393224 | tf_op jit(solution)/shard_map/ppermute | solution.py:28
  31.1 17.3 %collective-permute-start.12 = (bf16[32,2048]{1,0:T(8,128)(2,1)S(1)}, bf16[32,2048]{1,0:T(8,128)(2,1)S(1)}, u32[]{:S(2)}, u32[]{:S(2)}) collective-permute-start(bf16[32,2048]{1,0:T(8,128)(2,1)S(1)} %stack.2.refs_0_), channel_id=1, source_target_pairs={{0,18},{2,16},{4,22},{6,20},{8,26},{10,24},{12,30},{14,28},{16,2},... | collective-permute-start | bytes 393224 | tf_op jit(solution)/shard_map/ppermute | solution.py:28
  48.4 11.3 %copy-start.9 = (bf16[896,2048]{1,0:T(8,128)(2,1)S(1)}, bf16[896,2048]{1,0:T(8,128)(2,1)}, u32[]{:S(2)}) copy-start(bf16[896,2048]{1,0:T(8,128)(2,1)} %get-tuple-element.149) | copy-start | bytes 11010052 | tf_op jit(solution)/shard_map/cond
  48.5 12.6 %copy-start.14 = (bf16[2048]{0:T(1024)(128)(2,1)S(1)}, bf16[2048]{0:T(1024)(128)(2,1)}, u32[]{:S(2)}) copy-start(bf16[2048]{0:T(1024)(128)(2,1)} %get-tuple-element.152) | copy-start | bytes 12292 | tf_op jit(solution)/shard_map/cond
  48.5 12.6 %copy-start.6 = (bf16[2048,896]{1,0:T(8,128)(2,1)S(1)}, bf16[2048,896]{1,0:T(8,128)(2,1)}, u32[]{:S(2)}) copy-start(bf16[2048,896]{1,0:T(8,128)(2,1)} %get-tuple-element.154) | copy-start | bytes 11010052 | tf_op jit(solution)/shard_map/cond
  59.6 3.1 %collective-permute-start.2 = (bf16[128,2048]{1,0:T(8,128)(2,1)S(1)}, bf16[128,2048]{1,0:T(8,128)(2,1)S(1)}, u32[]{:S(2)}, u32[]{:S(2)}) collective-permute-start(bf16[128,2048]{1,0:T(8,128)(2,1)S(1)} %get-tuple-element.151), channel_id=1, source_target_pairs={{0,1},{1,0},{2,3},{3,2},{4,5},{5,4},{6,7},{7,6},{8,9},{9,8},{10,11... | collective-permute-start | bytes 1572872 | tf_op jit(solution)/shard_map/cond/branch_1_fun/ppermute | solution.py:28
  59.7 2.1 %copy-start.2 = (bf16[2048,896]{1,0:T(8,128)(2,1)S(1)}, bf16[2048,896]{1,0:T(8,128)(2,1)}, u32[]{:S(2)}) copy-start(bf16[2048,896]{1,0:T(8,128)(2,1)} %get-tuple-element.153) | copy-start | bytes 11010052 | tf_op jit(solution)/shard_map/cond
  60.5 2.1 %collective-permute-start.1 = (bf16[32,2048]{1,0:T(8,128)(2,1)S(1)}, bf16[32,2048]{1,0:T(8,128)(2,1)S(1)}, u32[]{:S(2)}, u32[]{:S(2)}) collective-permute-start(bf16[32,2048]{1,0:T(8,128)(2,1)S(1)} %slice.131), channel_id=1, source_target_pairs={{0,1},{1,0},{2,3},{3,2},{4,5},{5,4},{6,7},{7,6},{8,9},{9,8},{10,11... | collective-permute-start | bytes 393224 | tf_op jit(solution)/shard_map/cond/branch_1_fun/ppermute | solution.py:28
  64.6 14.5 %copy-start.12 = (bf16[2048]{0:T(1024)(128)(2,1)S(1)}, bf16[2048]{0:T(1024)(128)(2,1)}, u32[]{:S(2)}) copy-start(bf16[2048]{0:T(1024)(128)(2,1)} %param.34) | copy-start | bytes 12292
  64.7 13.6 %collective-permute-start.13 = (bf16[128,1920]{1,0:T(8,128)(2,1)S(1)}, bf16[128,1920]{1,0:T(8,128)(2,1)S(1)}, u32[]{:S(2)}, u32[]{:S(2)}) collective-permute-start(bf16[128,1920]{1,0:T(8,128)(2,1)S(1)} %get-tuple-element.275), channel_id=1, source_target_pairs={{0,64},{64,0},{128,192},{192,128},{1,65},{65,1},{129,193},{193,129... | collective-permute-start | bytes 1474568 | tf_op jit(solution)/shard_map/ppermute | solution.py:28
  78.4 15.7 %collective-permute-start.14 = (bf16[64,1920]{1,0:T(8,128)(2,1)S(1)}, bf16[64,1920]{1,0:T(8,128)(2,1)S(1)}, u32[]{:S(2)}, u32[]{:S(2)}) collective-permute-start(bf16[64,1920]{1,0:T(8,128)(2,1)S(1)} %broadcast_select_fusion.1), channel_id=1, source_target_pairs={{0,32},{32,0},{1,33},{33,1},{2,34},{34,2},{3,35},{35,3},{4,36},{36... | collective-permute-start | bytes 737288 | tf_op jit(solution)/shard_map/ppermute | solution.py:28
  79.2 13.5 %copy-start.7 = (bf16[2048,896]{1,0:T(8,128)(2,1)S(1)}, bf16[2048,896]{1,0:T(8,128)(2,1)}, u32[]{:S(2)}) copy-start(bf16[2048,896]{1,0:T(8,128)(2,1)} %get-tuple-element.162) | copy-start | bytes 11010052 | tf_op jit(solution)/shard_map/cond
  79.2 14.1 %copy-start.3 = (bf16[2048,896]{1,0:T(8,128)(2,1)S(1)}, bf16[2048,896]{1,0:T(8,128)(2,1)}, u32[]{:S(2)}) copy-start(bf16[2048,896]{1,0:T(8,128)(2,1)} %get-tuple-element.161) | copy-start | bytes 11010052 | tf_op jit(solution)/shard_map/cond
  91.0 1.4 collective-permute-start.3
  94.2 16.2 %collective-permute-start.15 = (bf16[32,1920]{1,0:T(8,128)(2,1)S(1)}, bf16[32,1920]{1,0:T(8,128)(2,1)S(1)}, u32[]{:S(2)}, u32[]{:S(2)}) collective-permute-start(bf16[32,1920]{1,0:T(8,128)(2,1)S(1)} %broadcast_select_fusion.2), channel_id=1, source_target_pairs={{0,128},{64,192},{128,0},{192,64},{1,129},{65,193},{129,1},{193,65... | collective-permute-start | bytes 368648 | tf_op jit(solution)/shard_map/ppermute | solution.py:28
  110.9 13.9 %copy-start.10 = (bf16[896,2048]{1,0:T(8,128)(2,1)S(1)}, bf16[896,2048]{1,0:T(8,128)(2,1)}, u32[]{:S(2)}) copy-start(bf16[896,2048]{1,0:T(8,128)(2,1)} %get-tuple-element.167) | copy-start | bytes 11010052 | tf_op jit(solution)/shard_map/cond
  125.6 1.6 collective-permute-start.4
  127.2 12.5 %collective-permute-start.16 = (bf16[128,2048]{1,0:T(8,128)(2,1)S(1)}, bf16[128,2048]{1,0:T(8,128)(2,1)S(1)}, u32[]{:S(2)}, u32[]{:S(2)}) collective-permute-start(bf16[128,2048]{1,0:T(8,128)(2,1)S(1)} %get-tuple-element.294), channel_id=1, source_target_pairs={{0,1},{1,0},{2,3},{3,2},{4,5},{5,4},{6,7},{7,6},{8,9},{9,8},{10,11... | collective-permute-start | bytes 1572872 | tf_op jit(solution)/shard_map/ppermute | solution.py:28
  139.9 16.6 %collective-permute-start.17 = (bf16[64,2048]{1,0:T(8,128)(2,1)S(1)}, bf16[64,2048]{1,0:T(8,128)(2,1)S(1)}, u32[]{:S(2)}, u32[]{:S(2)}) collective-permute-start(bf16[64,2048]{1,0:T(8,128)(2,1)S(1)} %slice.161), channel_id=1, source_target_pairs={{0,16},{16,0},{1,17},{17,1},{2,18},{18,2},{3,19},{19,3},{4,20},{20... | collective-permute-start | bytes 786440 | tf_op jit(solution)/shard_map/ppermute | solution.py:28
  140.8 14.2 %copy-start.8 = (bf16[2048,896]{1,0:T(8,128)(2,1)S(1)}, bf16[2048,896]{1,0:T(8,128)(2,1)}, u32[]{:S(2)}) copy-start(bf16[2048,896]{1,0:T(8,128)(2,1)} %get-tuple-element.173) | copy-start | bytes 11010052 | tf_op jit(solution)/shard_map/cond
  140.8 14.9 %copy-start.4 = (bf16[2048,896]{1,0:T(8,128)(2,1)S(1)}, bf16[2048,896]{1,0:T(8,128)(2,1)}, u32[]{:S(2)}) copy-start(bf16[2048,896]{1,0:T(8,128)(2,1)} %get-tuple-element.172) | copy-start | bytes 11010052 | tf_op jit(solution)/shard_map/cond
  153.4 1.4 collective-permute-start.5
  156.6 12.6 %collective-permute-start.18 = (bf16[32,2048]{1,0:T(8,128)(2,1)S(1)}, bf16[32,2048]{1,0:T(8,128)(2,1)S(1)}, u32[]{:S(2)}, u32[]{:S(2)}) collective-permute-start(bf16[32,2048]{1,0:T(8,128)(2,1)S(1)} %slice.163), channel_id=1, source_target_pairs={{0,2},{2,0},{4,6},{6,4},{8,10},{10,8},{12,14},{14,12},{1,3},{3,1},... | collective-permute-start | bytes 393224 | tf_op jit(solution)/shard_map/ppermute | solution.py:28
  169.2 14.7 %collective-permute-start.19 = (bf16[16,2048]{1,0:T(8,128)(2,1)S(1)}, bf16[16,2048]{1,0:T(8,128)(2,1)S(1)}, u32[]{:S(2)}, u32[]{:S(2)}) collective-permute-start(bf16[16,2048]{1,0:T(8,128)(2,1)S(1)} %slice.165), channel_id=1, source_target_pairs={{0,4},{2,6},{4,0},{6,2},{8,12},{10,14},{12,8},{14,10},{1,5},{3,7},... | collective-permute-start | bytes 196616 | tf_op jit(solution)/shard_map/ppermute | solution.py:28
  170.6 15.9 %copy-start.16 = (s32[2]{0:T(128)S(1)}, s32[2]{0:T(128)}, u32[]{:S(2)}) copy-start(s32[2]{0:T(128)} %param.33) | copy-start | bytes 28
  170.6 11.0 %copy-start.11 = (bf16[896,2048]{1,0:T(8,128)(2,1)S(1)}, bf16[896,2048]{1,0:T(8,128)(2,1)}, u32[]{:S(2)}) copy-start(bf16[896,2048]{1,0:T(8,128)(2,1)} %get-tuple-element.177) | copy-start | bytes 11010052 | tf_op jit(solution)/shard_map/cond
  182.4 1.4 collective-permute-start.6
  184.0 16.6 %collective-permute-start.20 = (bf16[8,2048]{1,0:T(8,128)(2,1)S(1)}, bf16[8,2048]{1,0:T(8,128)(2,1)S(1)}, u32[]{:S(2)}, u32[]{:S(2)}) collective-permute-start(bf16[8,2048]{1,0:T(8,128)(2,1)S(1)} %slice.166), channel_id=1, source_target_pairs={{0,8},{2,10},{4,12},{6,14},{8,0},{10,2},{12,4},{14,6},{1,9},{3,11}... | collective-permute-start | bytes 98312 | tf_op jit(solution)/shard_map/ppermute | solution.py:28
  200.6 0.7 copy-start.15

commit v6 on v5

--- a/solution.py
+++ b/solution.py
@@ -172,7 +172,7 @@
         return wide(keep) + wide(arrived)
 
     def first_rows(draft, gain, marks):
-        draft = spread(draft, CHIPS, N_CHIPS)
+        draft = exchange(draft, CHIPS)
         draft, gain = lax.optimization_barrier((draft, gain))
         draft = draft.reshape(all_draft, width)
         own = rearrange(copy_kernel, (draft,), draft.shape, "own", LOAD)
@@ -201,7 +201,8 @@
         keep, send = halves(down_product(hidden, weights))
         partial = narrow(add(keep, swap(send, "c", 1)))
         own = up_product(verify, gain, marks, weights)
-        other = up_product(swap(verify, "c", 1), gain, marks, weights)
+        partial, other = lax.optimization_barrier((partial, swap(verify, "c", 1)))
+        other = up_product(other, gain, marks, weights)
         return partial, jnp.where(near, other, own), jnp.where(near, own, other)
 
     def share_both(hidden, verify):
@@ -228,8 +229,9 @@
         return narrow(summed(exchange(partial.reshape(N_CHIPS, n_draft, width), CHIPS)))
 
     swaps = [("z", 4), ("z", 2), ("z", 6)]
+    copies = rearrange(repeat_kernel, (draft_in,), (N_CHIPS,) + draft_in.shape, "repeat")
     far_z, near_z, both_z, (packet, state) = beside(
-        verify_in, swaps, first_rows, draft_in, norm_gain, marks
+        verify_in, swaps, first_rows, copies, norm_gain, marks
     )
     verify = stack(verify_in, near_z, far_z, both_z)
     swaps = [(CHIPS, 1), (CHIPS, 8), (CHIPS, 9)]

time: 202 us -> 202 us (level)
  no operation moved by 1% of the time
where the time goes in v6:
time: 202 us; the launch traced here: 201 us
  blocking collectives  154 us (76%)
  starting transfers between devices  21.4 us (11%)
  matrix products  10.7 us (5%)
  waiting for transfers between devices  5.88 us (3%)
  other arithmetic  4.63 us (2%)
  local copies, waits for them, and re-layouts  2.66 us (1%)
    all_to_all x12, blocking collectives, exchange(): return lax.all_to_all(x, axes, 0, 0)  154 us
    ppermute x21, starting transfers between devices, swap(): return lax.ppermute(x, axes, [(i, i ^ distance) for i in range(count)])  21.4 us
    ppermute x21, waiting for transfers between devices, swap(): return lax.ppermute(x, axes, [(i, i ^ distance) for i in range(count)])  5.88 us
  transfers between devices with their start and end apart: 21, of which 5 were waited for; matrix products, arithmetic and copies ran while one was open for 6% of the time, Pallas kernels for 0%

profile of v6, /device:TPU:32, one launch (start us, length us, event | category | flops | bytes accessed | tf_op | source)
XLA Modules:
  0.0 201.3 jit_solution(8773849047808203234)
XLA Ops:
  1.4 6.4 %collective-permute-start.7 = (bf16[8,2048]{1,0:T(8,128)(2,1)}, bf16[8,2048]{1,0:T(8,128)(2,1)S(1)}, u32[]{:S(2)}, u32[]{:S(2)}) collective-permute-start(bf16[8,2048]{1,0:T(8,128)(2,1)} %refs_0_.1), channel_id=1, source_target_pairs={{0,8},{2,10},{4,12},{6,14},{8,0},{10,2},{12,4},{14,6},{1,9},{3,11}... | collective-permute-start | bytes 98312 | tf_op jit(solution)/shard_map/ppermute | solution.py:28
  7.8 1.5 collective-permute-start.8
  9.2 20.1 %conditional.12 = (bf16[64,1920]{1,0:T(8,128)(2,1)S(1)}, bf16[32,128]{1,0:T(8,128)(2,1)S(1)}) conditional(s32[]{:T(128)} %convert_element_type.394, () %tuple.120, (bf16[16,2,2048]{2,1,0:T(2,128)(2,1)S(1)}, bf16[2048]{0:T(1024)(128)(2,1)}, bf16[2048,896]{1,0:T(8,128)(2,1)}, bf16[2048,896]{1,0:T(8,128)(2,1)}, pred[1,128]{1,0:T(4,128)(4,1)S(1)}, ...), branch_computations={%region_0.1_spmd, %region_1.3_spmd} | conditional | flops 20605652992 | bytes 73151888 | solution.py:163
  9.2 16.2 %all_to_all.48 = bf16[16,2,2048]{2,1,0:T(2,128)(2,1)S(1)} all-to-all(bf16[16,2,2048]{2,1,0:T(2,128)(2,1)S(1)} %get-tuple-element.136), channel_id=1, replica_groups=mesh['y'=4,'xh'=2,'xl'=2,'z'=8,'c'=2] {'xl','z'}, dimensions={0} | all-to-all | bytes 262144 | tf_op jit(solution)/shard_map/cond/branch_1_fun/all_to_all | solution.py:32
  26.2 0.7 collective-permute-done
  29.4 0.8 collective-permute-start.10
  30.2 1.0 collective-permute-start.11
  31.2 1.8 collective-permute-start.12
  33.0 15.4 %conditional.13 = (bf16[8,896]{1,0:T(8,128)(2,1)S(1)}) conditional(s32[]{:T(128)} %convert_element_type.394, () %tuple.124, bf16[64,1920]{1,0:T(8,128)(2,1)S(1)} %get-tuple-element.267), branch_computations={%region_3.4_spmd, %region_4.6_spmd} | conditional | flops 287776 | bytes 870536 | solution.py:163
  33.0 15.1 %all_to_all.49 = bf16[8,8,1920]{2,1,0:T(8,128)(2,1)S(1)} all-to-all(bf16[8,8,1920]{2,1,0:T(8,128)(2,1)S(1)} %bitcast.55), channel_id=1, replica_groups=mesh['y'=4,'xh'=2,'xl'=2,'z'=8,'c'=2] {'y','xh'}, dimensions={0} | all-to-all | bytes 491520 | tf_op jit(solution)/shard_map/cond/branch_1_fun/all_to_all | solution.py:32
  48.5 16.2 %conditional.14 = (bf16[32,2048]{1,0:T(8,128)(2,1)S(1)}, bf16[128,1920]{1,0:T(8,128)(2,1)S(1)}, f32[128,1920]{1,0:T(8,128)S(1)}) conditional(s32[]{:T(128)} %convert_element_type.394, () %tuple.118, (bf16[8,896]{1,0:T(8,128)(2,1)S(1)}, bf16[128,2048]{1,0:T(8,128)(2,1)S(1)}, bf16[2048]{0:T(1024)(128)(2,1)}, bf16[896,2048]{1,0:T(8,128)(2,1)}, ...), branch_computations={%region_6.7_spmd, %region_7.10_spmd} | conditional | flops 22255915008 | bytes 106709472 | solution.py:163
  48.6 10.9 %all_to_all.50 = bf16[8,8,896]{2,1,0:T(8,128)(2,1)S(1)} all-to-all(bf16[8,8,896]{2,1,0:T(8,128)(2,1)S(1)} %repeat.6), channel_id=1, replica_groups=mesh['y'=4,'xh'=2,'xl'=2,'z'=8,'c'=2] {'y','xh'}, dimensions={0} | all-to-all | bytes 229376 | tf_op jit(solution)/shard_map/cond/branch_1_fun/all_to_all | solution.py:32
  59.7 0.8 convolution_convert_fusion.2
  61.2 0.7 convolution_convert_fusion.5
  61.9 0.7 convolution_convert_fusion.6
  62.9 0.7 convolution_convert_fusion.3
  63.7 0.7 convolution_convert_fusion.4
  65.2 11.8 %conditional.15 = (bf16[32,128]{1,0:T(8,128)(2,1)S(1)}) conditional(s32[]{:T(128)} %convert_element_type.394, () %tuple.128, (bf16[32,128]{1,0:T(8,128)(2,1)S(1)}, bf16[32,2048]{1,0:T(8,128)(2,1)S(1)}) %tuple.129), branch_computations={%region_10.11_spmd, %region_11.13_spmd} | conditional | flops 139264 | bytes 966664 | solution.py:163
  65.3 11.7 %all_to_all.51 = bf16[16,32,128]{2,1,0:T(8,128)(2,1)S(1)} all-to-all(bf16[16,32,128]{2,1,0:T(8,128)(2,1)S(1)} %copy.17), channel_id=1, replica_groups=mesh['y'=4,'xh'=2,'xl'=2,'z'=8,'c'=2] {'xl','z'}, dimensions={0} | all-to-all | bytes 262144 | tf_op jit(solution)/shard_map/cond/branch_1_fun/all_to_all | solution.py:32
  77.1 1.2 collective-permute-done.13
  78.4 0.8 collective-permute-start.14
  79.2 14.9 %conditional.16 = (bf16[64,1920]{1,0:T(8,128)(2,1)S(1)}) conditional(s32[]{:T(128)} %convert_element_type.394, () %tuple.132, (bf16[32,128]{1,0:T(8,128)(2,1)S(1)}, bf16[2048]{0:T(1024)(128)(2,1)S(1)}, bf16[2048,896]{1,0:T(8,128)(2,1)}, bf16[2048,896]{1,0:T(8,128)(2,1)}, pred[1,128]{1,0:T(4,128)(4,1)S(1)}, ...), branch_computations={%region_13.14_spmd, %region_14.16_spmd} | conditional | flops 20605652992 | bytes 73119080 | solution.py:163
  79.3 11.7 %all_to_all.52.blocks = bf16[16,32,128]{2,1,0:T(8,128)(2,1)S(1)} all-to-all(bf16[16,32,128]{2,1,0:T(8,128)(2,1)S(1)} %repeat.7), channel_id=1, replica_groups=mesh['y'=4,'xh'=2,'xl'=2,'z'=8,'c'=2] {'xl','z'}, dimensions={0} | all-to-all | bytes 262144 | tf_op jit(solution)/shard_map/cond/branch_1_fun/all_to_all | solution.py:32
  91.1 1.3 collective-permute-done.3
  94.3 1.2 collective-permute-start.15
  95.5 15.0 %conditional.17 = (bf16[8,896]{1,0:T(8,128)(2,1)S(1)}) conditional(s32[]{:T(128)} %convert_element_type.394, () %tuple.136, bf16[64,1920]{1,0:T(8,128)(2,1)S(1)} %get-tuple-element.391), branch_computations={%region_16.17_spmd, %region_17.19_spmd} | conditional | flops 287776 | bytes 870536 | solution.py:163
  95.5 14.7 %all_to_all.53 = bf16[8,8,1920]{2,1,0:T(8,128)(2,1)S(1)} all-to-all(bf16[8,8,1920]{2,1,0:T(8,128)(2,1)S(1)} %bitcast.56), channel_id=1, replica_groups=mesh['y'=4,'xh'=2,'xl'=2,'z'=8,'c'=2] {'y','xh'}, dimensions={0} | all-to-all | bytes 491520 | tf_op jit(solution)/shard_map/cond/branch_1_fun/all_to_all | solution.py:32
  110.9 16.4 %conditional.18 = (bf16[32,2048]{1,0:T(8,128)(2,1)S(1)}, bf16[128,2048]{1,0:T(8,128)(2,1)S(1)}, f32[128,2048]{1,0:T(8,128)S(1)}) conditional(s32[]{:T(128)} %convert_element_type.394, () %tuple.117, (bf16[8,896]{1,0:T(8,128)(2,1)S(1)}, bf16[32,896]{1,0:T(8,128)(2,1)S(1)}, bf16[896,2048]{1,0:T(8,128)(2,1)}) %tuple.138), branch_computations={%region_19.20_spmd, %region_20.21_spmd} | conditional | flops 21308387328 | bytes 65531996 | solution.py:163
  111.0 13.8 %all_to_all.54 = bf16[8,40,896]{2,1,0:T(8,128)(2,1)S(1)} all-to-all(bf16[8,40,896]{2,1,0:T(8,128)(2,1)S(1)} %repeat.8), channel_id=1, replica_groups=mesh['y'=4,'xh'=2,'xl'=2,'z'=8,'c'=2] {'y','xh'}, dimensions={0} | all-to-all | bytes 1146880 | tf_op jit(solution)/shard_map/cond/branch_1_fun/all_to_all | solution.py:32
  124.8 0.8 convolution_convert_fusion.10
  125.8 1.3 convolution_convert_fusion.9
  127.9 11.9 %conditional.19 = (bf16[32,128]{1,0:T(8,128)(2,1)S(1)}) conditional(s32[]{:T(128)} %convert_element_type.394, () %tuple.140, (bf16[32,128]{1,0:T(8,128)(2,1)S(1)}, bf16[32,2048]{1,0:T(8,128)(2,1)S(1)}) %tuple.141), branch_computations={%region_21.22_spmd, %region_22.24_spmd} | conditional | flops 139264 | bytes 966664 | solution.py:163
  127.9 11.8 %all_to_all.55 = bf16[16,32,128]{2,1,0:T(8,128)(2,1)S(1)} all-to-all(bf16[16,32,128]{2,1,0:T(8,128)(2,1)S(1)} %copy.19), channel_id=1, replica_groups=mesh['y'=4,'xh'=2,'xl'=2,'z'=8,'c'=2] {'xl','z'}, dimensions={0} | all-to-all | bytes 262144 | tf_op jit(solution)/shard_map/cond/branch_1_fun/all_to_all | solution.py:32
  139.9 0.9 collective-permute-start.17
  140.9 15.7 %conditional.20 = (bf16[64,1920]{1,0:T(8,128)(2,1)S(1)}) conditional(s32[]{:T(128)} %convert_element_type.394, () %tuple.144, (bf16[32,128]{1,0:T(8,128)(2,1)S(1)}, bf16[2048]{0:T(1024)(128)(2,1)S(1)}, bf16[2048,896]{1,0:T(8,128)(2,1)}, bf16[2048,896]{1,0:T(8,128)(2,1)}, pred[1,128]{1,0:T(4,128)(4,1)S(1)}, ...), branch_computations={%region_24.25_spmd, %region_25.27_spmd} | conditional | flops 20605652992 | bytes 73119080 | solution.py:163
  140.9 12.5 %all_to_all.56.blocks = bf16[16,32,128]{2,1,0:T(8,128)(2,1)S(1)} all-to-all(bf16[16,32,128]{2,1,0:T(8,128)(2,1)S(1)} %repeat.9), channel_id=1, replica_groups=mesh['y'=4,'xh'=2,'xl'=2,'z'=8,'c'=2] {'xl','z'}, dimensions={0} | all-to-all | bytes 262144 | tf_op jit(solution)/shard_map/cond/branch_1_fun/all_to_all | solution.py:32
  153.5 1.3 collective-permute-done.5
  156.6 0.9 collective-permute-start.18
  157.6 11.6 %conditional.21 = (bf16[8,896]{1,0:T(8,128)(2,1)S(1)}) conditional(s32[]{:T(128)} %convert_element_type.394, () %tuple.148, bf16[64,1920]{1,0:T(8,128)(2,1)S(1)} %get-tuple-element.394), branch_computations={%region_27.28_spmd, %region_28.30_spmd} | conditional | flops 287776 | bytes 870536 | solution.py:163
  157.6 11.3 %all_to_all.57 = bf16[8,8,1920]{2,1,0:T(8,128)(2,1)S(1)} all-to-all(bf16[8,8,1920]{2,1,0:T(8,128)(2,1)S(1)} %bitcast.57), channel_id=1, replica_groups=mesh['y'=4,'xh'=2,'xl'=2,'z'=8,'c'=2] {'y','xh'}, dimensions={0} | all-to-all | bytes 491520 | tf_op jit(solution)/shard_map/cond/branch_1_fun/all_to_all | solution.py:32
  169.3 1.4 collective-permute-start.19
  170.7 13.3 %conditional.22 = (bf16[32,2048]{1,0:T(8,128)(2,1)S(1)}) conditional(s32[]{:T(128)} %convert_element_type.394, () %tuple.151, (bf16[8,896]{1,0:T(8,128)(2,1)S(1)}, bf16[896,2048]{1,0:T(8,128)(2,1)}, s32[1,2048]{1,0:T(1,128)S(1)}, s32[]{:T(128)}, bf16[32,128]{1,0:T(8,128)(2,1)S(1)}) %tuple.152), branch_computations={%region_30.31_spmd, %region_31.32_spmd} | conditional | flops 20368082944 | bytes 54464592 | solution.py:163
  170.7 10.9 %all_to_all.58 = bf16[8,8,896]{2,1,0:T(8,128)(2,1)S(1)} all-to-all(bf16[8,8,896]{2,1,0:T(8,128)(2,1)S(1)} %repeat.10), channel_id=1, replica_groups=mesh['y'=4,'xh'=2,'xl'=2,'z'=8,'c'=2] {'y','xh'}, dimensions={0} | all-to-all | bytes 229376 | tf_op jit(solution)/shard_map/cond/branch_1_fun/all_to_all | solution.py:32
  181.6 0.8 convolution_convert_fusion.13
  182.6 1.3 collective-permute-done.6
  184.0 2.5 %collective-permute-start.20 = (bf16[8,2048]{1,0:T(8,128)(2,1)S(1)}, bf16[8,2048]{1,0:T(8,128)(2,1)S(1)}, u32[]{:S(2)}, u32[]{:S(2)}) collective-permute-start(bf16[8,2048]{1,0:T(8,128)(2,1)S(1)} %slice.166), channel_id=1, source_target_pairs={{0,8},{2,10},{4,12},{6,14},{8,0},{10,2},{12,4},{14,6},{1,9},{3,11}... | collective-permute-start | bytes 98312 | tf_op jit(solution)/shard_map/ppermute | solution.py:28
  186.7 13.9 %conditional.23 = (bf16[2,2048]{1,0:T(2,128)(2,1)S(1)}) conditional(s32[]{:T(128)} %convert_element_type.394, () %tuple.155, bf16[32,2048]{1,0:T(8,128)(2,1)S(1)} %get-tuple-element.396), branch_computations={%region_32.33_spmd, %region_33.35_spmd} | conditional | flops 61440 | bytes 663562 | solution.py:163
  186.9 13.6 %all_to_all.59 = bf16[16,2,2048]{2,1,0:T(2,128)(2,1)S(1)} all-to-all(bf16[16,2,2048]{2,1,0:T(2,128)(2,1)S(1)} %reshape.174), channel_id=1, replica_groups=mesh['y'=4,'xh'=2,'xl'=2,'z'=8,'c'=2] {'xl','z'}, dimensions={0} | all-to-all | bytes 262144 | tf_op jit(solution)/shard_map/cond/branch_1_fun/all_to_all | solution.py:32
  (155 shorter events, 13.9 us)
Async XLA Ops:
  0.7 0.7 copy-start.1
  1.4 28.0 %collective-permute-start.7 = (bf16[8,2048]{1,0:T(8,128)(2,1)}, bf16[8,2048]{1,0:T(8,128)(2,1)S(1)}, u32[]{:S(2)}, u32[]{:S(2)}) collective-permute-start(bf16[8,2048]{1,0:T(8,128)(2,1)} %refs_0_.1), channel_id=1, source_target_pairs={{0,8},{2,10},{4,12},{6,14},{8,0},{10,2},{12,4},{14,6},{1,9},{3,11}... | collective-permute-start | bytes 98312 | tf_op jit(solution)/shard_map/ppermute | solution.py:28
  7.8 21.6 %collective-permute-start.8 = (bf16[8,2048]{1,0:T(8,128)(2,1)}, bf16[8,2048]{1,0:T(8,128)(2,1)S(1)}, u32[]{:S(2)}, u32[]{:S(2)}) collective-permute-start(bf16[8,2048]{1,0:T(8,128)(2,1)} %refs_0_.1), channel_id=1, source_target_pairs={{0,4},{2,6},{4,0},{6,2},{8,12},{10,14},{12,8},{14,10},{1,5},{3,7},... | collective-permute-start | bytes 98312 | tf_op jit(solution)/shard_map/ppermute | solution.py:28
  9.2 20.2 %collective-permute-start.9 = (bf16[8,2048]{1,0:T(8,128)(2,1)}, bf16[8,2048]{1,0:T(8,128)(2,1)S(1)}, u32[]{:S(2)}, u32[]{:S(2)}) collective-permute-start(bf16[8,2048]{1,0:T(8,128)(2,1)} %refs_0_.1), channel_id=1, source_target_pairs={{0,12},{2,14},{4,8},{6,10},{8,4},{10,6},{12,0},{14,2},{1,13},{3,15... | collective-permute-start | bytes 98312 | tf_op jit(solution)/shard_map/ppermute | solution.py:28
  9.2 20.2 %copy-start = (bf16[8,2048]{1,0:T(8,128)(2,1)S(1)}, bf16[8,2048]{1,0:T(8,128)(2,1)}, u32[]{:S(2)}) copy-start(bf16[8,2048]{1,0:T(8,128)(2,1)} %refs_0_.1) | copy-start | bytes 98308
  25.5 0.7 copy-start.14
  25.5 2.0 %copy-start.6 = (bf16[2048,896]{1,0:T(8,128)(2,1)S(1)}, bf16[2048,896]{1,0:T(8,128)(2,1)}, u32[]{:S(2)}) copy-start(bf16[2048,896]{1,0:T(8,128)(2,1)} %get-tuple-element.141) | copy-start | bytes 11010052 | tf_op jit(solution)/shard_map/cond
  25.5 3.1 %copy-start.2 = (bf16[2048,896]{1,0:T(8,128)(2,1)S(1)}, bf16[2048,896]{1,0:T(8,128)(2,1)}, u32[]{:S(2)}) copy-start(bf16[2048,896]{1,0:T(8,128)(2,1)} %get-tuple-element.140) | copy-start | bytes 11010052 | tf_op jit(solution)/shard_map/cond
  25.5 1.4 collective-permute-start
  29.4 19.0 %collective-permute-start.10 = (bf16[32,2048]{1,0:T(8,128)(2,1)S(1)}, bf16[32,2048]{1,0:T(8,128)(2,1)S(1)}, u32[]{:S(2)}, u32[]{:S(2)}) collective-permute-start(bf16[32,2048]{1,0:T(8,128)(2,1)S(1)} %stack.2.refs_0_), channel_id=1, source_target_pairs={{0,2},{2,0},{4,6},{6,4},{8,10},{10,8},{12,14},{14,12},{16,18},{18,... | collective-permute-start | bytes 393224 | tf_op jit(solution)/shard_map/ppermute | solution.py:28
  30.2 18.3 %collective-permute-start.11 = (bf16[32,2048]{1,0:T(8,128)(2,1)S(1)}, bf16[32,2048]{1,0:T(8,128)(2,1)S(1)}, u32[]{:S(2)}, u32[]{:S(2)}) collective-permute-start(bf16[32,2048]{1,0:T(8,128)(2,1)S(1)} %stack.2.refs_0_), channel_id=1, source_target_pairs={{0,16},{2,18},{4,20},{6,22},{8,24},{10,26},{12,28},{14,30},{16,0},... | collective-permute-start | bytes 393224 | tf_op jit(solution)/shard_map/ppermute | solution.py:28
  31.2 17.3 %collective-permute-start.12 = (bf16[32,2048]{1,0:T(8,128)(2,1)S(1)}, bf16[32,2048]{1,0:T(8,128)(2,1)S(1)}, u32[]{:S(2)}, u32[]{:S(2)}) collective-permute-start(bf16[32,2048]{1,0:T(8,128)(2,1)S(1)} %stack.2.refs_0_), channel_id=1, source_target_pairs={{0,18},{2,16},{4,22},{6,20},{8,26},{10,24},{12,30},{14,28},{16,2},... | collective-permute-start | bytes 393224 | tf_op jit(solution)/shard_map/ppermute | solution.py:28
  48.5 11.2 %copy-start.10 = (bf16[896,2048]{1,0:T(8,128)(2,1)S(1)}, bf16[896,2048]{1,0:T(8,128)(2,1)}, u32[]{:S(2)}) copy-start(bf16[896,2048]{1,0:T(8,128)(2,1)} %get-tuple-element.149) | copy-start | bytes 11010052 | tf_op jit(solution)/shard_map/cond
  48.6 12.6 %copy-start.15 = (bf16[2048]{0:T(1024)(128)(2,1)S(1)}, bf16[2048]{0:T(1024)(128)(2,1)}, u32[]{:S(2)}) copy-start(bf16[2048]{0:T(1024)(128)(2,1)} %get-tuple-element.153) | copy-start | bytes 12292 | tf_op jit(solution)/shard_map/cond
  48.6 12.6 %copy-start.7 = (bf16[2048,896]{1,0:T(8,128)(2,1)S(1)}, bf16[2048,896]{1,0:T(8,128)(2,1)}, u32[]{:S(2)}) copy-start(bf16[2048,896]{1,0:T(8,128)(2,1)} %get-tuple-element.155) | copy-start | bytes 11010052 | tf_op jit(solution)/shard_map/cond
  59.5 3.2 %collective-permute-start.2 = (bf16[128,2048]{1,0:T(8,128)(2,1)S(1)}, bf16[128,2048]{1,0:T(8,128)(2,1)S(1)}, u32[]{:S(2)}, u32[]{:S(2)}) collective-permute-start(bf16[128,2048]{1,0:T(8,128)(2,1)S(1)} %get-tuple-element.150), channel_id=1, source_target_pairs={{0,1},{1,0},{2,3},{3,2},{4,5},{5,4},{6,7},{7,6},{8,9},{9,8},{10,11... | collective-permute-start | bytes 1572872 | tf_op jit(solution)/shard_map/cond/branch_1_fun/ppermute | solution.py:28
  59.7 2.2 %copy-start.3 = (bf16[2048,896]{1,0:T(8,128)(2,1)S(1)}, bf16[2048,896]{1,0:T(8,128)(2,1)}, u32[]{:S(2)}) copy-start(bf16[2048,896]{1,0:T(8,128)(2,1)} %get-tuple-element.154) | copy-start | bytes 11010052 | tf_op jit(solution)/shard_map/cond
  60.6 2.1 %collective-permute-start.1 = (bf16[32,2048]{1,0:T(8,128)(2,1)S(1)}, bf16[32,2048]{1,0:T(8,128)(2,1)S(1)}, u32[]{:S(2)}, u32[]{:S(2)}) collective-permute-start(bf16[32,2048]{1,0:T(8,128)(2,1)S(1)} %slice.131), channel_id=1, source_target_pairs={{0,1},{1,0},{2,3},{3,2},{4,5},{5,4},{6,7},{7,6},{8,9},{9,8},{10,11... | collective-permute-start | bytes 393224 | tf_op jit(solution)/shard_map/cond/branch_1_fun/ppermute | solution.py:28
  64.7 14.5 %copy-start.13 = (bf16[2048]{0:T(1024)(128)(2,1)S(1)}, bf16[2048]{0:T(1024)(128)(2,1)}, u32[]{:S(2)}) copy-start(bf16[2048]{0:T(1024)(128)(2,1)} %param.34) | copy-start | bytes 12292
  64.7 13.6 %collective-permute-start.13 = (bf16[128,1920]{1,0:T(8,128)(2,1)S(1)}, bf16[128,1920]{1,0:T(8,128)(2,1)S(1)}, u32[]{:S(2)}, u32[]{:S(2)}) collective-permute-start(bf16[128,1920]{1,0:T(8,128)(2,1)S(1)} %get-tuple-element.277), channel_id=1, source_target_pairs={{0,64},{64,0},{128,192},{192,128},{1,65},{65,1},{129,193},{193,129... | collective-permute-start | bytes 1474568 | tf_op jit(solution)/shard_map/ppermute | solution.py:28
  78.4 15.7 %collective-permute-start.14 = (bf16[64,1920]{1,0:T(8,128)(2,1)S(1)}, bf16[64,1920]{1,0:T(8,128)(2,1)S(1)}, u32[]{:S(2)}, u32[]{:S(2)}) collective-permute-start(bf16[64,1920]{1,0:T(8,128)(2,1)S(1)} %broadcast_select_fusion.1), channel_id=1, source_target_pairs={{0,32},{32,0},{1,33},{33,1},{2,34},{34,2},{3,35},{35,3},{4,36},{36... | collective-permute-start | bytes 737288 | tf_op jit(solution)/shard_map/ppermute | solution.py:28
  79.2 13.5 %copy-start.8 = (bf16[2048,896]{1,0:T(8,128)(2,1)S(1)}, bf16[2048,896]{1,0:T(8,128)(2,1)}, u32[]{:S(2)}) copy-start(bf16[2048,896]{1,0:T(8,128)(2,1)} %get-tuple-element.164) | copy-start | bytes 11010052 | tf_op jit(solution)/shard_map/cond
  79.3 14.1 %copy-start.4 = (bf16[2048,896]{1,0:T(8,128)(2,1)S(1)}, bf16[2048,896]{1,0:T(8,128)(2,1)}, u32[]{:S(2)}) copy-start(bf16[2048,896]{1,0:T(8,128)(2,1)} %get-tuple-element.163) | copy-start | bytes 11010052 | tf_op jit(solution)/shard_map/cond
  91.0 1.4 collective-permute-start.3
  94.3 16.2 %collective-permute-start.15 = (bf16[32,1920]{1,0:T(8,128)(2,1)S(1)}, bf16[32,1920]{1,0:T(8,128)(2,1)S(1)}, u32[]{:S(2)}, u32[]{:S(2)}) collective-permute-start(bf16[32,1920]{1,0:T(8,128)(2,1)S(1)} %broadcast_select_fusion.2), channel_id=1, source_target_pairs={{0,128},{64,192},{128,0},{192,64},{1,129},{65,193},{129,1},{193,65... | collective-permute-start | bytes 368648 | tf_op jit(solution)/shard_map/ppermute | solution.py:28
  110.9 13.9 %copy-start.11 = (bf16[896,2048]{1,0:T(8,128)(2,1)S(1)}, bf16[896,2048]{1,0:T(8,128)(2,1)}, u32[]{:S(2)}) copy-start(bf16[896,2048]{1,0:T(8,128)(2,1)} %get-tuple-element.169) | copy-start | bytes 11010052 | tf_op jit(solution)/shard_map/cond
  125.6 1.6 collective-permute-start.4
  127.3 12.5 %collective-permute-start.16 = (bf16[128,2048]{1,0:T(8,128)(2,1)S(1)}, bf16[128,2048]{1,0:T(8,128)(2,1)S(1)}, u32[]{:S(2)}, u32[]{:S(2)}) collective-permute-start(bf16[128,2048]{1,0:T(8,128)(2,1)S(1)} %get-tuple-element.296), channel_id=1, source_target_pairs={{0,1},{1,0},{2,3},{3,2},{4,5},{5,4},{6,7},{7,6},{8,9},{9,8},{10,11... | collective-permute-start | bytes 1572872 | tf_op jit(solution)/shard_map/ppermute | solution.py:28
  139.9 16.6 %collective-permute-start.17 = (bf16[64,2048]{1,0:T(8,128)(2,1)S(1)}, bf16[64,2048]{1,0:T(8,128)(2,1)S(1)}, u32[]{:S(2)}, u32[]{:S(2)}) collective-permute-start(bf16[64,2048]{1,0:T(8,128)(2,1)S(1)} %slice.161), channel_id=1, source_target_pairs={{0,16},{16,0},{1,17},{17,1},{2,18},{18,2},{3,19},{19,3},{4,20},{20... | collective-permute-start | bytes 786440 | tf_op jit(solution)/shard_map/ppermute | solution.py:28
  140.9 14.2 %copy-start.9 = (bf16[2048,896]{1,0:T(8,128)(2,1)S(1)}, bf16[2048,896]{1,0:T(8,128)(2,1)}, u32[]{:S(2)}) copy-start(bf16[2048,896]{1,0:T(8,128)(2,1)} %get-tuple-element.175) | copy-start | bytes 11010052 | tf_op jit(solution)/shard_map/cond
  140.9 14.9 %copy-start.5 = (bf16[2048,896]{1,0:T(8,128)(2,1)S(1)}, bf16[2048,896]{1,0:T(8,128)(2,1)}, u32[]{:S(2)}) copy-start(bf16[2048,896]{1,0:T(8,128)(2,1)} %get-tuple-element.174) | copy-start | bytes 11010052 | tf_op jit(solution)/shard_map/cond
  153.4 1.4 collective-permute-start.5
  156.6 12.6 %collective-permute-start.18 = (bf16[32,2048]{1,0:T(8,128)(2,1)S(1)}, bf16[32,2048]{1,0:T(8,128)(2,1)S(1)}, u32[]{:S(2)}, u32[]{:S(2)}) collective-permute-start(bf16[32,2048]{1,0:T(8,128)(2,1)S(1)} %slice.163), channel_id=1, source_target_pairs={{0,2},{2,0},{4,6},{6,4},{8,10},{10,8},{12,14},{14,12},{1,3},{3,1},... | collective-permute-start | bytes 393224 | tf_op jit(solution)/shard_map/ppermute | solution.py:28
  169.3 14.7 %collective-permute-start.19 = (bf16[16,2048]{1,0:T(8,128)(2,1)S(1)}, bf16[16,2048]{1,0:T(8,128)(2,1)S(1)}, u32[]{:S(2)}, u32[]{:S(2)}) collective-permute-start(bf16[16,2048]{1,0:T(8,128)(2,1)S(1)} %slice.165), channel_id=1, source_target_pairs={{0,4},{2,6},{4,0},{6,2},{8,12},{10,14},{12,8},{14,10},{1,5},{3,7},... | collective-permute-start | bytes 196616 | tf_op jit(solution)/shard_map/ppermute | solution.py:28
  170.7 15.9 %copy-start.17 = (s32[2]{0:T(128)S(1)}, s32[2]{0:T(128)}, u32[]{:S(2)}) copy-start(s32[2]{0:T(128)} %param.33) | copy-start | bytes 28
  170.7 11.0 %copy-start.12 = (bf16[896,2048]{1,0:T(8,128)(2,1)S(1)}, bf16[896,2048]{1,0:T(8,128)(2,1)}, u32[]{:S(2)}) copy-start(bf16[896,2048]{1,0:T(8,128)(2,1)} %get-tuple-element.179) | copy-start | bytes 11010052 | tf_op jit(solution)/shard_map/cond
  182.4 1.4 collective-permute-start.6
  184.0 16.6 %collective-permute-start.20 = (bf16[8,2048]{1,0:T(8,128)(2,1)S(1)}, bf16[8,2048]{1,0:T(8,128)(2,1)S(1)}, u32[]{:S(2)}, u32[]{:S(2)}) collective-permute-start(bf16[8,2048]{1,0:T(8,128)(2,1)S(1)} %slice.166), channel_id=1, source_target_pairs={{0,8},{2,10},{4,12},{6,14},{8,0},{10,2},{12,4},{14,6},{1,9},{3,11}... | collective-permute-start | bytes 98312 | tf_op jit(solution)/shard_map/ppermute | solution.py:28
  200.6 0.7 copy-start.16

commit v7 on v6

--- a/solution.py
+++ b/solution.py
@@ -212,7 +212,7 @@
         keep, send = halves(down_product(hidden, weights))
         partial = narrow(add(keep, swap(send, "c", 1)))
         verify = both[:, n_own:].reshape(2, 2, 2, 2, 2, n_verify, units)
-        verify = jnp.transpose(verify, (1, 2, 0, 4, 3, 5, 6)).reshape(-1, units)
+        verify = jnp.transpose(verify, (1, 2, 0, 3, 4, 5, 6)).reshape(-1, units)
         return partial, *halves(down_product(verify, weights))
 
     def share_last(hidden, state):
@@ -251,9 +251,9 @@
     keep, send = halves(narrow(add(keep, arrived)))
     arrived, hidden = beside(send, [("z", 1)], sum_width, packet)
     keep, send = halves(narrow(add(keep, arrived)))
-    arrived, partial = beside(send, [("z", 2)], share_last, hidden, state)
-    keep, send = halves(narrow(add(keep, arrived)))
-    arrived, draft_out = beside(send, [("z", 4)], last_sum, partial)
+    arrived, partial = beside(send, [("z", 4)], share_last, hidden, state)
+    keep, send = halves(narrow(add(keep, arrived)))
+    arrived, draft_out = beside(send, [("z", 2)], last_sum, partial)
     live = (
         (jnp.arange(POS, dtype=jnp.int32)[None, :] <= accept_len[:, None])
         .reshape(-1, 1)

time: 202 us -> 202 us (level)
  no operation moved by 1% of the time
where the time goes in v7:
time: 202 us; the launch traced here: 201 us
  blocking collectives  154 us (76%)
  starting transfers between devices  21.4 us (11%)
  matrix products  10.7 us (5%)
  waiting for transfers between devices  5.88 us (3%)
  other arithmetic  4.63 us (2%)
  local copies, waits for them, and re-layouts  2.66 us (1%)
    all_to_all x12, blocking collectives, exchange(): return lax.all_to_all(x, axes, 0, 0)  154 us
    ppermute x21, starting transfers between devices, swap(): return lax.ppermute(x, axes, [(i, i ^ distance) for i in range(count)])  21.4 us
    ppermute x21, waiting for transfers between devices, swap(): return lax.ppermute(x, axes, [(i, i ^ distance) for i in range(count)])  5.88 us
  transfers between devices with their start and end apart: 21, of which 5 were waited for; matrix products, arithmetic and copies ran while one was open for 6% of the time, Pallas kernels for 0%

profile of v7, /device:TPU:32, one launch (start us, length us, event | category | flops | bytes accessed | tf_op | source)
XLA Modules:
  0.0 201.3 jit_solution(4604713680700405417)
XLA Ops:
  1.4 6.4 %collective-permute-start.7 = (bf16[8,2048]{1,0:T(8,128)(2,1)}, bf16[8,2048]{1,0:T(8,128)(2,1)S(1)}, u32[]{:S(2)}, u32[]{:S(2)}) collective-permute-start(bf16[8,2048]{1,0:T(8,128)(2,1)} %refs_0_.1), channel_id=1, source_target_pairs={{0,8},{2,10},{4,12},{6,14},{8,0},{10,2},{12,4},{14,6},{1,9},{3,11}... | collective-permute-start | bytes 98312 | tf_op jit(solution)/shard_map/ppermute | solution.py:28
  7.8 1.5 collective-permute-start.8
  9.2 20.1 %conditional.12 = (bf16[64,1920]{1,0:T(8,128)(2,1)S(1)}, bf16[32,128]{1,0:T(8,128)(2,1)S(1)}) conditional(s32[]{:T(128)} %convert_element_type.394, () %tuple.120, (bf16[16,2,2048]{2,1,0:T(2,128)(2,1)S(1)}, bf16[2048]{0:T(1024)(128)(2,1)}, bf16[2048,896]{1,0:T(8,128)(2,1)}, bf16[2048,896]{1,0:T(8,128)(2,1)}, pred[1,128]{1,0:T(4,128)(4,1)S(1)}, ...), branch_computations={%region_0.1_spmd, %region_1.3_spmd} | conditional | flops 20605652992 | bytes 73151888 | solution.py:163
  9.2 16.2 %all_to_all.48 = bf16[16,2,2048]{2,1,0:T(2,128)(2,1)S(1)} all-to-all(bf16[16,2,2048]{2,1,0:T(2,128)(2,1)S(1)} %get-tuple-element.136), channel_id=1, replica_groups=mesh['y'=4,'xh'=2,'xl'=2,'z'=8,'c'=2] {'xl','z'}, dimensions={0} | all-to-all | bytes 262144 | tf_op jit(solution)/shard_map/cond/branch_1_fun/all_to_all | solution.py:32
  26.2 0.7 collective-permute-done
  29.4 0.8 collective-permute-start.10
  30.2 1.0 collective-permute-start.11
  31.2 1.8 collective-permute-start.12
  33.0 15.4 %conditional.13 = (bf16[8,896]{1,0:T(8,128)(2,1)S(1)}) conditional(s32[]{:T(128)} %convert_element_type.394, () %tuple.124, bf16[64,1920]{1,0:T(8,128)(2,1)S(1)} %get-tuple-element.267), branch_computations={%region_3.4_spmd, %region_4.6_spmd} | conditional | flops 287776 | bytes 870536 | solution.py:163
  33.0 15.1 %all_to_all.49 = bf16[8,8,1920]{2,1,0:T(8,128)(2,1)S(1)} all-to-all(bf16[8,8,1920]{2,1,0:T(8,128)(2,1)S(1)} %bitcast.55), channel_id=1, replica_groups=mesh['y'=4,'xh'=2,'xl'=2,'z'=8,'c'=2] {'y','xh'}, dimensions={0} | all-to-all | bytes 491520 | tf_op jit(solution)/shard_map/cond/branch_1_fun/all_to_all | solution.py:32
  48.5 16.2 %conditional.14 = (bf16[32,2048]{1,0:T(8,128)(2,1)S(1)}, bf16[128,1920]{1,0:T(8,128)(2,1)S(1)}, f32[128,1920]{1,0:T(8,128)S(1)}) conditional(s32[]{:T(128)} %convert_element_type.394, () %tuple.118, (bf16[8,896]{1,0:T(8,128)(2,1)S(1)}, bf16[128,2048]{1,0:T(8,128)(2,1)S(1)}, bf16[2048]{0:T(1024)(128)(2,1)}, bf16[896,2048]{1,0:T(8,128)(2,1)}, ...), branch_computations={%region_6.7_spmd, %region_7.10_spmd} | conditional | flops 22255915008 | bytes 106709472 | solution.py:163
  48.6 10.9 %all_to_all.50 = bf16[8,8,896]{2,1,0:T(8,128)(2,1)S(1)} all-to-all(bf16[8,8,896]{2,1,0:T(8,128)(2,1)S(1)} %repeat.6), channel_id=1, replica_groups=mesh['y'=4,'xh'=2,'xl'=2,'z'=8,'c'=2] {'y','xh'}, dimensions={0} | all-to-all | bytes 229376 | tf_op jit(solution)/shard_map/cond/branch_1_fun/all_to_all | solution.py:32
  59.7 0.8 convolution_convert_fusion.2
  61.2 0.7 convolution_convert_fusion.5
  61.9 0.7 convolution_convert_fusion.6
  62.9 0.7 convolution_convert_fusion.3
  63.7 0.7 convolution_convert_fusion.4
  65.2 11.8 %conditional.15 = (bf16[32,128]{1,0:T(8,128)(2,1)S(1)}) conditional(s32[]{:T(128)} %convert_element_type.394, () %tuple.128, (bf16[32,128]{1,0:T(8,128)(2,1)S(1)}, bf16[32,2048]{1,0:T(8,128)(2,1)S(1)}) %tuple.129), branch_computations={%region_10.11_spmd, %region_11.13_spmd} | conditional | flops 139264 | bytes 966664 | solution.py:163
  65.3 11.7 %all_to_all.51 = bf16[16,32,128]{2,1,0:T(8,128)(2,1)S(1)} all-to-all(bf16[16,32,128]{2,1,0:T(8,128)(2,1)S(1)} %copy.17), channel_id=1, replica_groups=mesh['y'=4,'xh'=2,'xl'=2,'z'=8,'c'=2] {'xl','z'}, dimensions={0} | all-to-all | bytes 262144 | tf_op jit(solution)/shard_map/cond/branch_1_fun/all_to_all | solution.py:32
  77.1 1.2 collective-permute-done.13
  78.4 0.8 collective-permute-start.14
  79.2 14.9 %conditional.16 = (bf16[64,1920]{1,0:T(8,128)(2,1)S(1)}) conditional(s32[]{:T(128)} %convert_element_type.394, () %tuple.132, (bf16[32,128]{1,0:T(8,128)(2,1)S(1)}, bf16[2048]{0:T(1024)(128)(2,1)S(1)}, bf16[2048,896]{1,0:T(8,128)(2,1)}, bf16[2048,896]{1,0:T(8,128)(2,1)}, pred[1,128]{1,0:T(4,128)(4,1)S(1)}, ...), branch_computations={%region_13.14_spmd, %region_14.16_spmd} | conditional | flops 20605652992 | bytes 73119080 | solution.py:163
  79.3 11.7 %all_to_all.52.blocks = bf16[16,32,128]{2,1,0:T(8,128)(2,1)S(1)} all-to-all(bf16[16,32,128]{2,1,0:T(8,128)(2,1)S(1)} %repeat.7), channel_id=1, replica_groups=mesh['y'=4,'xh'=2,'xl'=2,'z'=8,'c'=2] {'xl','z'}, dimensions={0} | all-to-all | bytes 262144 | tf_op jit(solution)/shard_map/cond/branch_1_fun/all_to_all | solution.py:32
  91.1 1.3 collective-permute-done.3
  94.3 1.2 collective-permute-start.15
  95.5 15.0 %conditional.17 = (bf16[8,896]{1,0:T(8,128)(2,1)S(1)}) conditional(s32[]{:T(128)} %convert_element_type.394, () %tuple.136, bf16[64,1920]{1,0:T(8,128)(2,1)S(1)} %get-tuple-element.391), branch_computations={%region_16.17_spmd, %region_17.19_spmd} | conditional | flops 287776 | bytes 870536 | solution.py:163
  95.5 14.7 %all_to_all.53 = bf16[8,8,1920]{2,1,0:T(8,128)(2,1)S(1)} all-to-all(bf16[8,8,1920]{2,1,0:T(8,128)(2,1)S(1)} %bitcast.56), channel_id=1, replica_groups=mesh['y'=4,'xh'=2,'xl'=2,'z'=8,'c'=2] {'y','xh'}, dimensions={0} | all-to-all | bytes 491520 | tf_op jit(solution)/shard_map/cond/branch_1_fun/all_to_all | solution.py:32
  110.9 16.4 %conditional.18 = (bf16[32,2048]{1,0:T(8,128)(2,1)S(1)}, bf16[128,2048]{1,0:T(8,128)(2,1)S(1)}, f32[128,2048]{1,0:T(8,128)S(1)}) conditional(s32[]{:T(128)} %convert_element_type.394, () %tuple.117, (bf16[8,896]{1,0:T(8,128)(2,1)S(1)}, bf16[32,896]{1,0:T(8,128)(2,1)S(1)}, bf16[896,2048]{1,0:T(8,128)(2,1)}) %tuple.138), branch_computations={%region_19.20_spmd, %region_20.21_spmd} | conditional | flops 21308387328 | bytes 65531996 | solution.py:163
  111.0 13.8 %all_to_all.54 = bf16[8,40,896]{2,1,0:T(8,128)(2,1)S(1)} all-to-all(bf16[8,40,896]{2,1,0:T(8,128)(2,1)S(1)} %repeat.8), channel_id=1, replica_groups=mesh['y'=4,'xh'=2,'xl'=2,'z'=8,'c'=2] {'y','xh'}, dimensions={0} | all-to-all | bytes 1146880 | tf_op jit(solution)/shard_map/cond/branch_1_fun/all_to_all | solution.py:32
  124.8 0.8 convolution_convert_fusion.10
  125.8 1.3 convolution_convert_fusion.9
  127.9 11.9 %conditional.19 = (bf16[32,128]{1,0:T(8,128)(2,1)S(1)}) conditional(s32[]{:T(128)} %convert_element_type.394, () %tuple.140, (bf16[32,128]{1,0:T(8,128)(2,1)S(1)}, bf16[32,2048]{1,0:T(8,128)(2,1)S(1)}) %tuple.141), branch_computations={%region_21.22_spmd, %region_22.24_spmd} | conditional | flops 139264 | bytes 966664 | solution.py:163
  127.9 11.8 %all_to_all.55 = bf16[16,32,128]{2,1,0:T(8,128)(2,1)S(1)} all-to-all(bf16[16,32,128]{2,1,0:T(8,128)(2,1)S(1)} %copy.19), channel_id=1, replica_groups=mesh['y'=4,'xh'=2,'xl'=2,'z'=8,'c'=2] {'xl','z'}, dimensions={0} | all-to-all | bytes 262144 | tf_op jit(solution)/shard_map/cond/branch_1_fun/all_to_all | solution.py:32
  139.9 0.9 collective-permute-start.17
  140.9 15.7 %conditional.20 = (bf16[64,1920]{1,0:T(8,128)(2,1)S(1)}) conditional(s32[]{:T(128)} %convert_element_type.394, () %tuple.144, (bf16[32,128]{1,0:T(8,128)(2,1)S(1)}, bf16[2048]{0:T(1024)(128)(2,1)S(1)}, bf16[2048,896]{1,0:T(8,128)(2,1)}, bf16[2048,896]{1,0:T(8,128)(2,1)}, pred[1,128]{1,0:T(4,128)(4,1)S(1)}, ...), branch_computations={%region_24.25_spmd, %region_25.27_spmd} | conditional | flops 20605652992 | bytes 73119080 | solution.py:163
  140.9 12.5 %all_to_all.56.blocks = bf16[16,32,128]{2,1,0:T(8,128)(2,1)S(1)} all-to-all(bf16[16,32,128]{2,1,0:T(8,128)(2,1)S(1)} %repeat.9), channel_id=1, replica_groups=mesh['y'=4,'xh'=2,'xl'=2,'z'=8,'c'=2] {'xl','z'}, dimensions={0} | all-to-all | bytes 262144 | tf_op jit(solution)/shard_map/cond/branch_1_fun/all_to_all | solution.py:32
  153.5 1.3 collective-permute-done.5
  156.6 0.9 collective-permute-start.18
  157.6 11.6 %conditional.21 = (bf16[8,896]{1,0:T(8,128)(2,1)S(1)}) conditional(s32[]{:T(128)} %convert_element_type.394, () %tuple.148, bf16[64,1920]{1,0:T(8,128)(2,1)S(1)} %get-tuple-element.394), branch_computations={%region_27.28_spmd, %region_28.30_spmd} | conditional | flops 287776 | bytes 870536 | solution.py:163
  157.6 11.3 %all_to_all.57 = bf16[8,8,1920]{2,1,0:T(8,128)(2,1)S(1)} all-to-all(bf16[8,8,1920]{2,1,0:T(8,128)(2,1)S(1)} %bitcast.57), channel_id=1, replica_groups=mesh['y'=4,'xh'=2,'xl'=2,'z'=8,'c'=2] {'y','xh'}, dimensions={0} | all-to-all | bytes 491520 | tf_op jit(solution)/shard_map/cond/branch_1_fun/all_to_all | solution.py:32
  169.3 1.6 collective-permute-start.19
  170.9 13.3 %conditional.22 = (bf16[32,2048]{1,0:T(8,128)(2,1)S(1)}) conditional(s32[]{:T(128)} %convert_element_type.394, () %tuple.151, (bf16[8,896]{1,0:T(8,128)(2,1)S(1)}, bf16[896,2048]{1,0:T(8,128)(2,1)}, s32[1,2048]{1,0:T(1,128)S(1)}, s32[]{:T(128)}, bf16[32,128]{1,0:T(8,128)(2,1)S(1)}) %tuple.152), branch_computations={%region_30.31_spmd, %region_31.32_spmd} | conditional | flops 20368082944 | bytes 54464592 | solution.py:163
  170.9 10.9 %all_to_all.58 = bf16[8,8,896]{2,1,0:T(8,128)(2,1)S(1)} all-to-all(bf16[8,8,896]{2,1,0:T(8,128)(2,1)S(1)} %repeat.10), channel_id=1, replica_groups=mesh['y'=4,'xh'=2,'xl'=2,'z'=8,'c'=2] {'y','xh'}, dimensions={0} | all-to-all | bytes 229376 | tf_op jit(solution)/shard_map/cond/branch_1_fun/all_to_all | solution.py:32
  181.8 0.8 convolution_convert_fusion.13
  182.8 1.3 collective-permute-done.6
  184.2 2.3 %collective-permute-start.20 = (bf16[8,2048]{1,0:T(8,128)(2,1)S(1)}, bf16[8,2048]{1,0:T(8,128)(2,1)S(1)}, u32[]{:S(2)}, u32[]{:S(2)}) collective-permute-start(bf16[8,2048]{1,0:T(8,128)(2,1)S(1)} %slice.166), channel_id=1, source_target_pairs={{0,4},{2,6},{4,0},{6,2},{8,12},{10,14},{12,8},{14,10},{1,5},{3,7},... | collective-permute-start | bytes 98312 | tf_op jit(solution)/shard_map/ppermute | solution.py:28
  186.7 13.9 %conditional.23 = (bf16[2,2048]{1,0:T(2,128)(2,1)S(1)}) conditional(s32[]{:T(128)} %convert_element_type.394, () %tuple.155, bf16[32,2048]{1,0:T(8,128)(2,1)S(1)} %get-tuple-element.396), branch_computations={%region_32.33_spmd, %region_33.35_spmd} | conditional | flops 61440 | bytes 663562 | solution.py:163
  186.9 13.6 %all_to_all.59 = bf16[16,2,2048]{2,1,0:T(2,128)(2,1)S(1)} all-to-all(bf16[16,2,2048]{2,1,0:T(2,128)(2,1)S(1)} %reshape.174), channel_id=1, replica_groups=mesh['y'=4,'xh'=2,'xl'=2,'z'=8,'c'=2] {'xl','z'}, dimensions={0} | all-to-all | bytes 262144 | tf_op jit(solution)/shard_map/cond/branch_1_fun/all_to_all | solution.py:32
  (155 shorter events, 13.9 us)
Async XLA Ops:
  0.7 0.7 copy-start.1
  1.4 28.0 %collective-permute-start.7 = (bf16[8,2048]{1,0:T(8,128)(2,1)}, bf16[8,2048]{1,0:T(8,128)(2,1)S(1)}, u32[]{:S(2)}, u32[]{:S(2)}) collective-permute-start(bf16[8,2048]{1,0:T(8,128)(2,1)} %refs_0_.1), channel_id=1, source_target_pairs={{0,8},{2,10},{4,12},{6,14},{8,0},{10,2},{12,4},{14,6},{1,9},{3,11}... | collective-permute-start | bytes 98312 | tf_op jit(solution)/shard_map/ppermute | solution.py:28
  7.8 21.6 %collective-permute-start.8 = (bf16[8,2048]{1,0:T(8,128)(2,1)}, bf16[8,2048]{1,0:T(8,128)(2,1)S(1)}, u32[]{:S(2)}, u32[]{:S(2)}) collective-permute-start(bf16[8,2048]{1,0:T(8,128)(2,1)} %refs_0_.1), channel_id=1, source_target_pairs={{0,4},{2,6},{4,0},{6,2},{8,12},{10,14},{12,8},{14,10},{1,5},{3,7},... | collective-permute-start | bytes 98312 | tf_op jit(solution)/shard_map/ppermute | solution.py:28
  9.2 20.2 %collective-permute-start.9 = (bf16[8,2048]{1,0:T(8,128)(2,1)}, bf16[8,2048]{1,0:T(8,128)(2,1)S(1)}, u32[]{:S(2)}, u32[]{:S(2)}) collective-permute-start(bf16[8,2048]{1,0:T(8,128)(2,1)} %refs_0_.1), channel_id=1, source_target_pairs={{0,12},{2,14},{4,8},{6,10},{8,4},{10,6},{12,0},{14,2},{1,13},{3,15... | collective-permute-start | bytes 98312 | tf_op jit(solution)/shard_map/ppermute | solution.py:28
  9.2 20.2 %copy-start = (bf16[8,2048]{1,0:T(8,128)(2,1)S(1)}, bf16[8,2048]{1,0:T(8,128)(2,1)}, u32[]{:S(2)}) copy-start(bf16[8,2048]{1,0:T(8,128)(2,1)} %refs_0_.1) | copy-start | bytes 98308
  25.5 0.7 copy-start.14
  25.5 2.0 %copy-start.6 = (bf16[2048,896]{1,0:T(8,128)(2,1)S(1)}, bf16[2048,896]{1,0:T(8,128)(2,1)}, u32[]{:S(2)}) copy-start(bf16[2048,896]{1,0:T(8,128)(2,1)} %get-tuple-element.141) | copy-start | bytes 11010052 | tf_op jit(solution)/shard_map/cond
  25.5 3.1 %copy-start.2 = (bf16[2048,896]{1,0:T(8,128)(2,1)S(1)}, bf16[2048,896]{1,0:T(8,128)(2,1)}, u32[]{:S(2)}) copy-start(bf16[2048,896]{1,0:T(8,128)(2,1)} %get-tuple-element.140) | copy-start | bytes 11010052 | tf_op jit(solution)/shard_map/cond
  25.5 1.4 collective-permute-start
  29.4 19.0 %collective-permute-start.10 = (bf16[32,2048]{1,0:T(8,128)(2,1)S(1)}, bf16[32,2048]{1,0:T(8,128)(2,1)S(1)}, u32[]{:S(2)}, u32[]{:S(2)}) collective-permute-start(bf16[32,2048]{1,0:T(8,128)(2,1)S(1)} %stack.2.refs_0_), channel_id=1, source_target_pairs={{0,2},{2,0},{4,6},{6,4},{8,10},{10,8},{12,14},{14,12},{16,18},{18,... | collective-permute-start | bytes 393224 | tf_op jit(solution)/shard_map/ppermute | solution.py:28
  30.2 18.3 %collective-permute-start.11 = (bf16[32,2048]{1,0:T(8,128)(2,1)S(1)}, bf16[32,2048]{1,0:T(8,128)(2,1)S(1)}, u32[]{:S(2)}, u32[]{:S(2)}) collective-permute-start(bf16[32,2048]{1,0:T(8,128)(2,1)S(1)} %stack.2.refs_0_), channel_id=1, source_target_pairs={{0,16},{2,18},{4,20},{6,22},{8,24},{10,26},{12,28},{14,30},{16,0},... | collective-permute-start | bytes 393224 | tf_op jit(solution)/shard_map/ppermute | solution.py:28
  31.2 17.3 %collective-permute-start.12 = (bf16[32,2048]{1,0:T(8,128)(2,1)S(1)}, bf16[32,2048]{1,0:T(8,128)(2,1)S(1)}, u32[]{:S(2)}, u32[]{:S(2)}) collective-permute-start(bf16[32,2048]{1,0:T(8,128)(2,1)S(1)} %stack.2.refs_0_), channel_id=1, source_target_pairs={{0,18},{2,16},{4,22},{6,20},{8,26},{10,24},{12,30},{14,28},{16,2},... | collective-permute-start | bytes 393224 | tf_op jit(solution)/shard_map/ppermute | solution.py:28
  48.5 11.2 %copy-start.10 = (bf16[896,2048]{1,0:T(8,128)(2,1)S(1)}, bf16[896,2048]{1,0:T(8,128)(2,1)}, u32[]{:S(2)}) copy-start(bf16[896,2048]{1,0:T(8,128)(2,1)} %get-tuple-element.149) | copy-start | bytes 11010052 | tf_op jit(solution)/shard_map/cond
  48.6 12.6 %copy-start.15 = (bf16[2048]{0:T(1024)(128)(2,1)S(1)}, bf16[2048]{0:T(1024)(128)(2,1)}, u32[]{:S(2)}) copy-start(bf16[2048]{0:T(1024)(128)(2,1)} %get-tuple-element.153) | copy-start | bytes 12292 | tf_op jit(solution)/shard_map/cond
  48.6 12.6 %copy-start.7 = (bf16[2048,896]{1,0:T(8,128)(2,1)S(1)}, bf16[2048,896]{1,0:T(8,128)(2,1)}, u32[]{:S(2)}) copy-start(bf16[2048,896]{1,0:T(8,128)(2,1)} %get-tuple-element.155) | copy-start | bytes 11010052 | tf_op jit(solution)/shard_map/cond
  59.5 3.2 %collective-permute-start.2 = (bf16[128,2048]{1,0:T(8,128)(2,1)S(1)}, bf16[128,2048]{1,0:T(8,128)(2,1)S(1)}, u32[]{:S(2)}, u32[]{:S(2)}) collective-permute-start(bf16[128,2048]{1,0:T(8,128)(2,1)S(1)} %get-tuple-element.150), channel_id=1, source_target_pairs={{0,1},{1,0},{2,3},{3,2},{4,5},{5,4},{6,7},{7,6},{8,9},{9,8},{10,11... | collective-permute-start | bytes 1572872 | tf_op jit(solution)/shard_map/cond/branch_1_fun/ppermute | solution.py:28
  59.7 2.2 %copy-start.3 = (bf16[2048,896]{1,0:T(8,128)(2,1)S(1)}, bf16[2048,896]{1,0:T(8,128)(2,1)}, u32[]{:S(2)}) copy-start(bf16[2048,896]{1,0:T(8,128)(2,1)} %get-tuple-element.154) | copy-start | bytes 11010052 | tf_op jit(solution)/shard_map/cond
  60.6 2.1 %collective-permute-start.1 = (bf16[32,2048]{1,0:T(8,128)(2,1)S(1)}, bf16[32,2048]{1,0:T(8,128)(2,1)S(1)}, u32[]{:S(2)}, u32[]{:S(2)}) collective-permute-start(bf16[32,2048]{1,0:T(8,128)(2,1)S(1)} %slice.131), channel_id=1, source_target_pairs={{0,1},{1,0},{2,3},{3,2},{4,5},{5,4},{6,7},{7,6},{8,9},{9,8},{10,11... | collective-permute-start | bytes 393224 | tf_op jit(solution)/shard_map/cond/branch_1_fun/ppermute | solution.py:28
  64.7 14.5 %copy-start.13 = (bf16[2048]{0:T(1024)(128)(2,1)S(1)}, bf16[2048]{0:T(1024)(128)(2,1)}, u32[]{:S(2)}) copy-start(bf16[2048]{0:T(1024)(128)(2,1)} %param.34) | copy-start | bytes 12292
  64.7 13.6 %collective-permute-start.13 = (bf16[128,1920]{1,0:T(8,128)(2,1)S(1)}, bf16[128,1920]{1,0:T(8,128)(2,1)S(1)}, u32[]{:S(2)}, u32[]{:S(2)}) collective-permute-start(bf16[128,1920]{1,0:T(8,128)(2,1)S(1)} %get-tuple-element.277), channel_id=1, source_target_pairs={{0,64},{64,0},{128,192},{192,128},{1,65},{65,1},{129,193},{193,129... | collective-permute-start | bytes 1474568 | tf_op jit(solution)/shard_map/ppermute | solution.py:28
  78.4 15.7 %collective-permute-start.14 = (bf16[64,1920]{1,0:T(8,128)(2,1)S(1)}, bf16[64,1920]{1,0:T(8,128)(2,1)S(1)}, u32[]{:S(2)}, u32[]{:S(2)}) collective-permute-start(bf16[64,1920]{1,0:T(8,128)(2,1)S(1)} %broadcast_select_fusion.1), channel_id=1, source_target_pairs={{0,32},{32,0},{1,33},{33,1},{2,34},{34,2},{3,35},{35,3},{4,36},{36... | collective-permute-start | bytes 737288 | tf_op jit(solution)/shard_map/ppermute | solution.py:28
  79.2 13.5 %copy-start.8 = (bf16[2048,896]{1,0:T(8,128)(2,1)S(1)}, bf16[2048,896]{1,0:T(8,128)(2,1)}, u32[]{:S(2)}) copy-start(bf16[2048,896]{1,0:T(8,128)(2,1)} %get-tuple-element.164) | copy-start | bytes 11010052 | tf_op jit(solution)/shard_map/cond
  79.3 14.1 %copy-start.4 = (bf16[2048,896]{1,0:T(8,128)(2,1)S(1)}, bf16[2048,896]{1,0:T(8,128)(2,1)}, u32[]{:S(2)}) copy-start(bf16[2048,896]{1,0:T(8,128)(2,1)} %get-tuple-element.163) | copy-start | bytes 11010052 | tf_op jit(solution)/shard_map/cond
  91.0 1.4 collective-permute-start.3
  94.3 16.2 %collective-permute-start.15 = (bf16[32,1920]{1,0:T(8,128)(2,1)S(1)}, bf16[32,1920]{1,0:T(8,128)(2,1)S(1)}, u32[]{:S(2)}, u32[]{:S(2)}) collective-permute-start(bf16[32,1920]{1,0:T(8,128)(2,1)S(1)} %broadcast_select_fusion.2), channel_id=1, source_target_pairs={{0,128},{64,192},{128,0},{192,64},{1,129},{65,193},{129,1},{193,65... | collective-permute-start | bytes 368648 | tf_op jit(solution)/shard_map/ppermute | solution.py:28
  110.9 13.9 %copy-start.11 = (bf16[896,2048]{1,0:T(8,128)(2,1)S(1)}, bf16[896,2048]{1,0:T(8,128)(2,1)}, u32[]{:S(2)}) copy-start(bf16[896,2048]{1,0:T(8,128)(2,1)} %get-tuple-element.169) | copy-start | bytes 11010052 | tf_op jit(solution)/shard_map/cond
  125.6 1.6 collective-permute-start.4
  127.3 12.5 %collective-permute-start.16 = (bf16[128,2048]{1,0:T(8,128)(2,1)S(1)}, bf16[128,2048]{1,0:T(8,128)(2,1)S(1)}, u32[]{:S(2)}, u32[]{:S(2)}) collective-permute-start(bf16[128,2048]{1,0:T(8,128)(2,1)S(1)} %get-tuple-element.296), channel_id=1, source_target_pairs={{0,1},{1,0},{2,3},{3,2},{4,5},{5,4},{6,7},{7,6},{8,9},{9,8},{10,11... | collective-permute-start | bytes 1572872 | tf_op jit(solution)/shard_map/ppermute | solution.py:28
  139.9 16.6 %collective-permute-start.17 = (bf16[64,2048]{1,0:T(8,128)(2,1)S(1)}, bf16[64,2048]{1,0:T(8,128)(2,1)S(1)}, u32[]{:S(2)}, u32[]{:S(2)}) collective-permute-start(bf16[64,2048]{1,0:T(8,128)(2,1)S(1)} %slice.161), channel_id=1, source_target_pairs={{0,16},{16,0},{1,17},{17,1},{2,18},{18,2},{3,19},{19,3},{4,20},{20... | collective-permute-start | bytes 786440 | tf_op jit(solution)/shard_map/ppermute | solution.py:28
  140.9 14.2 %copy-start.9 = (bf16[2048,896]{1,0:T(8,128)(2,1)S(1)}, bf16[2048,896]{1,0:T(8,128)(2,1)}, u32[]{:S(2)}) copy-start(bf16[2048,896]{1,0:T(8,128)(2,1)} %get-tuple-element.175) | copy-start | bytes 11010052 | tf_op jit(solution)/shard_map/cond
  140.9 14.9 %copy-start.5 = (bf16[2048,896]{1,0:T(8,128)(2,1)S(1)}, bf16[2048,896]{1,0:T(8,128)(2,1)}, u32[]{:S(2)}) copy-start(bf16[2048,896]{1,0:T(8,128)(2,1)} %get-tuple-element.174) | copy-start | bytes 11010052 | tf_op jit(solution)/shard_map/cond
  153.4 1.4 collective-permute-start.5
  156.6 12.6 %collective-permute-start.18 = (bf16[32,2048]{1,0:T(8,128)(2,1)S(1)}, bf16[32,2048]{1,0:T(8,128)(2,1)S(1)}, u32[]{:S(2)}, u32[]{:S(2)}) collective-permute-start(bf16[32,2048]{1,0:T(8,128)(2,1)S(1)} %slice.163), channel_id=1, source_target_pairs={{0,2},{2,0},{4,6},{6,4},{8,10},{10,8},{12,14},{14,12},{1,3},{3,1},... | collective-permute-start | bytes 393224 | tf_op jit(solution)/shard_map/ppermute | solution.py:28
  169.3 14.9 %collective-permute-start.19 = (bf16[16,2048]{1,0:T(8,128)(2,1)S(1)}, bf16[16,2048]{1,0:T(8,128)(2,1)S(1)}, u32[]{:S(2)}, u32[]{:S(2)}) collective-permute-start(bf16[16,2048]{1,0:T(8,128)(2,1)S(1)} %slice.165), channel_id=1, source_target_pairs={{0,8},{2,10},{4,12},{6,14},{8,0},{10,2},{12,4},{14,6},{1,9},{3,11}... | collective-permute-start | bytes 196616 | tf_op jit(solution)/shard_map/ppermute | solution.py:28
  170.9 15.7 %copy-start.17 = (s32[2]{0:T(128)S(1)}, s32[2]{0:T(128)}, u32[]{:S(2)}) copy-start(s32[2]{0:T(128)} %param.33) | copy-start | bytes 28
  170.9 11.0 %copy-start.12 = (bf16[896,2048]{1,0:T(8,128)(2,1)S(1)}, bf16[896,2048]{1,0:T(8,128)(2,1)}, u32[]{:S(2)}) copy-start(bf16[896,2048]{1,0:T(8,128)(2,1)} %get-tuple-element.179) | copy-start | bytes 11010052 | tf_op jit(solution)/shard_map/cond
  182.6 1.4 collective-permute-start.6
  184.2 16.4 %collective-permute-start.20 = (bf16[8,2048]{1,0:T(8,128)(2,1)S(1)}, bf16[8,2048]{1,0:T(8,128)(2,1)S(1)}, u32[]{:S(2)}, u32[]{:S(2)}) collective-permute-start(bf16[8,2048]{1,0:T(8,128)(2,1)S(1)} %slice.166), channel_id=1, source_target_pairs={{0,4},{2,6},{4,0},{6,2},{8,12},{10,14},{12,8},{14,10},{1,5},{3,7},... | collective-permute-start | bytes 98312 | tf_op jit(solution)/shard_map/ppermute | solution.py:28
  200.6 0.7 copy-start.16
